TPU v7x, 32 devices: a whole 2x2x4 slice. The times are simulated.
32 devices in a mesh: replica: 16 (over z, y, core), fsdp: 2 (over x).
Axes of the slice: x: 2, y: 2, z: 4, core: 2. Of those that a mesh axis runs over, the one named last changes fastest.
Arguments:
- tokens: bfloat16 [4096, 1024], P(('replica', 'fsdp')), may hold values from -6 to 6
- seq_lens: int32 [32, 2], P(('replica', 'fsdp')), may hold values from 16 to 96, as said below
- norm_gain: bfloat16 [1024], P('fsdp'), may hold values from 0.099609375 to 1.8984375
- in_weight: bfloat16 [1024, 4384], P('fsdp'), may hold values from -0.1875 to 0.1875
- conv_weight: bfloat16 [4, 2304], P(None, 'fsdp'), may hold values from -3 to 3
- conv_bias: bfloat16 [2304], P('fsdp'), may hold values from -1.5 to 1.5
- step_bias: bfloat16 [32], P('fsdp'), may hold values from -4.5 to -2
- decay_log: bfloat16 [32], P('fsdp'), may hold values from -4 to 0
- skip_gain: bfloat16 [32], P('fsdp'), may hold values from 0.5 to 2
- out_gain: bfloat16 [2048], P('fsdp'), may hold values from 0.099609375 to 1.8984375
- out_weight: bfloat16 [2048, 1024], P('fsdp'), may hold values from -0.125 to 0.125
- cotangent: bfloat16 [4096, 1024], P(('replica', 'fsdp')), may hold values from -6 to 6
Outputs:
- block_out: bfloat16 [4096, 1024], P(('replica', 'fsdp'))
- grad_tokens: float32 [4096, 1024], P(('replica', 'fsdp'))
- norm_gain_grad: float32 [1024], P('fsdp')
- in_weight_grad: float32 [1024, 4384], P('fsdp')
- conv_weight_grad: float32 [4, 2304], P(None, 'fsdp')
- conv_bias_grad: float32 [2304], P('fsdp')
- step_bias_grad: float32 [32], P('fsdp')
- decay_log_grad: float32 [32], P('fsdp')
- skip_gain_grad: float32 [32], P('fsdp')
- out_gain_grad: float32 [2048], P('fsdp')
- out_weight_grad: float32 [2048, 1024], P('fsdp')
Inputs may be any that keep to these rules, and one draw needn't show every extreme that they name: `seq_lens`: on each device the sequences fill the first slots, the rest being padding; each length is at least 16, a device's two lengths sum to at most 128, and some device holds exactly 128 tokens of sequences.
All inputs are finite; a program needn't handle non-finite values.
Results may differ from a plain program's by a relative error of at most 0.0074.
Values may be sent and summed in bfloat16 or wider, within the bound.
No kernel may reach another device: no remote copies, remote signals or barrier semaphores. Data moves between devices by JAX's collectives and lax.ppermute only.
A program may use at most 192 MiB of HBM per device.

v0:
```python
from functools import partial

import jax
import jax.numpy as jnp
from jax import lax
from jax.sharding import PartitionSpec as P

EPSILON = 1e-05


def segment_layout(lengths_row, row_count):
    position = jnp.arange(row_count, dtype=jnp.int32)
    bounds = jnp.cumsum(lengths_row)
    segment = jnp.sum((position[:, None] >= bounds[None, :]).astype(jnp.int32), axis=1)
    starts = jnp.concatenate([jnp.zeros((1,), jnp.int32), bounds])
    labels = jnp.arange(starts.shape[0], dtype=jnp.int32)
    seg_start = jnp.sum(jnp.where(segment[:, None] == labels[None, :], starts[None, :], 0), axis=1)
    return (position, segment, seg_start)


def input_norm(values, norm_scale):
    inverse_rms = lax.rsqrt(jnp.mean(values * values, axis=-1, keepdims=True) + EPSILON)
    return values * inverse_rms * norm_scale


def gated_norm(mixed_values, gate_part, out_scale):
    gated = mixed_values * jax.nn.silu(gate_part)
    inverse_rms = lax.rsqrt(jnp.mean(gated * gated, axis=-1, keepdims=True) + EPSILON)
    return gated * inverse_rms * out_scale


def conv_and_rates(
    mixed_in, rate_raw, conv_kernel, conv_shift, rate_bias, decay_rate, position, seg_start
):
    row_count = mixed_in.shape[0]
    tap_count = conv_kernel.shape[0]
    summed = jnp.broadcast_to(conv_shift, mixed_in.shape)
    for offset in range(tap_count):
        behind = tap_count - 1 - offset
        shifted = jnp.concatenate(
            [
                jnp.zeros((behind, mixed_in.shape[1]), mixed_in.dtype),
                mixed_in[: row_count - behind],
            ],
            axis=0,
        )
        usable = (position - behind >= seg_start)[:, None]
        summed = summed + conv_kernel[offset] * jnp.where(usable, shifted, 0.0)
    active = jax.nn.silu(summed)
    step_size = jax.nn.softplus(rate_raw + rate_bias)
    cumulative = jnp.cumsum(step_size * -jnp.exp(decay_rate), axis=0)
    return (active, step_size, cumulative)


def decay_weights(inner_part, cum_rows, cum_keys, step_keys, same_mask):
    spread = cum_rows.T[:, :, None] - cum_keys.T[:, None, :]
    masked = jnp.where(same_mask[None], spread, 0.0)
    decays = jnp.where(same_mask[None], jnp.exp(masked), 0.0)
    return inner_part[None] * decays * step_keys.T[:, None, :]


def per_device(
    tokens,
    seq_lens,
    norm_gain,
    in_weight,
    conv_weight,
    conv_bias,
    step_bias,
    decay_log,
    skip_gain,
    out_gain,
    out_weight,
    cotangent,
):
    gathered = (
        lax.all_gather(norm_gain, "fsdp", axis=0, tiled=True),
        lax.all_gather(in_weight, "fsdp", axis=0, tiled=True),
        lax.all_gather(conv_weight, "fsdp", axis=1, tiled=True),
        lax.all_gather(conv_bias, "fsdp", axis=0, tiled=True),
        lax.all_gather(step_bias, "fsdp", axis=0, tiled=True),
        lax.all_gather(decay_log, "fsdp", axis=0, tiled=True),
        lax.all_gather(skip_gain, "fsdp", axis=0, tiled=True),
        lax.all_gather(out_gain, "fsdp", axis=0, tiled=True),
        lax.all_gather(out_weight, "fsdp", axis=0, tiled=True),
    )
    (
        norm_full,
        in_full,
        conv_full,
        shift_full,
        bias_full,
        log_full,
        skip_full,
        out_scale_full,
        out_full,
    ) = gathered
    row_count = tokens.shape[0]
    inner_width = out_full.shape[0]
    channels = shift_full.shape[0]
    head_count = skip_full.shape[0]
    state_width = (channels - inner_width) // 2
    head_size = inner_width // head_count
    position, segment, seg_start = segment_layout(seq_lens[0], row_count)
    values = tokens.astype(jnp.float32)
    normed_float, norm_pullback = jax.vjp(input_norm, values, norm_full.astype(jnp.float32))
    normed = normed_float.astype(jnp.bfloat16)
    projected = jnp.dot(normed, in_full, preferred_element_type=jnp.float32)
    gate_part = projected[:, :inner_width]
    mixed_in = projected[:, inner_width : inner_width + channels]
    rate_raw = projected[:, inner_width + channels :]
    prepare = partial(conv_and_rates, position=position, seg_start=seg_start)
    (active, step_size, cumulative), prepare_pullback = jax.vjp(
        prepare,
        mixed_in,
        rate_raw,
        conv_full.astype(jnp.float32),
        shift_full.astype(jnp.float32),
        bias_full.astype(jnp.float32),
        log_full.astype(jnp.float32),
    )
    x_active = active[:, :inner_width]
    head_input = x_active.reshape(row_count, head_count, head_size).astype(jnp.bfloat16)
    state_input = active[:, inner_width : inner_width + state_width].astype(jnp.bfloat16)
    state_output = active[:, inner_width + state_width :].astype(jnp.bfloat16)
    span = min(256, row_count)
    span_index = 0
    row_begin = span_index * span
    row_end = row_begin + span
    inner_part = lax.dot_general(
        state_output, state_input, (((1,), (1,)), ((), ())), preferred_element_type=jnp.float32
    )
    same_mask = (position[None, :row_end] <= position[row_begin:row_end, None]) & (
        segment[None, :row_end] == segment[row_begin:row_end, None]
    )
    mixing_float, mixing_pullback = jax.vjp(
        partial(decay_weights, same_mask=same_mask), inner_part, cumulative, cumulative, step_size
    )
    mixing = mixing_float.astype(jnp.bfloat16)
    scan_parts = jnp.einsum("hts,shp->thp", mixing, head_input, preferred_element_type=jnp.float32)
    saved_terms = [(mixing, mixing_pullback)]
    scan_out = scan_parts.reshape(row_count, inner_width)
    skip_float = skip_full.astype(jnp.float32)
    direct = (
        x_active.reshape(row_count, head_count, head_size) * skip_float[None, :, None]
    ).reshape(row_count, inner_width)
    mixed_out = scan_out + direct
    out_normed, gated_pullback = jax.vjp(
        gated_norm, mixed_out, gate_part, out_scale_full.astype(jnp.float32)
    )
    out_low = out_normed.astype(jnp.bfloat16)
    branch = jnp.dot(out_low, out_full, preferred_element_type=jnp.float32)
    block_out = (values + branch).astype(jnp.bfloat16)
    in_back, out_back = (
        lax.all_gather(in_weight, "fsdp", axis=0, tiled=True),
        lax.all_gather(out_weight, "fsdp", axis=0, tiled=True),
    )
    out_weight_grad = lax.dot_general(
        out_low, cotangent, (((0,), (0,)), ((), ())), preferred_element_type=jnp.float32
    )
    grad_out_normed = lax.dot_general(
        cotangent, out_back, (((1,), (1,)), ((), ())), preferred_element_type=jnp.float32
    )
    grad_mixed, grad_gate, out_gain_grad = gated_pullback(grad_out_normed)
    grad_heads = grad_mixed.reshape(row_count, head_count, head_size)
    skip_gain_grad = jnp.sum(
        grad_heads * x_active.reshape(row_count, head_count, head_size), axis=(0, 2)
    )
    grad_low = grad_heads.astype(jnp.bfloat16)
    grad_input = grad_heads * skip_float[None, :, None]
    span_index = 0
    mixing, mixing_pullback = saved_terms[span_index]
    grad_mixing = jnp.einsum(
        "thp,shp->hts", grad_low, head_input, preferred_element_type=jnp.float32
    )
    grad_input = grad_input + jnp.einsum(
        "hts,thp->shp", mixing, grad_low, preferred_element_type=jnp.float32
    )
    grad_inner, grad_cum_rows, grad_cum_keys, grad_step_keys = mixing_pullback(grad_mixing)
    grad_inner_low = grad_inner.astype(jnp.bfloat16)
    grad_state_out_parts = jnp.dot(grad_inner_low, state_input, preferred_element_type=jnp.float32)
    grad_state_in = lax.dot_general(
        grad_inner_low, state_output, (((0,), (0,)), ((), ())), preferred_element_type=jnp.float32
    )
    grad_cum = grad_cum_keys + grad_cum_rows
    grad_active = jnp.concatenate(
        [grad_input.reshape(row_count, inner_width), grad_state_in, grad_state_out_parts], axis=1
    )
    grad_mixed_in, grad_rate_raw, conv_grad, shift_grad, bias_grad, log_grad = prepare_pullback(
        (grad_active, grad_step_keys, grad_cum)
    )
    grad_projected = jnp.concatenate([grad_gate, grad_mixed_in, grad_rate_raw], axis=1).astype(
        jnp.bfloat16
    )
    in_weight_grad = lax.dot_general(
        normed, grad_projected, (((0,), (0,)), ((), ())), preferred_element_type=jnp.float32
    )
    grad_normed = lax.dot_general(
        grad_projected, in_back, (((1,), (1,)), ((), ())), preferred_element_type=jnp.float32
    )
    grad_values, norm_gain_grad = norm_pullback(grad_normed)
    grad_tokens = cotangent.astype(jnp.float32) + grad_values
    shares = (
        lax.psum_scatter(norm_gain_grad, "fsdp", scatter_dimension=0, tiled=True),
        lax.psum_scatter(in_weight_grad, "fsdp", scatter_dimension=0, tiled=True),
        lax.psum_scatter(conv_grad, "fsdp", scatter_dimension=1, tiled=True),
        lax.psum_scatter(shift_grad, "fsdp", scatter_dimension=0, tiled=True),
        lax.psum_scatter(bias_grad, "fsdp", scatter_dimension=0, tiled=True),
        lax.psum_scatter(log_grad, "fsdp", scatter_dimension=0, tiled=True),
        lax.psum_scatter(skip_gain_grad, "fsdp", scatter_dimension=0, tiled=True),
        lax.psum_scatter(out_gain_grad, "fsdp", scatter_dimension=0, tiled=True),
        lax.psum_scatter(out_weight_grad, "fsdp", scatter_dimension=0, tiled=True),
    )
    totals = lax.psum(
        (
            shares[0],
            shares[1],
            shares[2],
            shares[3],
            shares[4],
            shares[5],
            shares[6],
            shares[7],
            shares[8],
        ),
        "replica",
    )
    return (
        block_out,
        grad_tokens,
        totals[0],
        totals[1],
        totals[2],
        totals[3],
        totals[4],
        totals[5],
        totals[6],
        totals[7],
        totals[8],
    )


def solution(mesh):
    placed = (
        P(("replica", "fsdp"), None),
        P(("replica", "fsdp"), None),
        P("fsdp"),
        P("fsdp", None),
        P(None, "fsdp"),
        P("fsdp"),
        P("fsdp"),
        P("fsdp"),
        P("fsdp"),
        P("fsdp"),
        P("fsdp", None),
        P(("replica", "fsdp"), None),
    )
    return jax.shard_map(
        per_device,
        mesh=mesh,
        in_specs=placed,
        out_specs=(
            P(("replica", "fsdp"), None),
            P(("replica", "fsdp"), None),
            P("fsdp"),
            P("fsdp", None),
            P(None, "fsdp"),
            P("fsdp"),
            P("fsdp"),
            P("fsdp"),
            P("fsdp"),
            P("fsdp"),
            P("fsdp", None),
        ),
        check_vma=False,
    )
```

profile of v0, /device:TPU:0, one launch (start us, length us, event | category | flops | bytes accessed | tf_op | source)
XLA Modules:
  0.0 779.3 jit_solution(17464153344092833214)
XLA Ops:
  9.2 5.3 all_gather.30
  14.6 4.3 all-gather
  19.1 4.3 all-gather.1
  25.5 4.9 all-reduce.22
  31.7 4.4 all_gather.36
  37.5 87.8 %all-gather.5.cloned.1.call-done = bf16[1024,4384]{0,1:T(8,128)(2,1)} async-done(((bf16[512,4384]{0,1:T(8,128)(2,1)}), bf16[1024,4384]{0,1:T(8,128)(2,1)}) %all-gather.5.cloned.1.call-update) | async-done | bytes 8978448 | tf_op jit(solution)/shard_map/all_gather | solution.py:78
  125.4 6.1 fusion.32
  133.1 3.6 fusion.63
  144.1 4.7 fusion.56
  153.8 29.9 %all-gather.7.cloned.1.call-done = bf16[2048,1024]{1,0:T(8,128)(2,1)} async-done(((bf16[1024,1024]{1,0:T(8,128)(2,1)}), bf16[2048,1024]{1,0:T(8,128)(2,1)}) %all-gather.7.cloned.1.call-update) | async-done | bytes 4194320 | tf_op jit(solution)/shard_map/all_gather | solution.py:85
  183.7 4.3 multiply_reduce_fusion.6
  188.2 2.6 multiply_reduce_fusion.7
  190.8 2.7 fusion.11
  206.1 3.4 fusion.57
  212.6 8.8 %fusion.25 = f32[1024,4384]{0,1:T(8,128)} fusion(bf16[128,32]{0,1:T(8,128)(2,1)S(1)} %get-tuple-element.49, bf16[128,2304]{0,1:T(8,128)(2,1)S(1)} %add_convert_fusion, bf16[128,2048]{0,1:T(8,128)(2,1)S(1)} %copy-done.11, bf16[128,1024]{1,0:T(8,128)(2,1)S(1)} %copy-done.9, f32[1024]{0:T(1024)S(1)} %bitcast.52, f32[128]{0:T(128)S(1)} %copy-done.54), kind=kOutput, calls=%fused_computation.64 | convolution fusion | flops 1153130496 | bytes 19345920 | tf_op jit(solution)/shard_map/dot_general | solution.py:195
  224.0 61.9 %reduce-scatter.8.cloned.1.call-done = f32[1024,1024]{1,0:T(8,128)} async-done(((f32[2048,1024]{1,0:T(8,128)}), f32[1024,1024]{1,0:T(8,128)}) %reduce-scatter.8.cloned.1.call-update) | async-done | bytes 4194320 | tf_op jit(solution)/shard_map/reduce_scatter | solution.py:212
  285.8 204.1 %reduce-scatter.6.cloned.1.call-done = f32[512,4384]{0,1:T(8,128)} async-done(((f32[1024,4384]{0,1:T(8,128)}), f32[512,4384]{0,1:T(8,128)}) %reduce-scatter.6.cloned.1.call-update) | async-done | bytes 8978448 | tf_op jit(solution)/shard_map/reduce_scatter | solution.py:205
  492.9 5.1 fusion.20
  498.1 7.8 %all-reduce.21 = (f32[1024]{0:T(1024)S(1)}, f32[2304]{0:T(1024)S(1)}, f32[32]{0:T(128)S(1)}, f32[32]{0:T(128)S(1)}, f32[32]{0:T(128)S(1)}, /*index=5*/f32[2048]{0:T(1024)S(1)}) all-reduce(f32[1024]{0:T(1024)S(1)} %get-tuple-element.22, f32[2304]{0:T(1024)S(1)} %copy-done.40, ...), channel_id=2, replica_groups=mesh['replica'=16,'fsdp'=2] {'fsdp'}, use_global_device_ids=true, to_apply=%region_14.15.clone | all-reduce | flops 5472 | bytes 43776
  507.3 4.2 fusion.3
  511.5 3.7 reduce-scatter.10.cloned.1.call-done
  516.4 65.0 %all-reduce.19 = (f32[512]{0:T(512)}, f32[4,1152]{1,0:T(4,128)}, f32[1152]{0:T(1024)}, f32[16]{0:T(128)}, f32[16]{0:T(128)}, /*index=5*/f32[16]{0:T(128)}, f32[1024]{0:T(1024)}) all-reduce(f32[512]{0:T(512)S(1)} %dynamic-slice.4, f32[4,1152]{1,0:T(4,128)S(1)} %copy.48, ...), channel_id=1, replica_groups=mesh['replica'=16,'fsdp'=2] {'replica'}, use_global_device_ids=true, to_apply=%region_15.16 | all-reduce | flops 7344 | bytes 58752 | tf_op jit(solution)/shard_map/psum | solution.py:214
  581.4 180.7 %all-reduce.25.cloned.1.call-done = (f32[512,4384]{0,1:T(8,128)}, f32[1024,1024]{1,0:T(8,128)}) async-done(((f32[512,4384]{0,1:T(8,128)}, f32[1024,1024]{1,0:T(8,128)}), (f32[512,4384]{0,1:T(8,128)}, f32[1024,1024]{1,0:T(8,128)})) %all-reduce.25.cloned.1.call-update) | async-done | bytes 13172752 | tf_op jit(solution)/shard_map/psum | solution.py:214
  762.1 8.4 %copy.54 = f32[512,4384]{0,1:T(8,128)} copy(f32[512,4384]{0,1:T(8,128)} %get-tuple-element.74) | data formatting | bytes 17956864
  (265 shorter events, 42.9 us)
Async XLA Ops:
  7.2 118.2 %all-gather.5.cloned.1.call-start = ((), (), s32[]{:S(2)}) async-start(), calls=%async_computation.3 | async-start | bytes 13467648 | tf_op jit(solution)/shard_map/all_gather | solution.py:78
  8.0 16.8 %copy-start.84 = (bf16[16]{0:T(256)(128)(2,1)S(1)}, bf16[16]{0:T(256)(128)(2,1)}, u32[]{:S(2)}) copy-start(bf16[16]{0:T(256)(128)(2,1)} %param.20) | copy-start | bytes 100
  8.0 17.0 %copy-start.85 = (bf16[16]{0:T(256)(128)(2,1)S(1)}, bf16[16]{0:T(256)(128)(2,1)}, u32[]{:S(2)}) copy-start(bf16[16]{0:T(256)(128)(2,1)} %param.18) | copy-start | bytes 100
  8.0 17.2 %copy-start.86 = (bf16[16]{0:T(256)(128)(2,1)S(1)}, bf16[16]{0:T(256)(128)(2,1)}, u32[]{:S(2)}) copy-start(bf16[16]{0:T(256)(128)(2,1)} %param.19) | copy-start | bytes 100
  8.0 23.7 %copy-start.68 = (bf16[1024]{0:T(1024)(128)(2,1)S(1)}, bf16[1024]{0:T(1024)(128)(2,1)}, u32[]{:S(2)}) copy-start(bf16[1024]{0:T(1024)(128)(2,1)} %param.21) | copy-start | bytes 6148
  8.0 28.7 %copy-start.9 = (bf16[128,1024]{1,0:T(8,128)(2,1)S(1)}, bf16[128,1024]{1,0:T(8,128)(2,1)}, u32[]{:S(2)}) copy-start(bf16[128,1024]{1,0:T(8,128)(2,1)} %param.12) | copy-start | bytes 786436
  8.0 175.7 %all-gather.7.cloned.1.call-start = ((), (), s32[]{:S(2)}) async-start(), calls=%async_computation.4 | async-start | bytes 6291456 | tf_op jit(solution)/shard_map/all_gather | solution.py:85
  8.8 277.1 %reduce-scatter.8.cloned.1.call-start = ((), (), s32[]{:S(2)}) async-start(), calls=%async_computation.6 | async-start | bytes 12582912 | tf_op jit(solution)/shard_map/reduce_scatter | solution.py:212
  14.5 117.3 %copy-start.26 = (f32[2304]{0:T(1024)}, f32[2304]{0:T(1024)S(1)}, u32[]{:S(2)}) copy-start(f32[2304]{0:T(1024)S(1)} %get-tuple-element.25) | copy-start | bytes 27652
  14.5 117.3 %copy-start.28 = (f32[2304]{0:T(1024)}, f32[2304]{0:T(1024)S(1)}, u32[]{:S(2)}) copy-start(f32[2304]{0:T(1024)S(1)} %get-tuple-element.26) | copy-start | bytes 27652
  14.6 117.3 %copy-start.30 = (f32[2304]{0:T(1024)}, f32[2304]{0:T(1024)S(1)}, u32[]{:S(2)}) copy-start(f32[2304]{0:T(1024)S(1)} %get-tuple-element.27) | copy-start | bytes 27652
  14.6 117.3 %copy-start.32 = (f32[2304]{0:T(1024)}, f32[2304]{0:T(1024)S(1)}, u32[]{:S(2)}) copy-start(f32[2304]{0:T(1024)S(1)} %get-tuple-element.24) | copy-start | bytes 27652
  23.4 108.1 %copy-start.24 = (f32[2,1,512]{2,1,0:T(1,128)}, f32[2,1,512]{2,1,0:T(1,128)S(1)}, u32[]{:S(2)}) copy-start(f32[2,1,512]{2,1,0:T(1,128)S(1)} %convert_element_type.76) | copy-start | bytes 12292
  31.7 106.9 %copy-start.70 = (f32[32]{0:T(128)}, f32[32]{0:T(128)S(1)}, u32[]{:S(2)}) copy-start(f32[32]{0:T(128)S(1)} %convert_element_type.65) | copy-start | bytes 388
  36.9 94.6 %copy-start.53 = (f32[128]{0:T(128)}, f32[128]{0:T(128)S(1)}, u32[]{:S(2)}) copy-start(f32[128]{0:T(128)S(1)} %fusion.49) | copy-start | bytes 1540
  37.4 101.2 %copy-start.71 = (f32[32]{0:T(128)}, f32[32]{0:T(128)S(1)}, u32[]{:S(2)}) copy-start(f32[32]{0:T(128)S(1)} %fusion.48) | copy-start | bytes 388
  37.4 94.5 %copy-start.59 = (pred[128]{0:T(512)(128)(4,1)}, pred[128]{0:T(512)(128)(4,1)S(1)}, u32[]{:S(2)}) copy-start(pred[128]{0:T(512)(128)(4,1)S(1)} %get-tuple-element.63) | copy-start | bytes 388
  37.4 94.5 %copy-start.61 = (pred[128]{0:T(512)(128)(4,1)}, pred[128]{0:T(512)(128)(4,1)S(1)}, u32[]{:S(2)}) copy-start(pred[128]{0:T(512)(128)(4,1)S(1)} %get-tuple-element.62) | copy-start | bytes 388
  37.4 94.5 %copy-start.63 = (pred[128]{0:T(512)(128)(4,1)}, pred[128]{0:T(512)(128)(4,1)S(1)}, u32[]{:S(2)}) copy-start(pred[128]{0:T(512)(128)(4,1)S(1)} %get-tuple-element.64) | copy-start | bytes 388
  37.4 94.5 %copy-start.65 = (pred[128]{0:T(512)(128)(4,1)}, pred[128]{0:T(512)(128)(4,1)S(1)}, u32[]{:S(2)}) copy-start(pred[128]{0:T(512)(128)(4,1)S(1)} %get-tuple-element.65) | copy-start | bytes 388
  37.5 101.7 %copy-start.51 = (pred[128,128]{1,0:T(8,128)(4,1)}, pred[128,128]{1,0:T(8,128)(4,1)S(1)}, u32[]{:S(2)}) copy-start(pred[128,128]{1,0:T(8,128)(4,1)S(1)} %fusion.34) | copy-start | bytes 49156
  148.8 341.1 %reduce-scatter.6.cloned.1.call-start = ((), (), s32[]{:S(2)}) async-start(), calls=%async_computation.5 | async-start | bytes 26935296 | tf_op jit(solution)/shard_map/reduce_scatter | solution.py:205
  221.5 293.7 %reduce-scatter.10.cloned.1.call-start = ((), (), s32[]{:S(2)}) async-start(), calls=%async_computation.7 | async-start | bytes 1769472
  223.7 538.4 %all-reduce.25.cloned.1.call-start = ((), (), s32[]{:S(2)}) async-start(), calls=%async_computation.8 | async-start | bytes 26345472 | tf_op jit(solution)/shard_map/psum | solution.py:214
  (71 other events, 242.2 us)
Sparse Core Ops, SparseCore 0:
  9.6 115.7 all-gather.4
  126.9 56.7 all-gather.6
  186.6 99.2 reduce-scatter.7
  288.1 201.7 reduce-scatter.5
  492.7 22.4 reduce-scatter.9
  519.1 242.9 all-reduce.24
where the time goes:
time: 780 us; the launch traced here: 779 us
  waiting for transfers between devices  569 us (73%)
  blocking collectives  96.1 us (12%)
  matrix products  42.7 us (5%)
  local copies, waits for them, and re-layouts  31 us (4%)
  other arithmetic  21.2 us (3%)
  between operations  18.5 us (2%)
    reduce_scatter x1, waiting for transfers between devices, per_device(): lax.psum_scatter(in_weight_grad, 'fsdp', scatter_dimension=0, tiled=True)  204 us
    psum x1, waiting for transfers between devices, per_device(): lax.psum((shares[0], shares[1], shares[2], shares[3], shares[4], shares[5...  181 us
    all_gather x1, waiting for transfers between devices, per_device(): lax.all_gather(in_weight, 'fsdp', axis=0, tiled=True)  87.8 us
    psum x1, blocking collectives, per_device(): lax.psum((shares[0], shares[1], shares[2], shares[3], shares[4], shares[5...  65 us
    reduce_scatter x1, waiting for transfers between devices, per_device(): lax.psum_scatter(out_weight_grad, 'fsdp', scatter_dimension=0, tiled=True)  61.9 us
    all_gather x1, waiting for transfers between devices, per_device(): lax.all_gather(out_weight, 'fsdp', axis=0, tiled=True)  29.9 us
    unnamed x197, local copies, waits for them, and re-layouts  22.1 us
  transfers between devices with their start and end apart: 6, of which 6 were waited for; matrix products, arithmetic and copies ran while one was open for 10% of the time, Pallas kernels for 0%

commit v1 on v0

v1 whole, which is shorter than its diff:
```python
from functools import partial

import jax
import jax.numpy as jnp
from jax import lax
from jax.sharding import PartitionSpec as P

EPSILON = 1e-05


def segment_layout(lengths_row, row_count):
    position = jnp.arange(row_count, dtype=jnp.int32)
    bounds = jnp.cumsum(lengths_row)
    segment = jnp.sum((position[:, None] >= bounds[None, :]).astype(jnp.int32), axis=1)
    starts = jnp.concatenate([jnp.zeros((1,), jnp.int32), bounds])
    labels = jnp.arange(starts.shape[0], dtype=jnp.int32)
    seg_start = jnp.sum(jnp.where(segment[:, None] == labels[None, :], starts[None, :], 0), axis=1)
    return (position, segment, seg_start)


def input_norm(values, norm_scale):
    inverse_rms = lax.rsqrt(jnp.mean(values * values, axis=-1, keepdims=True) + EPSILON)
    return values * inverse_rms * norm_scale


def gated_norm(mixed_values, gate_part, out_scale):
    gated = mixed_values * jax.nn.silu(gate_part)
    inverse_rms = lax.rsqrt(jnp.mean(gated * gated, axis=-1, keepdims=True) + EPSILON)
    return gated * inverse_rms * out_scale


def conv_and_rates(
    mixed_in, rate_raw, conv_kernel, conv_shift, rate_bias, decay_rate, position, seg_start
):
    row_count = mixed_in.shape[0]
    tap_count = conv_kernel.shape[0]
    summed = jnp.broadcast_to(conv_shift, mixed_in.shape)
    for offset in range(tap_count):
        behind = tap_count - 1 - offset
        shifted = jnp.concatenate(
            [
                jnp.zeros((behind, mixed_in.shape[1]), mixed_in.dtype),
                mixed_in[: row_count - behind],
            ],
            axis=0,
        )
        usable = (position - behind >= seg_start)[:, None]
        summed = summed + conv_kernel[offset] * jnp.where(usable, shifted, 0.0)
    active = jax.nn.silu(summed)
    step_size = jax.nn.softplus(rate_raw + rate_bias)
    cumulative = jnp.cumsum(step_size * -jnp.exp(decay_rate), axis=0)
    return (active, step_size, cumulative)


def decay_weights(inner_part, cum_rows, cum_keys, step_keys, same_mask):
    spread = cum_rows.T[:, :, None] - cum_keys.T[:, None, :]
    masked = jnp.where(same_mask[None], spread, 0.0)
    decays = jnp.where(same_mask[None], jnp.exp(masked), 0.0)
    return inner_part[None] * decays * step_keys.T[:, None, :]


AXES = ("replica", "fsdp")


def swap(value, replica_bits, fsdp_bits):
    replicas, owners = lax.axis_size("replica"), lax.axis_size("fsdp")
    pairs = [
        (r * owners + f, (r ^ replica_bits) * owners + (f ^ fsdp_bits))
        for r in range(replicas)
        for f in range(owners)
    ]
    return lax.ppermute(value, AXES, pairs)


def swap_owner(value):
    return swap(value, 0, 1)


def swap_core(value):
    return swap(value, 1, 0)


def join(place, own, other, axis):
    return jnp.where(
        place == 0,
        jnp.concatenate([own, other], axis=axis),
        jnp.concatenate([other, own], axis=axis),
    )


def part_of(value, place, parts, axis):
    size = value.shape[axis] // parts
    return lax.dynamic_slice_in_dim(value, place * size, size, axis)


def chip_bits():
    chips = lax.axis_size("replica") // 2
    return max(chips.bit_length() - 1, 0)


def scatter_sum(block, order):
    chip = lax.axis_index("replica") // 2
    rows, cols = block.shape
    kept = block.reshape((2,) * len(order) + (rows >> len(order), cols))
    for bit in order:
        mine = (chip >> bit) & 1
        sent = lax.dynamic_index_in_dim(kept, 1 - mine, 0, keepdims=False).astype(jnp.bfloat16)
        got = swap(sent, 2 << bit, 0)
        kept = lax.dynamic_index_in_dim(kept, mine, 0, keepdims=False) + got.astype(jnp.float32)
    return kept


def spread(chunk, order):
    chip = lax.axis_index("replica") // 2
    chunk = chunk.astype(jnp.bfloat16)
    for bit in reversed(order):
        chunk = join((chip >> bit) & 1, chunk, swap(chunk, 2 << bit, 0), 0)
    return chunk


def orders():
    first = list(range(chip_bits()))
    second = first[1:2] + first[:1] + first[2:]
    return (first, second)


def total_over_chips(block):
    half = block.shape[0] // 2
    parts = []
    for at, order in enumerate(orders()):
        parts.append(spread(scatter_sum(block[at * half : (at + 1) * half], order), order))
    return jnp.concatenate(parts, axis=0)


def rows_product(left, right):
    return lax.dot_general(
        left, right, (((0,), (0,)), ((), ())), preferred_element_type=jnp.float32
    )


def per_device(
    tokens,
    seq_lens,
    norm_gain,
    in_weight,
    conv_weight,
    conv_bias,
    step_bias,
    decay_log,
    skip_gain,
    out_gain,
    out_weight,
    cotangent,
):
    owner = lax.axis_index("fsdp")
    core = lax.axis_index("replica") % 2
    owners = lax.axis_size("fsdp")
    row_count, width = tokens.shape
    inner_width = out_weight.shape[0] * owners
    channels = conv_bias.shape[0] * owners
    head_count = skip_gain.shape[0] * owners
    state_width = (channels - inner_width) // 2
    head_size = inner_width // head_count
    taps = conv_weight.shape[0]
    pieces = (conv_weight, conv_bias, step_bias, decay_log, skip_gain, out_gain)
    packed = jnp.concatenate([piece.reshape(-1) for piece in pieces])
    packed_other = swap_owner(packed)
    full = []
    at = 0
    for piece in pieces:
        other = packed_other[at : at + piece.size].reshape(piece.shape)
        at += piece.size
        full.append(join(owner, piece, other, piece.ndim - 1).astype(jnp.float32))
    conv_full, shift_full, bias_full, log_full, skip_float, out_scale_full = full
    tokens_pair = jnp.concatenate([tokens, swap_owner(tokens)], axis=0)
    cotangent_pair = jnp.concatenate([cotangent, swap_owner(cotangent)], axis=0)
    values_pair = tokens_pair.astype(jnp.float32)
    inverse_rms = lax.rsqrt(jnp.mean(values_pair * values_pair, axis=-1, keepdims=True) + EPSILON)
    gain_half = norm_gain.astype(jnp.float32)
    means_half = part_of(values_pair, owner, owners, 1) * inverse_rms
    normed_half = (means_half * gain_half).astype(jnp.bfloat16)
    part_rest = jnp.dot(
        normed_half, in_weight[:, inner_width:], preferred_element_type=jnp.float32
    )
    rest_other = swap_owner(part_rest[row_count:].astype(jnp.bfloat16))
    part_gate = jnp.dot(
        normed_half, in_weight[:, :inner_width], preferred_element_type=jnp.float32
    )
    gate_other = swap_owner(part_gate[row_count:].astype(jnp.bfloat16))
    part_q = lax.dot_general(
        cotangent_pair, out_weight, (((1,), (1,)), ((), ())), preferred_element_type=jnp.float32
    )
    q_other = swap_owner(part_q[row_count:].astype(jnp.bfloat16))
    grad_out_normed = join(owner, part_q[:row_count], q_other.astype(jnp.float32), 1)
    rest = part_rest[:row_count] + rest_other.astype(jnp.float32)
    gate_part = part_gate[:row_count] + gate_other.astype(jnp.float32)
    normed_all = jnp.concatenate([normed_half, swap_core(normed_half)], axis=0)
    cotangent_all = jnp.concatenate([cotangent_pair, swap_core(cotangent_pair)], axis=0)

    position, segment, seg_start = segment_layout(seq_lens[0], row_count)
    mixed_in = rest[:, :channels]
    rate_raw = rest[:, channels:]
    prepare = partial(conv_and_rates, position=position, seg_start=seg_start)
    (active, step_size, cumulative), prepare_pullback = jax.vjp(
        prepare, mixed_in, rate_raw, conv_full, shift_full, bias_full, log_full
    )
    x_active = active[:, :inner_width]
    head_input = x_active.reshape(row_count, head_count, head_size).astype(jnp.bfloat16)
    state_input = active[:, inner_width : inner_width + state_width].astype(jnp.bfloat16)
    state_output = active[:, inner_width + state_width :].astype(jnp.bfloat16)
    inner_part = lax.dot_general(
        state_output, state_input, (((1,), (1,)), ((), ())), preferred_element_type=jnp.float32
    )
    same_mask = (position[None, :] <= position[:, None]) & (
        segment[None, :] == segment[:, None]
    )
    mixing_float, mixing_pullback = jax.vjp(
        partial(decay_weights, same_mask=same_mask), inner_part, cumulative, cumulative, step_size
    )
    mixing = mixing_float.astype(jnp.bfloat16)
    scan_parts = jnp.einsum("hts,shp->thp", mixing, head_input, preferred_element_type=jnp.float32)
    scan_out = scan_parts.reshape(row_count, inner_width)
    direct = (
        x_active.reshape(row_count, head_count, head_size) * skip_float[None, :, None]
    ).reshape(row_count, inner_width)
    mixed_out = scan_out + direct
    out_normed, gated_pullback = jax.vjp(gated_norm, mixed_out, gate_part, out_scale_full)
    out_low = out_normed.astype(jnp.bfloat16)
    out_pair = jnp.concatenate(
        [
            part_of(out_low, owner, owners, 1),
            swap_owner(part_of(out_low, 1 - owner, owners, 1)),
        ],
        axis=0,
    )
    branch = jnp.dot(out_pair, out_weight, preferred_element_type=jnp.float32)
    branch_other = swap_owner(branch[row_count:].astype(jnp.bfloat16))
    block_out = (
        values_pair[:row_count] + branch[:row_count] + branch_other.astype(jnp.float32)
    ).astype(jnp.bfloat16)
    out_all = jnp.concatenate(
        [part_of(out_pair, core, 2, 1), swap_core(part_of(out_pair, 1 - core, 2, 1))], axis=0
    )
    out_total = total_over_chips(rows_product(out_all, cotangent_all))

    grad_mixed, grad_gate, out_gain_grad = gated_pullback(grad_out_normed)
    gate_low = grad_gate.astype(jnp.bfloat16)
    gate_pair = jnp.concatenate([gate_low, swap_owner(gate_low)], axis=0)
    gate_all = jnp.concatenate(
        [part_of(gate_pair, core, 2, 1), swap_core(part_of(gate_pair, 1 - core, 2, 1))], axis=0
    )
    gate_total = total_over_chips(rows_product(normed_all, gate_all))
    grad_heads = grad_mixed.reshape(row_count, head_count, head_size)
    skip_gain_grad = jnp.sum(
        grad_heads * x_active.reshape(row_count, head_count, head_size), axis=(0, 2)
    )
    grad_low = grad_heads.astype(jnp.bfloat16)
    grad_input = grad_heads * skip_float[None, :, None]
    grad_mixing = jnp.einsum(
        "thp,shp->hts", grad_low, head_input, preferred_element_type=jnp.float32
    )
    grad_input = grad_input + jnp.einsum(
        "hts,thp->shp", mixing, grad_low, preferred_element_type=jnp.float32
    )
    grad_inner, grad_cum_rows, grad_cum_keys, grad_step_keys = mixing_pullback(grad_mixing)
    grad_inner_low = grad_inner.astype(jnp.bfloat16)
    grad_state_out = jnp.dot(grad_inner_low, state_input, preferred_element_type=jnp.float32)
    grad_state_in = rows_product(grad_inner_low, state_output)
    grad_cum = grad_cum_keys + grad_cum_rows
    grad_active = jnp.concatenate(
        [grad_input.reshape(row_count, inner_width), grad_state_in, grad_state_out], axis=1
    )
    grad_mixed_in, grad_rate_raw, conv_grad, shift_grad, bias_grad, log_grad = prepare_pullback(
        (grad_active, grad_step_keys, grad_cum)
    )
    rest_low = jnp.concatenate([grad_mixed_in, grad_rate_raw], axis=1).astype(jnp.bfloat16)
    rest_pair = jnp.concatenate([rest_low, swap_owner(rest_low)], axis=0)
    mixed_pair, rate_pair = rest_pair[:, :channels], rest_pair[:, channels:]
    rest_all = jnp.concatenate(
        [
            jnp.concatenate([part_of(mixed_pair, core, 2, 1), rate_pair], axis=1),
            swap_core(
                jnp.concatenate([part_of(mixed_pair, 1 - core, 2, 1), rate_pair], axis=1)
            ),
        ],
        axis=0,
    )
    rest_total = total_over_chips(rows_product(normed_all, rest_all))
    grad_normed = lax.dot_general(
        gate_pair,
        in_weight[:, :inner_width],
        (((1,), (1,)), ((), ())),
        preferred_element_type=jnp.float32,
    ) + lax.dot_general(
        rest_pair,
        in_weight[:, inner_width:],
        (((1,), (1,)), ((), ())),
        preferred_element_type=jnp.float32,
    )
    norm_gain_grad = jnp.sum(grad_normed * means_half, axis=0)
    grad_means = grad_normed * gain_half
    grad_means_full = join(
        owner, grad_means[:row_count], swap_owner(grad_means[row_count:]), 1
    )
    means = values_pair[:row_count] * inverse_rms[:row_count]
    grad_values = inverse_rms[:row_count] * (
        grad_means_full
        - means * jnp.mean(grad_means_full * means, axis=-1, keepdims=True)
    )
    grad_tokens = cotangent.astype(jnp.float32) + grad_values
    norm_wide = join(owner, norm_gain_grad, jnp.zeros_like(norm_gain_grad), 0)
    smalls = (norm_wide, conv_grad, shift_grad, bias_grad, log_grad, skip_gain_grad, out_gain_grad)
    sums = lax.psum(jnp.concatenate([item.reshape(-1) for item in smalls]), AXES)
    small_out = []
    at = 0
    for item in smalls:
        whole = sums[at : at + item.size].reshape(item.shape)
        at += item.size
        small_out.append(part_of(whole, owner, owners, item.ndim - 1))
    out_weight_grad = join(core, out_total, swap_core(out_total), 0).astype(jnp.float32)
    gate_full = join(core, gate_total, swap_core(gate_total), 1)
    half_channels = channels // 2
    rest_other_core = swap_core(rest_total)
    mixed_full = join(
        core, rest_total[:, :half_channels], rest_other_core[:, :half_channels], 1
    )
    in_weight_grad = jnp.concatenate(
        [gate_full, mixed_full, rest_total[:, half_channels:]], axis=1
    ).astype(jnp.float32)
    return (
        block_out,
        grad_tokens,
        small_out[0],
        in_weight_grad,
        small_out[1],
        small_out[2],
        small_out[3],
        small_out[4],
        small_out[5],
        small_out[6],
        out_weight_grad,
    )


def solution(mesh):
    placed = (
        P(("replica", "fsdp"), None),
        P(("replica", "fsdp"), None),
        P("fsdp"),
        P("fsdp", None),
        P(None, "fsdp"),
        P("fsdp"),
        P("fsdp"),
        P("fsdp"),
        P("fsdp"),
        P("fsdp"),
        P("fsdp", None),
        P(("replica", "fsdp"), None),
    )
    return jax.shard_map(
        per_device,
        mesh=mesh,
        in_specs=placed,
        out_specs=(
            P(("replica", "fsdp"), None),
            P(("replica", "fsdp"), None),
            P("fsdp"),
            P("fsdp", None),
            P(None, "fsdp"),
            P("fsdp"),
            P("fsdp"),
            P("fsdp"),
            P("fsdp"),
            P("fsdp"),
            P("fsdp", None),
        ),
        check_vma=False,
    )
```

time: 780 us -> 382 us (0.49)
  waiting for transfers between devices: 569 us -> 103 us
  other arithmetic: 21.2 us -> 85.7 us
  blocking collectives: 96.1 us -> 40.6 us
  starting transfers between devices: 0.46 us -> 51.9 us
  local copies, waits for them, and re-layouts: 31 us -> 63.6 us
  between operations: 18.5 us -> 2.77 us
  matrix products: 42.7 us -> 27 us
    reduce_scatter x2 -> x0, waiting for transfers between devices: 266 us -> none  [the longest x1 204 us: per_device(): lax.psum_scatter(in_weight_grad, 'fsdp', scatter_dimension=0, tiled=True)]
    psum x1 -> x0, waiting for transfers between devices: 181 us -> none  [per_device(): lax.psum((shares[0], shares[1], shares[2], shares[3], shares[4], shares[5...]
    all_gather x2 -> x0, waiting for transfers between devices: 118 us -> none  [the longest x1 87.8 us: per_device(): lax.all_gather(in_weight, 'fsdp', axis=0, tiled=True)]
    ppermute x0 -> x55, waiting for transfers between devices: none -> 103 us  [swap(): return lax.ppermute(value, AXES, pairs)]
    ppermute x0 -> x55, starting transfers between devices: none -> 51.9 us  [swap(): return lax.ppermute(value, AXES, pairs)]
    psum x1, blocking collectives: 65 us -> 40.6 us  [per_device(): lax.psum(jnp.concatenate([item.reshape(-1) for item in smalls]), AXES)]
    select_n x0 -> x21, other arithmetic: none -> 18.6 us  [join(): jnp.where(place == 0, jnp.concatenate([own, other], axis=axis), jnp.conca...]
    all_gather x4 -> x0, blocking collectives: 18.3 us -> none  [the longest x1 5.25 us: per_device(): lax.all_gather(conv_weight, 'fsdp', axis=1, tiled=True)]
  transfers between devices with their start and end apart: 6 -> 55, of which waited for: 6 -> 23; matrix products, arithmetic and copies ran while one was open for 10% -> 41% of each run, Pallas kernels for 0% -> 0%
where the time goes in v1:
time: 382 us; the launch traced here: 375 us
  waiting for transfers between devices  103 us (27%)
  other arithmetic  85.7 us (22%)
  local copies, waits for them, and re-layouts  63.6 us (17%)
  starting transfers between devices  51.9 us (14%)
  blocking collectives  40.6 us (11%)
  matrix products  27 us (7%)
    ppermute x55, waiting for transfers between devices, swap(): return lax.ppermute(value, AXES, pairs)  103 us
    ppermute x55, starting transfers between devices, swap(): return lax.ppermute(value, AXES, pairs)  51.9 us
    psum x1, blocking collectives, per_device(): lax.psum(jnp.concatenate([item.reshape(-1) for item in smalls]), AXES)  40.6 us
    unnamed x195, local copies, waits for them, and re-layouts  19.1 us
    select_n x21, other arithmetic, join(): jnp.where(place == 0, jnp.concatenate([own, other], axis=axis), jnp.conca...  18.6 us
  transfers between devices with their start and end apart: 55, of which 23 were waited for; matrix products, arithmetic and copies ran while one was open for 41% of the time, Pallas kernels for 0%

profile of v1, /device:TPU:0, one launch (start us, length us, event | category | flops | bytes accessed | tf_op | source)
XLA Modules:
  0.0 374.7 jit_solution(8296229301308879064)
XLA Ops:
  0.7 3.0 collective-permute-start
  4.4 3.5 concatenate.289
  40.4 12.0 %collective-permute-done.7 = bf16[128,1024]{0,1:T(8,128)(2,1)S(1)} collective-permute-done((bf16[128,1024]{0,1:T(8,128)(2,1)S(1)}, bf16[128,1024]{0,1:T(8,128)(2,1)S(1)}, u32[]{:S(2)}, u32[]{:S(2)}) %collective-permute-start.7) | collective-permute-done | bytes 262176 | tf_op jit(solution)/shard_map/ppermute | solution.py:72
  54.6 4.4 %fusion.121 = (bf16[128,2304]{0,1:T(8,128)(2,1)}, f32[128,2304]{0,1:T(8,128)}, f32[128,2304]{0,1:T(8,128)}) fusion(f32[128,2336]{0,1:T(8,128)S(1)} %slice_add_fusion, pred[128]{0:T(512)(128)(4,1)S(1)} %copy-done.65, f32[2304]{0:T(1024)S(1)} %get-tuple-element.56, f32[127,2304]{0,1:T(8,128)S(1)} %slice.224, pred[128]{0:T(512)(128)(4,1)S(1)} %copy-done.74, ...), kind=kLoop, calls=%fused_computation.286 | loop fusion | flops 5013504 | bytes 7659008 | tf_op jit(solution)/shard_map/convert.6
  88.0 5.9 %fusion.115 = (f32[2304]{0:T(1024)}, f32[2304]{0:T(1024)S(1)}, f32[2304]{0:T(1024)S(1)}, f32[2304]{0:T(1024)S(1)}, f32[2304]{0:T(1024)S(1)}, /*index=5*/f32[128,2304]{0,1:T(8,128)S(1)}) fusion(f32[125,2304]{0,1:T(8,128)} %copy-done.11, pred[128]{0:T(512)(128)(4,1)} %copy-done.71, f32[126,2304]{0,1:T(8,128)} %copy-done.10, pred[128]{0:T(512)(128)(4,1)} %copy-done.75, ...), kind=kLoop, calls=%fused_computation.284 | loop fusion | flops 7066368 | bytes 8248832 | tf_op jit(solution)/shard_map/transpose(jvp())/reduce_sum | solution.py:37
  100.0 3.2 fusion.32
  111.3 15.6 %collective-permute-done.4 = bf16[128,1024]{0,1:T(8,128)(2,1)} collective-permute-done((bf16[128,1024]{0,1:T(8,128)(2,1)}, bf16[128,1024]{0,1:T(8,128)(2,1)}, u32[]{:S(2)}, u32[]{:S(2)}) %collective-permute-start.4) | collective-permute-done | bytes 262176 | tf_op jit(solution)/shard_map/ppermute | solution.py:72
  147.0 40.6 %psum.7 = f32[14688]{0:T(1024)} all-reduce(f32[14688]{0:T(1024)} %concatenate.318), channel_id=1, replica_groups=mesh['replica'=16,'fsdp'=2] {'replica','fsdp'}, use_global_device_ids=true, to_apply=%region_24.25 | all-reduce | flops 14688 | bytes 117504 | tf_op jit(solution)/shard_map/psum | solution.py:313
  202.0 3.0 collective-permute-done.10
  210.5 5.2 %collective-permute-done.43 = bf16[2,32,1024]{2,1,0:T(8,128)(2,1)S(1)} collective-permute-done((bf16[2,32,1024]{2,1,0:T(8,128)(2,1)S(1)}, bf16[2,32,1024]{2,1,0:T(8,128)(2,1)S(1)}, u32[]{:S(2)}, u32[]{:S(2)}) %collective-permute-start.43) | collective-permute-done | bytes 131104 | tf_op jit(solution)/shard_map/ppermute | solution.py:72
  216.8 4.7 %collective-permute-done.50 = bf16[32,1024]{1,0:T(8,128)(2,1)S(1)} collective-permute-done((bf16[32,1024]{1,0:T(8,128)(2,1)S(1)}, bf16[32,1024]{1,0:T(8,128)(2,1)S(1)}, u32[]{:S(2)}, u32[]{:S(2)}) %collective-permute-start.50) | collective-permute-done | bytes 65568 | tf_op jit(solution)/shard_map/ppermute | solution.py:72
  222.0 6.3 %collective-permute-done.44 = bf16[32,1024]{1,0:T(8,128)(2,1)S(1)} collective-permute-done((bf16[32,1024]{1,0:T(8,128)(2,1)S(1)}, bf16[32,1024]{1,0:T(8,128)(2,1)S(1)}, u32[]{:S(2)}, u32[]{:S(2)}) %collective-permute-start.44) | collective-permute-done | bytes 65568 | tf_op jit(solution)/shard_map/ppermute | solution.py:72
  256.7 4.3 %collective-permute-done.20 = bf16[2,32,1024]{2,1,0:T(8,128)(2,1)S(1)} collective-permute-done((bf16[2,32,1024]{2,1,0:T(8,128)(2,1)S(1)}, bf16[2,32,1024]{2,1,0:T(8,128)(2,1)S(1)}, u32[]{:S(2)}, u32[]{:S(2)}) %collective-permute-start.20) | collective-permute-done | bytes 131104 | tf_op jit(solution)/shard_map/ppermute | solution.py:72
  262.4 5.0 %collective-permute-done.14 = bf16[2,32,1024]{2,1,0:T(8,128)(2,1)S(1)} collective-permute-done((bf16[2,32,1024]{2,1,0:T(8,128)(2,1)S(1)}, bf16[2,32,1024]{2,1,0:T(8,128)(2,1)S(1)}, u32[]{:S(2)}, u32[]{:S(2)}) %collective-permute-start.14) | collective-permute-done | bytes 131104 | tf_op jit(solution)/shard_map/ppermute | solution.py:72
  279.6 3.7 collective-permute-done.22
  285.8 4.1 %collective-permute-done.16 = bf16[32,1024]{1,0:T(8,128)(2,1)S(1)} collective-permute-done((bf16[32,1024]{1,0:T(8,128)(2,1)S(1)}, bf16[32,1024]{1,0:T(8,128)(2,1)S(1)}, u32[]{:S(2)}, u32[]{:S(2)}) %collective-permute-start.16) | collective-permute-done | bytes 65568 | tf_op jit(solution)/shard_map/ppermute | solution.py:72
  302.5 6.9 %collective-permute-done.30 = bf16[32,1184]{1,0:T(8,128)(2,1)S(1)} collective-permute-done((bf16[32,1184]{1,0:T(8,128)(2,1)S(1)}, bf16[32,1184]{1,0:T(8,128)(2,1)S(1)}, u32[]{:S(2)}, u32[]{:S(2)}) %collective-permute-start.30) | collective-permute-done | bytes 75808 | tf_op jit(solution)/shard_map/ppermute | solution.py:72
  309.5 5.3 %collective-permute-done.36 = bf16[32,1184]{1,0:T(8,128)(2,1)S(1)} collective-permute-done((bf16[32,1184]{1,0:T(8,128)(2,1)S(1)}, bf16[32,1184]{1,0:T(8,128)(2,1)S(1)}, u32[]{:S(2)}, u32[]{:S(2)}) %collective-permute-start.36) | collective-permute-done | bytes 75808 | tf_op jit(solution)/shard_map/ppermute | solution.py:72
  314.8 5.3 %collective-permute-done.31 = bf16[64,1184]{1,0:T(8,128)(2,1)S(1)} collective-permute-done((bf16[64,1184]{1,0:T(8,128)(2,1)S(1)}, bf16[64,1184]{1,0:T(8,128)(2,1)S(1)}, u32[]{:S(2)}, u32[]{:S(2)}) %collective-permute-start.31) | collective-permute-done | bytes 151584 | tf_op jit(solution)/shard_map/ppermute | solution.py:72
  321.3 4.3 %collective-permute-done.37 = bf16[64,1184]{1,0:T(8,128)(2,1)S(1)} collective-permute-done((bf16[64,1184]{1,0:T(8,128)(2,1)S(1)}, bf16[64,1184]{1,0:T(8,128)(2,1)S(1)}, u32[]{:S(2)}, u32[]{:S(2)}) %collective-permute-start.37) | collective-permute-done | bytes 151584 | tf_op jit(solution)/shard_map/ppermute | solution.py:72
  340.9 3.6 fusion.4
  344.5 10.5 %maximum_select_fusion.1 = bf16[512,2048]{1,0:T(8,128)(2,1)S(1)} fusion(bf16[512,1024]{1,0:T(8,128)(2,1)} %collective-permute-done.25, bf16[256,1024]{1,0:T(8,128)(2,1)S(1)} %copy-done.22, bf16[256,1024]{1,0:T(8,128)(2,1)S(1)} %copy-done.24, pred[]{:T(512)S(6)} %eq.45), kind=kLoop, calls=%fused_computation.6 | loop fusion | flops 13631488 | bytes 4194305 | tf_op jit(solution)/shard_map/jit(_where)/select_n | solution.py:84
  360.7 3.9 %maximum_convert_fusion = f32[512,4384]{1,0:T(8,128)} fusion(bf16[512,32]{1,0:T(8,128)(2,1)S(1)} %fusion.69, bf16[512,2304]{1,0:T(8,128)(2,1)S(1)} %maximum_select_fusion, bf16[512,2048]{1,0:T(8,128)(2,1)S(1)} %maximum_select_fusion.1), kind=kLoop, calls=%fused_computation | loop fusion | flops 13467648 | bytes 13467648 | tf_op jit(solution)/shard_map/convert_element_type | solution.py:329
  364.7 9.6 %copy.78 = f32[512,4384]{0,1:T(8,128)} copy(f32[512,4384]{1,0:T(8,128)} %maximum_convert_fusion) | data formatting | bytes 17956864
  (471 shorter events, 198.1 us)
Async XLA Ops:
  0.7 23.7 %collective-permute-start = (bf16[128,1024]{1,0:T(8,128)(2,1)}, bf16[128,1024]{1,0:T(8,128)(2,1)S(1)}, u32[]{:S(2)}, u32[]{:S(2)}) collective-permute-start(bf16[128,1024]{1,0:T(8,128)(2,1)} %param.12), channel_id=1, source_target_pairs={{0,1},{1,0},{2,3},{3,2},{4,5},{5,4},{6,7},{7,6},{8,9},{9,8},{10,11... | collective-permute-start | bytes 786440 | tf_op jit(solution)/shard_map/ppermute | solution.py:72
  8.0 22.5 %collective-permute-start.6 = (bf16[128,1024]{1,0:T(8,128)(2,1)}, bf16[128,1024]{1,0:T(8,128)(2,1)S(1)}, u32[]{:S(2)}, u32[]{:S(2)}) collective-permute-start(bf16[128,1024]{1,0:T(8,128)(2,1)} %param.23), channel_id=1, source_target_pairs={{0,1},{1,0},{2,3},{3,2},{4,5},{5,4},{6,7},{7,6},{8,9},{9,8},{10,11... | collective-permute-start | bytes 786440 | tf_op jit(solution)/shard_map/ppermute | solution.py:72
  30.3 23.0 %collective-permute-start.2 = (bf16[128,2336]{0,1:T(8,128)(2,1)S(1)}, bf16[128,2336]{0,1:T(8,128)(2,1)S(1)}, u32[]{:S(2)}, u32[]{:S(2)}) collective-permute-start(bf16[128,2336]{0,1:T(8,128)(2,1)S(1)} %slice.349), channel_id=1, source_target_pairs={{0,1},{1,0},{2,3},{3,2},{4,5},{5,4},{6,7},{7,6},{8,9},{9,8},{10,11... | collective-permute-start | bytes 1794056 | tf_op jit(solution)/shard_map/ppermute | solution.py:72
  34.6 193.7 %collective-permute-start.11 = (bf16[256,512]{1,0:T(8,128)(2,1)S(1)}, bf16[256,512]{1,0:T(8,128)(2,1)}, u32[]{:S(2)}, u32[]{:S(2)}) collective-permute-start(bf16[256,512]{1,0:T(8,128)(2,1)S(1)} %multiply_convert_fusion.4), channel_id=1, source_target_pairs={{0,2},{1,3},{2,0},{3,1},{4,6},{5,7},{6,4},{7,5},{8,10},{9,11},{10,... | collective-permute-start | bytes 786440 | tf_op jit(solution)/shard_map/ppermute | solution.py:72
  34.6 99.5 %collective-permute-start.41 = (bf16[256,1024]{1,0:T(8,128)(2,1)}, bf16[256,1024]{1,0:T(8,128)(2,1)}, u32[]{:S(2)}, u32[]{:S(2)}) collective-permute-start(bf16[256,1024]{1,0:T(8,128)(2,1)} %constant_dynamic-update-slice_fusion), channel_id=1, source_target_pairs={{0,2},{1,3},{2,0},{3,1},{4,6},{5,7},{6,4},{7,5},{8,10},{9,11},{10,... | collective-permute-start | bytes 1572872 | tf_op jit(solution)/shard_map/ppermute | solution.py:72
  35.1 17.3 %collective-permute-start.7 = (bf16[128,1024]{0,1:T(8,128)(2,1)S(1)}, bf16[128,1024]{0,1:T(8,128)(2,1)S(1)}, u32[]{:S(2)}, u32[]{:S(2)}) collective-permute-start(bf16[128,1024]{0,1:T(8,128)(2,1)S(1)} %slice.352), channel_id=1, source_target_pairs={{0,1},{1,0},{2,3},{3,2},{4,5},{5,4},{6,7},{7,6},{8,9},{9,8},{10,11... | collective-permute-start | bytes 786440 | tf_op jit(solution)/shard_map/ppermute | solution.py:72
  40.3 28.1 %collective-permute-start.3 = (bf16[128,2048]{0,1:T(8,128)(2,1)}, bf16[128,2048]{0,1:T(8,128)(2,1)}, u32[]{:S(2)}, u32[]{:S(2)}) collective-permute-start(bf16[128,2048]{0,1:T(8,128)(2,1)} %slice.350), channel_id=1, source_target_pairs={{0,1},{1,0},{2,3},{3,2},{4,5},{5,4},{6,7},{7,6},{8,9},{9,8},{10,11... | collective-permute-start | bytes 1572872 | tf_op jit(solution)/shard_map/ppermute | solution.py:72
  98.3 41.3 %collective-permute-start.9 = (bf16[128,2336]{0,1:T(8,128)(2,1)}, bf16[128,2336]{0,1:T(8,128)(2,1)S(1)}, u32[]{:S(2)}, u32[]{:S(2)}) collective-permute-start(bf16[128,2336]{0,1:T(8,128)(2,1)} %pad_maximum_fusion.9), channel_id=1, source_target_pairs={{0,1},{1,0},{2,3},{3,2},{4,5},{5,4},{6,7},{7,6},{8,9},{9,8},{10,11... | collective-permute-start | bytes 1794056 | tf_op jit(solution)/shard_map/ppermute | solution.py:72
  103.1 27.6 %collective-permute-start.8 = (bf16[128,2048]{0,1:T(8,128)(2,1)}, bf16[128,2048]{0,1:T(8,128)(2,1)}, u32[]{:S(2)}, u32[]{:S(2)}) collective-permute-start(bf16[128,2048]{0,1:T(8,128)(2,1)} %get-tuple-element.82), channel_id=1, source_target_pairs={{0,1},{1,0},{2,3},{3,2},{4,5},{5,4},{6,7},{7,6},{8,9},{9,8},{10,11... | collective-permute-start | bytes 1572872 | tf_op jit(solution)/shard_map/ppermute | solution.py:72
  104.4 22.5 %collective-permute-start.4 = (bf16[128,1024]{0,1:T(8,128)(2,1)}, bf16[128,1024]{0,1:T(8,128)(2,1)}, u32[]{:S(2)}, u32[]{:S(2)}) collective-permute-start(bf16[128,1024]{0,1:T(8,128)(2,1)} %get-tuple-element.95), channel_id=1, source_target_pairs={{0,1},{1,0},{2,3},{3,2},{4,5},{5,4},{6,7},{7,6},{8,9},{9,8},{10,11... | collective-permute-start | bytes 786440 | tf_op jit(solution)/shard_map/ppermute | solution.py:72
  131.0 206.5 %collective-permute-start.5 = (bf16[128,1024]{1,0:T(8,128)(2,1)}, bf16[128,1024]{1,0:T(8,128)(2,1)}, u32[]{:S(2)}, u32[]{:S(2)}) collective-permute-start(bf16[128,1024]{1,0:T(8,128)(2,1)} %slice.353), channel_id=1, source_target_pairs={{0,1},{1,0},{2,3},{3,2},{4,5},{5,4},{6,7},{7,6},{8,9},{9,8},{10,11... | collective-permute-start | bytes 786440 | tf_op jit(solution)/shard_map/ppermute | solution.py:72
  134.1 97.2 %collective-permute-start.12 = (bf16[256,1024]{0,1:T(8,128)(2,1)}, bf16[256,1024]{0,1:T(8,128)(2,1)}, u32[]{:S(2)}, u32[]{:S(2)}) collective-permute-start(bf16[256,1024]{0,1:T(8,128)(2,1)} %get-tuple-element.85), channel_id=1, source_target_pairs={{0,2},{1,3},{2,0},{3,1},{4,6},{5,7},{6,4},{7,5},{8,10},{9,11},{10,... | collective-permute-start | bytes 1572872 | tf_op jit(solution)/shard_map/ppermute | solution.py:72
  137.2 60.3 %collective-permute-start.48 = (bf16[2,2,32,1024]{3,2,1,0:T(8,128)(2,1)}, bf16[2,2,32,1024]{3,2,1,0:T(8,128)(2,1)}, u32[]{:S(2)}, u32[]{:S(2)}) collective-permute-start(bf16[2,2,32,1024]{3,2,1,0:T(8,128)(2,1)} %fusion.59), channel_id=1, source_target_pairs={{0,8},{1,9},{2,10},{3,11},{4,12},{5,13},{6,14},{7,15},{8,0},{9,1},... | collective-permute-start | bytes 786440 | tf_op jit(solution)/shard_map/ppermute | solution.py:72
  139.6 61.2 %collective-permute-start.42 = (bf16[2,2,32,1024]{3,2,1,0:T(8,128)(2,1)}, bf16[2,2,32,1024]{3,2,1,0:T(8,128)(2,1)}, u32[]{:S(2)}, u32[]{:S(2)}) collective-permute-start(bf16[2,2,32,1024]{3,2,1,0:T(8,128)(2,1)} %fusion.58), channel_id=1, source_target_pairs={{0,4},{1,5},{2,6},{3,7},{4,0},{5,1},{6,2},{7,3},{8,12},{9,13},{10,... | collective-permute-start | bytes 786440 | tf_op jit(solution)/shard_map/ppermute | solution.py:72
  200.8 44.2 %collective-permute-start.26 = (bf16[256,1184]{0,1:T(8,128)(2,1)S(1)}, bf16[256,1184]{0,1:T(8,128)(2,1)S(1)}, u32[]{:S(2)}, u32[]{:S(2)}) collective-permute-start(bf16[256,1184]{0,1:T(8,128)(2,1)S(1)} %pad_maximum_fusion.8), channel_id=1, source_target_pairs={{0,2},{1,3},{2,0},{3,1},{4,6},{5,7},{6,4},{7,5},{8,10},{9,11},{10,... | collective-permute-start | bytes 1818632 | tf_op jit(solution)/shard_map/ppermute | solution.py:72
  234.2 18.1 %collective-permute-start.19 = (bf16[2,2,32,1024]{3,2,1,0:T(8,128)(2,1)}, bf16[2,2,32,1024]{3,2,1,0:T(8,128)(2,1)}, u32[]{:S(2)}, u32[]{:S(2)}) collective-permute-start(bf16[2,2,32,1024]{3,2,1,0:T(8,128)(2,1)} %fusion.57), channel_id=1, source_target_pairs={{0,8},{1,9},{2,10},{3,11},{4,12},{5,13},{6,14},{7,15},{8,0},{9,1},... | collective-permute-start | bytes 786440 | tf_op jit(solution)/shard_map/ppermute | solution.py:72
  243.3 25.7 %collective-permute-start.53 = (bf16[128,1024]{1,0:T(8,128)(2,1)}, bf16[128,1024]{1,0:T(8,128)(2,1)}, u32[]{:S(2)}, u32[]{:S(2)}) collective-permute-start(bf16[128,1024]{1,0:T(8,128)(2,1)} %maximum_select_fusion.16), channel_id=1, source_target_pairs={{0,8},{1,9},{2,10},{3,11},{4,12},{5,13},{6,14},{7,15},{8,0},{9,1},... | collective-permute-start | bytes 786440 | tf_op jit(solution)/shard_map/ppermute | solution.py:72
  245.0 26.2 %collective-permute-start.47 = (bf16[128,1024]{1,0:T(8,128)(2,1)}, bf16[128,1024]{1,0:T(8,128)(2,1)}, u32[]{:S(2)}, u32[]{:S(2)}) collective-permute-start(bf16[128,1024]{1,0:T(8,128)(2,1)} %maximum_select_fusion.15), channel_id=1, source_target_pairs={{0,4},{1,5},{2,6},{3,7},{4,0},{5,1},{6,2},{7,3},{8,12},{9,13},{10,... | collective-permute-start | bytes 786440 | tf_op jit(solution)/shard_map/ppermute | solution.py:72
  252.3 23.8 %collective-permute-start.27 = (bf16[2,2,32,1184]{3,2,1,0:T(8,128)(2,1)}, bf16[2,2,32,1184]{3,2,1,0:T(8,128)(2,1)S(1)}, u32[]{:S(2)}, u32[]{:S(2)}) collective-permute-start(bf16[2,2,32,1184]{3,2,1,0:T(8,128)(2,1)} %fusion.54), channel_id=1, source_target_pairs={{0,4},{1,5},{2,6},{3,7},{4,0},{5,1},{6,2},{7,3},{8,12},{9,13},{10,... | collective-permute-start | bytes 909320 | tf_op jit(solution)/shard_map/ppermute | solution.py:72
  276.1 63.9 %collective-permute-start.54 = (bf16[512,1024]{1,0:T(8,128)(2,1)}, bf16[512,1024]{1,0:T(8,128)(2,1)}, u32[]{:S(2)}, u32[]{:S(2)}) collective-permute-start(bf16[512,1024]{1,0:T(8,128)(2,1)} %pad_maximum_fusion.6), channel_id=1, source_target_pairs={{0,2},{1,3},{2,0},{3,1},{4,6},{5,7},{6,4},{7,5},{8,10},{9,11},{10,... | collective-permute-start | bytes 3145736 | tf_op jit(solution)/shard_map/ppermute | solution.py:72
  276.2 15.1 %collective-permute-start.28 = (bf16[2,32,1184]{2,1,0:T(8,128)(2,1)S(1)}, bf16[2,32,1184]{2,1,0:T(8,128)(2,1)S(1)}, u32[]{:S(2)}, u32[]{:S(2)}) collective-permute-start(bf16[2,32,1184]{2,1,0:T(8,128)(2,1)S(1)} %fusion.65), channel_id=1, source_target_pairs={{0,8},{1,9},{2,10},{3,11},{4,12},{5,13},{6,14},{7,15},{8,0},{9,1},... | collective-permute-start | bytes 454664 | tf_op jit(solution)/shard_map/ppermute | solution.py:72
  298.2 28.4 %collective-permute-start.24 = (bf16[128,1024]{1,0:T(8,128)(2,1)S(1)}, bf16[128,1024]{1,0:T(8,128)(2,1)S(1)}, u32[]{:S(2)}, u32[]{:S(2)}) collective-permute-start(bf16[128,1024]{1,0:T(8,128)(2,1)S(1)} %maximum_select_fusion.14), channel_id=1, source_target_pairs={{0,8},{1,9},{2,10},{3,11},{4,12},{5,13},{6,14},{7,15},{8,0},{9,1},... | collective-permute-start | bytes 786440 | tf_op jit(solution)/shard_map/ppermute | solution.py:72
  298.2 30.1 %collective-permute-start.18 = (bf16[128,1024]{1,0:T(8,128)(2,1)S(1)}, bf16[128,1024]{1,0:T(8,128)(2,1)S(1)}, u32[]{:S(2)}, u32[]{:S(2)}) collective-permute-start(bf16[128,1024]{1,0:T(8,128)(2,1)S(1)} %maximum_select_fusion.13), channel_id=1, source_target_pairs={{0,4},{1,5},{2,6},{3,7},{4,0},{5,1},{6,2},{7,3},{8,12},{9,13},{10,... | collective-permute-start | bytes 786440 | tf_op jit(solution)/shard_map/ppermute | solution.py:72
  337.5 17.6 %collective-permute-start.39 = (bf16[512,1184]{0,1:T(8,128)(2,1)}, bf16[512,1184]{0,1:T(8,128)(2,1)S(1)}, u32[]{:S(2)}, u32[]{:S(2)}) collective-permute-start(bf16[512,1184]{0,1:T(8,128)(2,1)} %copy.76), channel_id=1, source_target_pairs={{0,2},{1,3},{2,0},{3,1},{4,6},{5,7},{6,4},{7,5},{8,10},{9,11},{10,... | collective-permute-start | bytes 3637256 | tf_op jit(solution)/shard_map/ppermute | solution.py:72
  (129 other events, 794.8 us)

commit v2 on v0

v2 whole, which is shorter than its diff:
```python
import jax
import jax.numpy as jnp
from jax import lax
from jax.experimental import pallas as pl
from jax.experimental.pallas import tpu as pltpu
from jax.sharding import PartitionSpec as P

EPSILON = 1e-05
AXES = ("replica", "fsdp")
OWNER, LENGTH_ONE, LENGTH_TWO, CORE, BITS = 0, 1, 2, 3, 4
LANES = 128
FAR = -1e30


def full_rows(meta_ref, mine_ref, peer_ref):
    first = meta_ref[0] == 0
    mine, peer = mine_ref[...], peer_ref[...]
    return (jnp.where(first, mine, peer), jnp.where(first, peer, mine), mine + peer)


def row_marks(meta_ref, rows):
    end_one, end_two = meta_ref[1], meta_ref[1] + meta_ref[2]
    position = lax.broadcasted_iota(jnp.int32, (rows, 1), 0)
    start = jnp.where(position >= end_two, end_two, jnp.where(position >= end_one, end_one, 0))
    return (position, start)


def kept_pairs(start, rows):
    key = lax.broadcasted_iota(jnp.int32, (rows, rows), 1)
    query = lax.broadcasted_iota(jnp.int32, (rows, rows), 0)
    return (key <= query) & (key >= start)


def channel_row(low, high, row, tile):
    half = low.shape[1] // LANES
    source = low if tile < half else high
    at = (tile if tile < half else tile - half) * LANES
    return source[row : row + 1, at : at + LANES]


def exact_dot(left, right):
    return jnp.dot(
        left, right, precision=lax.Precision.HIGHEST, preferred_element_type=jnp.float32
    )


def pair_operand(values, lane):
    zero = jnp.zeros_like(values)
    return jnp.concatenate(
        [jnp.where(lane < LANES // 2, values, zero), jnp.where(lane < LANES // 2, zero, values)],
        axis=0,
    )


def forward_body(meta_ref, own_ref, got_ref, mine_ref, peer_ref, xbc_ref, conv_ref, mixed_ref, rates_ref):
    rows, channels = conv_ref.shape
    tiles = channels // LANES
    pairs = tiles - 2
    heads = 2 * pairs
    taps = 4
    low, high, both = full_rows(meta_ref, mine_ref, peer_ref)
    position, start = row_marks(meta_ref, rows)
    usable = [position - (taps - 1 - k) >= start for k in range(taps)]
    lane = lax.broadcasted_iota(jnp.int32, (1, LANES), 1)
    bias = both[6:7, 0:heads]
    decay = both[6:7, LANES : LANES + heads]
    skip = both[6:7, 2 * LANES : 2 * LANES + heads]
    rate = own_ref[:, channels:] + got_ref[:, channels:].astype(jnp.float32) + bias
    step = jnp.maximum(rate, 0.0) + jnp.log1p(jnp.exp(-jnp.abs(rate)))
    rate_sigmoid = jax.nn.sigmoid(rate)
    lower = jnp.where(
        lax.broadcasted_iota(jnp.int32, (rows, rows), 1)
        <= lax.broadcasted_iota(jnp.int32, (rows, rows), 0),
        1.0,
        0.0,
    ).astype(jnp.float32)
    cum = exact_dot(lower, step * -jnp.exp(decay))
    rates_ref[0] = step
    rates_ref[1] = cum
    rates_ref[2] = rate_sigmoid
    step_t, cum_t = step.T, cum.T
    mask = kept_pairs(start, rows)

    def active_tile(tile):
        at = tile * LANES
        xbc = own_ref[:, at : at + LANES] + got_ref[:, at : at + LANES].astype(jnp.float32)
        xbc_ref[:, at : at + LANES] = xbc
        conv = channel_row(low, high, 4, tile) + channel_row(low, high, taps - 1, tile) * xbc
        for k in range(taps - 1):
            shifted = pltpu.roll(xbc, taps - 1 - k, 0)
            conv = conv + channel_row(low, high, k, tile) * jnp.where(usable[k], shifted, 0.0)
        conv_ref[:, at : at + LANES] = conv
        return conv * jax.nn.sigmoid(conv)

    keys = active_tile(tiles - 2).astype(jnp.bfloat16)
    queries = active_tile(tiles - 1).astype(jnp.bfloat16)
    inner = lax.dot_general(
        queries, keys, (((1,), (1,)), ((), ())), preferred_element_type=jnp.float32
    )
    for pair in range(pairs):
        act = active_tile(pair)
        mixing = []
        for h in (2 * pair, 2 * pair + 1):
            spread = jnp.where(mask, cum[:, h : h + 1] - cum_t[h : h + 1, :], FAR)
            mixing.append((inner * jnp.exp(spread) * step_t[h : h + 1, :]).astype(jnp.bfloat16))
        scan = jnp.dot(
            jnp.concatenate(mixing, axis=1),
            pair_operand(act.astype(jnp.bfloat16), lane),
            preferred_element_type=jnp.float32,
        )
        gain = jnp.where(
            lane < LANES // 2, skip[:, 2 * pair : 2 * pair + 1], skip[:, 2 * pair + 1 : 2 * pair + 2]
        )
        mixed_ref[:, pair * LANES : (pair + 1) * LANES] = scan + gain * act


def gate_body(meta_ref, mixed_ref, own_ref, got_ref, q_own_ref, q_got_ref, mine_ref, peer_ref, keep_ref, send_ref, dgate_ref, dmixed_ref, gain_grad_ref):
    rows, inner_width = mixed_ref.shape
    half = inner_width // 2
    first = meta_ref[0] == 0
    low, high, _ = full_rows(meta_ref, mine_ref, peer_ref)
    width = 2 * LANES
    tiles = inner_width // width

    def cut(tile):
        return slice(tile * width, (tile + 1) * width)

    def gate_of(tile):
        gate = own_ref[:, cut(tile)] + got_ref[:, cut(tile)].astype(jnp.float32)
        return (gate, jax.nn.sigmoid(gate))

    def half_cut(tile):
        at = tile * width % half
        return slice(at, at + width)

    def gain_of(tile):
        return (low if tile * width < half else high)[5:6, half_cut(tile)]

    def q_of(tile):
        own = q_own_ref[:, half_cut(tile)]
        got = q_got_ref[:, half_cut(tile)].astype(jnp.float32)
        return jnp.where(first == (tile * width < half), own, got)

    squares = jnp.zeros((rows, 1), jnp.float32)
    cross = jnp.zeros((rows, 1), jnp.float32)
    for tile in range(tiles):
        gate, sigmoid = gate_of(tile)
        gated = mixed_ref[:, cut(tile)] * (gate * sigmoid)
        squares = squares + jnp.sum(gated * gated, axis=1, keepdims=True)
        cross = cross + jnp.sum(q_of(tile) * gain_of(tile) * gated, axis=1, keepdims=True)
    inverse = lax.rsqrt(squares / inner_width + EPSILON)
    mean_cross = cross * inverse / inner_width
    for tile in range(tiles):
        gate, sigmoid = gate_of(tile)
        silu = gate * sigmoid
        mixed = mixed_ref[:, cut(tile)]
        normed = mixed * silu * inverse
        gain = gain_of(tile)
        out = (normed * gain).astype(jnp.bfloat16)
        in_low = tile * width < half

        @pl.when(first == in_low)
        def _():
            keep_ref[:, half_cut(tile)] = out

        @pl.when(first != in_low)
        def _():
            send_ref[:, half_cut(tile)] = out

        q = q_of(tile)
        gain_grad_ref[:, cut(tile)] = jnp.sum(q * normed, axis=0, keepdims=True)
        dgated = inverse * (q * gain - normed * mean_cross)
        dmixed_ref[:, cut(tile)] = dgated * silu
        dgate_ref[tile * width // half, :, half_cut(tile)] = (
            dgated * mixed * (sigmoid * (1.0 + gate * (1.0 - sigmoid)))
        ).astype(jnp.bfloat16)


def backward_body(meta_ref, dmixed_ref, xbc_ref, conv_ref, rates_ref, mine_ref, peer_ref, gain_grad_ref, rest_ref, small_ref):
    rows, channels = conv_ref.shape
    tiles = channels // LANES
    pairs = tiles - 2
    heads = 2 * pairs
    taps = 4
    half_tiles = tiles // 2
    small_ref[...] = jnp.zeros(small_ref.shape, jnp.float32)
    low, high, both = full_rows(meta_ref, mine_ref, peer_ref)
    position, start = row_marks(meta_ref, rows)
    usable = [position - (taps - 1 - k) >= start for k in range(taps)]
    lane = lax.broadcasted_iota(jnp.int32, (1, LANES), 1)
    decay = both[6:7, LANES : LANES + heads]
    skip = both[6:7, 2 * LANES : 2 * LANES + heads]
    step, cum, rate_sigmoid = rates_ref[0], rates_ref[1], rates_ref[2]
    step_t, cum_t = step.T, cum.T
    mask = kept_pairs(start, rows)

    def cut(tile):
        return slice(tile * LANES, (tile + 1) * LANES)

    def act_of(tile):
        conv = conv_ref[:, cut(tile)]
        sigmoid = jax.nn.sigmoid(conv)
        return (conv * sigmoid, sigmoid * (1.0 + conv * (1.0 - sigmoid)))

    def finish_tile(tile, dconv):
        owner, at = tile // half_tiles, tile % half_tiles * LANES
        xbc = xbc_ref[:, cut(tile)]
        small_ref[owner, 4:5, at : at + LANES] = jnp.sum(dconv, axis=0, keepdims=True)
        small_ref[owner, taps - 1 : taps, at : at + LANES] = jnp.sum(
            dconv * xbc, axis=0, keepdims=True
        )
        total = channel_row(low, high, taps - 1, tile) * dconv
        for k in range(taps - 1):
            behind = taps - 1 - k
            kept = jnp.where(usable[k], dconv, 0.0)
            small_ref[owner, k : k + 1, at : at + LANES] = jnp.sum(
                kept * pltpu.roll(xbc, behind, 0), axis=0, keepdims=True
            )
            total = total + channel_row(low, high, k, tile) * pltpu.roll(kept, rows - behind, 0)
        rest_ref[owner, :, at : at + LANES] = total.astype(jnp.bfloat16)

    keys_act, keys_slope = act_of(tiles - 2)
    queries_act, queries_slope = act_of(tiles - 1)
    keys, queries = keys_act.astype(jnp.bfloat16), queries_act.astype(jnp.bfloat16)
    inner = lax.dot_general(
        queries, keys, (((1,), (1,)), ((), ())), preferred_element_type=jnp.float32
    )
    dinner = jnp.zeros((rows, rows), jnp.float32)
    dstep_rows = []
    dcum = jnp.zeros((rows, heads), jnp.float32)
    skip_grad = jnp.zeros((1, heads), jnp.float32)
    head_lane = lax.broadcasted_iota(jnp.int32, (1, heads), 1)
    for pair in range(pairs):
        act, slope = act_of(pair)
        dmixed = dmixed_ref[:, cut(pair)]
        dscan = dmixed.astype(jnp.bfloat16)
        operand = pair_operand(act.astype(jnp.bfloat16), lane)
        dmixing = lax.dot_general(
            dscan, operand, (((1,), (1,)), ((), ())), preferred_element_type=jnp.float32
        )
        direct = jnp.sum(dmixed * act, axis=0, keepdims=True)
        mixing = []
        for j in range(2):
            h = 2 * pair + j
            spread = jnp.where(mask, cum[:, h : h + 1] - cum_t[h : h + 1, :], FAR)
            decays = jnp.exp(spread)
            step_row = step_t[h : h + 1, :]
            weight = inner * decays
            mixing.append((weight * step_row).astype(jnp.bfloat16))
            grad = dmixing[:, j * rows : (j + 1) * rows]
            dinner = dinner + grad * decays * step_row
            term = grad * weight
            dstep_rows.append(jnp.sum(term, axis=0, keepdims=True))
            dcum = dcum + jnp.where(
                head_lane == h, jnp.sum(term * step_row, axis=1, keepdims=True), 0.0
            )
            in_head = (lane < LANES // 2) if j == 0 else (lane >= LANES // 2)
            skip_grad = skip_grad + jnp.where(
                head_lane == h,
                jnp.sum(jnp.where(in_head, direct, 0.0), axis=1, keepdims=True),
                0.0,
            )
        dinput = lax.dot_general(
            jnp.concatenate(mixing, axis=1),
            dscan,
            (((0,), (0,)), ((), ())),
            preferred_element_type=jnp.float32,
        )
        gain = jnp.where(
            lane < LANES // 2, skip[:, 2 * pair : 2 * pair + 1], skip[:, 2 * pair + 1 : 2 * pair + 2]
        )
        dact = jnp.where(lane < LANES // 2, dinput[:rows], dinput[rows:]) + gain * dmixed
        finish_tile(pair, dact * slope)
    dinner_low = dinner.astype(jnp.bfloat16)
    dqueries = jnp.dot(dinner_low, keys, preferred_element_type=jnp.float32)
    dkeys = lax.dot_general(
        dinner_low, queries, (((0,), (0,)), ((), ())), preferred_element_type=jnp.float32
    )
    finish_tile(tiles - 2, dkeys * keys_slope)
    finish_tile(tiles - 1, dqueries * queries_slope)
    dstep_t = jnp.concatenate(dstep_rows, axis=0)
    dstep = dstep_t.T
    dcum = dcum - step * dstep
    upper = jnp.where(
        lax.broadcasted_iota(jnp.int32, (rows, rows), 1)
        >= lax.broadcasted_iota(jnp.int32, (rows, rows), 0),
        1.0,
        0.0,
    ).astype(jnp.float32)
    drate = exact_dot(upper, dcum)
    speed = jnp.exp(decay)
    draw = (dstep - drate * speed) * rate_sigmoid
    for owner in range(2):
        rest_ref[owner, :, channels // 2 :] = draw.astype(jnp.bfloat16)
    bias_grad = jnp.sum(draw, axis=0, keepdims=True)
    decay_grad = jnp.sum(-drate * step * speed, axis=0, keepdims=True)
    half_inner = pairs * LANES // 2
    half_heads = heads // 2
    for owner in range(2):
        small_ref[owner, 5:6, 0:half_inner] = gain_grad_ref[
            :, owner * half_inner : (owner + 1) * half_inner
        ]
        for place, item in enumerate((bias_grad, decay_grad, skip_grad)):
            at = place * LANES
            small_ref[owner, 6:7, at : at + half_heads] = item[
                :, owner * half_heads : (owner + 1) * half_heads
            ]


def whole(shape, dtype):
    return jax.ShapeDtypeStruct(shape, dtype)


def call(body, out_shape, operands, flops):
    in_specs = [pl.BlockSpec(memory_space=pltpu.SMEM)] + [
        pl.BlockSpec(memory_space=pltpu.VMEM) for _ in operands[1:]
    ]
    moved = sum(item.size * item.dtype.itemsize for item in (*operands, *out_shape))
    return pl.pallas_call(
        body,
        out_shape=out_shape,
        in_specs=in_specs,
        out_specs=[pl.BlockSpec(memory_space=pltpu.VMEM) for _ in out_shape],
        compiler_params=pltpu.CompilerParams(vmem_limit_bytes=40 << 20),
        cost_estimate=pl.CostEstimate(flops=flops, bytes_accessed=moved, transcendentals=0),
    )(*operands)


def unit_rows(tokens):
    values = tokens.astype(jnp.float32)
    return lax.rsqrt(jnp.mean(values * values, axis=-1, keepdims=True) + EPSILON)


def project_body(meta_ref, tokens_ref, gain_ref, weight_ref, normed_ref, rest_ref, gate_ref):
    depth = weight_ref.shape[0]
    inner_width = gate_ref.shape[1]
    inverse = unit_rows(tokens_ref[...])
    mine = pl.ds(pl.multiple_of(meta_ref[OWNER] * depth, LANES), depth)
    means = tokens_ref[:, mine].astype(jnp.float32) * inverse
    normed = (means * gain_ref[...]).astype(jnp.bfloat16)
    normed_ref[...] = normed
    rest_ref[...] = jnp.dot(
        normed, weight_ref[:, inner_width:], preferred_element_type=jnp.float32
    ).astype(rest_ref.dtype)
    gate_ref[...] = jnp.dot(
        normed, weight_ref[:, :inner_width], preferred_element_type=jnp.float32
    ).astype(gate_ref.dtype)


def lanes_product(left, right):
    return lax.dot_general(
        left, right, (((1,), (1,)), ((), ())), preferred_element_type=jnp.float32
    )


def rows_product(left, right):
    return lax.dot_general(
        left, right, (((0,), (0,)), ((), ())), preferred_element_type=jnp.float32
    )


def cotangent_body(meta_ref, own_ref, other_ref, weight_ref, q_own_ref, q_send_ref):
    q_own_ref[...] = lanes_product(own_ref[...], weight_ref[...])
    q_send_ref[...] = lanes_product(other_ref[...], weight_ref[...]).astype(q_send_ref.dtype)


def branch_body(meta_ref, keep_ref, got_ref, weight_ref, own_ref, send_ref):
    own_ref[...] = jnp.dot(
        keep_ref[...], weight_ref[...], preferred_element_type=jnp.float32
    )
    send_ref[...] = jnp.dot(
        got_ref[...], weight_ref[...], preferred_element_type=jnp.float32
    ).astype(send_ref.dtype)


def input_grad_body(meta_ref, tokens_ref, other_ref, gain_ref, weight_ref, gate_own_ref, gate_got_ref, rest_own_ref, rest_got_ref, dmeans_ref, send_ref, gain_grad_ref):
    depth = weight_ref.shape[0]
    half_inner = gate_own_ref.shape[2]
    half_rest = rest_own_ref.shape[2] - (weight_ref.shape[1] - 2 * half_inner) % LANES
    mine = pl.ds(pl.multiple_of(meta_ref[OWNER] * depth, LANES), depth)
    gain = gain_ref[...]
    gain_grad = jnp.zeros_like(gain)
    for rows_ref, gate_ref, rest_ref, out_ref in (
        (other_ref, gate_got_ref, rest_got_ref, send_ref),
        (tokens_ref, gate_own_ref, rest_own_ref, dmeans_ref),
    ):
        dnormed = jnp.zeros(out_ref.shape, jnp.float32)
        at = 0
        for part in (
            gate_ref[0],
            gate_ref[1],
            rest_ref[0, :, :half_rest],
            rest_ref[1, :, :half_rest],
            rest_ref[0, :, half_rest:],
        ):
            width = part.shape[1]
            dnormed = dnormed + lanes_product(part, weight_ref[:, at : at + width])
            at += width
        means = rows_ref[:, mine].astype(jnp.float32) * unit_rows(rows_ref[...])
        gain_grad = gain_grad + jnp.sum(dnormed * means, axis=0, keepdims=True)
        out_ref[...] = dnormed * gain
    gain_grad_ref[...] = gain_grad


def tokens_grad_body(meta_ref, tokens_ref, cotangent_ref, own_ref, got_ref, out_ref):
    half = own_ref.shape[1]
    first = meta_ref[OWNER] == 0
    inverse = unit_rows(tokens_ref[...])
    parts = []
    cross = jnp.zeros_like(inverse)
    for side in range(2):
        cut = slice(side * half, (side + 1) * half)
        dmeans = jnp.where(first == (side == 0), own_ref[...], got_ref[...])
        means = tokens_ref[:, cut].astype(jnp.float32) * inverse
        cross = cross + jnp.sum(dmeans * means, axis=1, keepdims=True)
        parts.append((cut, dmeans, means))
    for cut, dmeans, means in parts:
        out_ref[:, cut] = cotangent_ref[:, cut].astype(jnp.float32) + inverse * (
            dmeans - means * (cross / (2 * half))
        )


def block_grad(left_refs, right_refs, left_at, core, outs, bits):
    half = 2 * LANES
    right = jnp.concatenate(
        [ref[...] if len(ref.shape) == 2 else ref[core] for ref in right_refs], axis=0
    )
    for order, (send_ref, keep_ref) in enumerate(outs):
        for ref, bit in ((send_ref, 1 - bits[order]), (keep_ref, bits[order])):
            cut = order * half + bit * LANES
            left = jnp.concatenate(
                [
                    left_ref[:, pl.ds(pl.multiple_of(at + cut, LANES), LANES)]
                    for left_ref, at in zip(left_refs, left_at)
                ],
                axis=0,
            )
            ref[...] = rows_product(left, right).astype(ref.dtype)


def block_grad_body(quarter_left, meta_ref, l_own, l_got, l_sib, r_own, r_got, r_sib, send_a, keep_a, send_b, keep_b):
    core = meta_ref[CORE]
    at = core * l_sib.shape[1] if quarter_left else 0
    block_grad(
        (l_own, l_got, l_sib),
        (r_own, r_got, r_sib),
        (at, at, 0),
        core,
        ((send_a, keep_a), (send_b, keep_b)),
        (meta_ref[BITS], meta_ref[BITS + 1]),
    )


def sum_step_body(step, meta_ref, keep_a, got_a, keep_b, got_b, *outs):
    if step == 2:
        for keep, got, out in ((keep_a, got_a, outs[0]), (keep_b, got_b, outs[1])):
            out[...] = (keep[...] + got[...].astype(jnp.float32)).astype(out.dtype)
        return
    rows = keep_a.shape[0] // 2
    bits = (
        (meta_ref[BITS + 1], meta_ref[BITS]) if step == 0 else (meta_ref[BITS + 2],) * 2
    )
    for order, (keep, got) in enumerate(((keep_a, got_a), (keep_b, got_b))):
        for out, bit in ((outs[2 * order], 1 - bits[order]), (outs[2 * order + 1], bits[order])):
            cut = pl.ds(pl.multiple_of(bit * rows, rows), rows)
            out[...] = (keep[cut, :] + got[cut, :].astype(jnp.float32)).astype(out.dtype)


def chunk_places(meta_ref, order):
    outer, inner = meta_ref[BITS + 1 - order], meta_ref[BITS + 2]
    places = []
    for p in range(4):
        high = outer if p < 2 else 1 - outer
        low = inner if p % 2 == 0 else 1 - inner
        places.append(2 * high + low)
    return places


def write_chunks(meta_ref, order, half, out_ref, groups):
    own_half = meta_ref[BITS + order] == half
    for p, place in enumerate(chunk_places(meta_ref, order)):
        size = LANES // 4
        rows = slice(p * size, (p + 1) * size)
        target = pl.ds(pl.multiple_of(place * size, size), size)
        for cut, choose in groups:
            out_ref[target, cut] = choose(own_half, rows).astype(jnp.float32)


def in_weight_body(meta_ref, *refs):
    out_ref = refs[-1]
    gate, rest = refs[0:8], refs[8:16]
    first = meta_ref[CORE] == 0
    step = pl.program_id(0)
    half_inner = gate[0].shape[1]
    half_channels = rest[0].shape[1] // LANES * LANES
    tail = rest[0].shape[1] - half_channels

    def chooser(group, order, side, cut):
        own, got, sib_own, sib_got = group[4 * order : 4 * order + 4]

        def choose(own_half, rows):
            mine = jnp.where(own_half, own[rows, cut], got[rows, cut])
            sibling = jnp.where(own_half, sib_own[rows, cut], sib_got[rows, cut])
            return jnp.where(first == (side == 0), mine, sibling)

        return choose

    for order in range(2):
        for half in range(2):

            @pl.when(step == 2 * order + half)
            def _():
                groups = []
                for side in range(2):
                    at = side * half_inner
                    groups.append(
                        (
                            slice(at, at + half_inner),
                            chooser(gate, order, side, slice(0, half_inner)),
                        )
                    )
                    at = 2 * half_inner + side * half_channels
                    groups.append(
                        (
                            slice(at, at + half_channels),
                            chooser(rest, order, side, slice(0, half_channels)),
                        )
                    )
                at = 2 * half_inner + 2 * half_channels
                groups.append(
                    (
                        slice(at, at + tail),
                        chooser(rest, order, 0, slice(half_channels, half_channels + tail)),
                    )
                )
                write_chunks(meta_ref, order, half, out_ref, groups)


def out_weight_body(meta_ref, *refs):
    out_ref = refs[-1]
    pieces = refs[:-1]
    step = pl.program_id(0)
    cut = slice(0, out_ref.shape[1])
    for side in range(2):
        for order in range(2):
            for half in range(2):

                @pl.when(step == 4 * side + 2 * order + half)
                def _():
                    own, got, sib_own, sib_got = pieces[4 * order : 4 * order + 4]

                    def choose(own_half, rows):
                        mine = jnp.where(own_half, own[rows, :], got[rows, :])
                        sibling = jnp.where(own_half, sib_own[rows, :], sib_got[rows, :])
                        return jnp.where((meta_ref[CORE] == 0) == (side == 0), mine, sibling)

                    write_chunks(meta_ref, order, half, out_ref, [(cut, choose)])


def assemble(body, out, operands):
    return pl.pallas_call(
        body,
        grid=(out.shape[0] // LANES,),
        out_shape=out,
        in_specs=[pl.BlockSpec(memory_space=pltpu.SMEM)]
        + [pl.BlockSpec(item.shape, lambda i: (0, 0)) for item in operands[1:]],
        out_specs=pl.BlockSpec((LANES, out.shape[1]), lambda i: (i, 0)),
        compiler_params=pltpu.CompilerParams(vmem_limit_bytes=48 << 20),
        cost_estimate=pl.CostEstimate(
            flops=out.size, bytes_accessed=out.size * 6, transcendentals=0
        ),
    )(*operands)


def swap(value, replica_bits, fsdp_bits):
    replicas, owners = lax.axis_size("replica"), lax.axis_size("fsdp")
    pairs = [
        (r * owners + f, (r ^ replica_bits) * owners + (f ^ fsdp_bits))
        for r in range(replicas)
        for f in range(owners)
    ]
    return lax.ppermute(value, AXES, pairs)


def swap_owner(value):
    return swap(value, 0, 1)


def swap_core(value):
    return swap(value, 1, 0)


def swap_chip(value, bit):
    return swap(value, 2 << bit, 0)


def join(place, own, other, axis):
    return jnp.where(
        place == 0,
        jnp.concatenate([own, other], axis=axis),
        jnp.concatenate([other, own], axis=axis),
    )


def part_of(value, place, parts, axis):
    size = value.shape[axis] // parts
    return lax.dynamic_slice_in_dim(value, place * size, size, axis)


def total_over_chips(block):
    chip = lax.axis_index("replica") // 2
    bits = range((lax.axis_size("replica") // 2).bit_length() - 1)
    rows, cols = block.shape
    kept = block.reshape((2,) * len(bits) + (rows >> len(bits), cols))
    for bit in bits:
        mine = (chip >> bit) & 1
        sent = lax.dynamic_index_in_dim(kept, 1 - mine, 0, keepdims=False).astype(jnp.bfloat16)
        got = swap_chip(sent, bit)
        kept = lax.dynamic_index_in_dim(kept, mine, 0, keepdims=False) + got.astype(jnp.float32)
    chunk = kept.astype(jnp.bfloat16)
    for bit in reversed(bits):
        chunk = join((chip >> bit) & 1, chunk, swap_chip(chunk, bit), 0)
    return chunk


def eight_chip_pieces(meta, left, right, quarter_left):
    f32, low = jnp.float32, jnp.bfloat16
    cols = right[2].shape[1]

    def pieces(rows):
        return [whole((rows, cols), low), whole((rows, cols), f32)] * 2

    def body(*refs):
        block_grad_body(quarter_left, *refs)

    send_a, keep_a, send_b, keep_b = call(body, pieces(LANES), (meta, *left, *right), 512 * 1024 * cols)
    got_a, got_b = swap_chip(send_a, 0), swap_chip(send_b, 1)

    def first(*refs):
        sum_step_body(0, *refs)

    def second(*refs):
        sum_step_body(1, *refs)

    def third(*refs):
        sum_step_body(2, *refs)

    send_a, keep_a, send_b, keep_b = call(
        first, pieces(LANES // 2), (meta, keep_a, got_a, keep_b, got_b), 0
    )
    got_a, got_b = swap_chip(send_a, 1), swap_chip(send_b, 0)
    send_a, keep_a, send_b, keep_b = call(
        second, pieces(LANES // 4), (meta, keep_a, got_a, keep_b, got_b), 0
    )
    got_a, got_b = swap_chip(send_a, 2), swap_chip(send_b, 2)
    sums = call(
        third, [whole((LANES // 4, cols), low)] * 2, (meta, keep_a, got_a, keep_b, got_b), 0
    )
    out = []
    for chunk, order in zip(sums, ((2, 1, 0), (2, 0, 1))):
        for bit in order[:2]:
            chunk = jnp.concatenate([chunk, swap_chip(chunk, bit)], axis=0)
        got = swap_chip(chunk, order[2])
        out += [chunk, got, swap_core(chunk), swap_core(got)]
    return out


def per_device(
    tokens,
    seq_lens,
    norm_gain,
    in_weight,
    conv_weight,
    conv_bias,
    step_bias,
    decay_log,
    skip_gain,
    out_gain,
    out_weight,
    cotangent,
):
    f32, low = jnp.float32, jnp.bfloat16
    owner = lax.axis_index("fsdp")
    replica = lax.axis_index("replica")
    core, chip = replica % 2, replica // 2
    chips = lax.axis_size("replica") // 2
    rows, width = tokens.shape
    half_inner = out_weight.shape[0]
    inner_width = 2 * half_inner
    half_channels = conv_bias.shape[0]
    channels = 2 * half_channels
    half_heads = skip_gain.shape[0]
    heads = 2 * half_heads
    rest_width = channels + heads
    meta = jnp.stack(
        [owner, seq_lens[0, 0], seq_lens[0, 1], core, chip & 1, (chip >> 1) & 1, (chip >> 2) & 1]
    ).astype(jnp.int32)

    def row(item):
        item = item.astype(f32).reshape(-1, item.shape[-1])
        return jnp.pad(item, ((0, 0), (0, half_channels - item.shape[-1])))

    def head_row(item):
        item = item.astype(f32)
        there = jnp.zeros_like(item)
        placed = jnp.where(
            owner == 0, jnp.concatenate([item, there]), jnp.concatenate([there, item])
        )
        return jnp.pad(placed, (0, LANES - heads))

    head_rows = jnp.concatenate([head_row(step_bias), head_row(decay_log), head_row(skip_gain)])
    mine = jnp.concatenate(
        [
            row(conv_weight),
            row(conv_bias),
            row(out_gain),
            row(head_rows),
            jnp.zeros((1, half_channels), f32),
        ],
        axis=0,
    )
    tokens_other = swap_owner(tokens)
    peer = swap_owner(mine)
    held, _ = lax.optimization_barrier((cotangent, tokens_other))
    cotangent_other = swap_owner(held)
    gain = norm_gain.astype(f32).reshape(1, -1)

    def project(source, dtype):
        return call(
            project_body,
            [
                whole((rows, width // 2), low),
                whole((rows, rest_width), dtype),
                whole((rows, inner_width), dtype),
            ],
            (meta, source, gain, in_weight),
            rows * width * (rest_width + inner_width),
        )

    normed_own, rest_own, gate_own = project(tokens, f32)
    normed_other, rest_send, gate_send = project(tokens_other, low)
    rest_got = swap_owner(rest_send)
    q_own, q_send = call(
        cotangent_body,
        [whole((rows, half_inner), f32), whole((rows, half_inner), low)],
        (meta, cotangent, cotangent_other, out_weight),
        4 * rows * width * half_inner,
    )
    q_got = swap_owner(q_send)
    gate_got = swap_owner(gate_send)
    normed_sib = swap_core(jnp.concatenate([normed_own, normed_other], axis=0))
    cotangent_sib = swap_core(jnp.concatenate([cotangent, cotangent_other], axis=0))

    xbc, conv, mixed, rates = call(
        forward_body,
        [
            whole((rows, channels), f32),
            whole((rows, channels), f32),
            whole((rows, inner_width), f32),
            whole((3, rows, heads), f32),
        ],
        (meta, rest_own, rest_got, mine, peer),
        10**9,
    )
    out_keep, out_send, dgate, dmixed, gain_grad = call(
        gate_body,
        [
            whole((rows, half_inner), low),
            whole((rows, half_inner), low),
            whole((2, rows, half_inner), low),
            whole((rows, inner_width), f32),
            whole((1, inner_width), f32),
        ],
        (meta, mixed, gate_own, gate_got, q_own, q_got, mine, peer),
        10**9,
    )
    out_got = swap_owner(out_send)
    dgate_got = swap_owner(dgate)
    drest, small = call(
        backward_body,
        [
            whole((2, rows, half_channels + heads), low),
            whole((2, 8, half_channels), f32),
        ],
        (meta, dmixed, xbc, conv, rates, mine, peer, gain_grad),
        10**9,
    )
    drest_got = swap_owner(drest)
    out_sib = swap_core(
        jnp.concatenate(
            [part_of(out_keep, 1 - core, 2, 1), part_of(out_got, 1 - core, 2, 1)], axis=0
        )
    )

    def sibling_part(own, got):
        return swap_core(
            jnp.concatenate(
                [
                    lax.dynamic_index_in_dim(own, 1 - core, 0, keepdims=False),
                    lax.dynamic_index_in_dim(got, 1 - core, 0, keepdims=False),
                ],
                axis=0,
            )
        )

    dgate_sib = sibling_part(dgate, dgate_got)
    drest_sib = sibling_part(drest, drest_got)
    normed_all = (normed_own, normed_other, normed_sib)
    out_sources = ((out_keep, out_got, out_sib), (cotangent, cotangent_other, cotangent_sib))
    gate_sources = (normed_all, (dgate, dgate_got, dgate_sib))
    rest_sources = (normed_all, (drest, drest_got, drest_sib))
    if chips == 8:
        out_pieces = eight_chip_pieces(meta, *out_sources, True)
        gate_pieces = eight_chip_pieces(meta, *gate_sources, False)
        rest_pieces = eight_chip_pieces(meta, *rest_sources, False)
        in_weight_grad = assemble(
            in_weight_body, whole(in_weight.shape, f32), (meta, *gate_pieces, *rest_pieces)
        )
        out_weight_grad = assemble(
            out_weight_body, whole(out_weight.shape, f32), (meta, *out_pieces)
        )
    else:

        def block_of(left, right, quarter_left):
            if quarter_left:
                left = (part_of(left[0], core, 2, 1), part_of(left[1], core, 2, 1), left[2])
            else:
                right = (right[0][core], right[1][core], right[2])
            return total_over_chips(
                rows_product(jnp.concatenate(left, axis=0), jnp.concatenate(right, axis=0))
            )

        out_total = block_of(*out_sources, True)
        gate_total = block_of(*gate_sources, False)
        rest_total = block_of(*rest_sources, False)
        rest_sib = swap_core(rest_total)
        out_weight_grad = join(core, out_total, swap_core(out_total), 0).astype(f32)
        in_weight_grad = jnp.concatenate(
            [
                join(core, gate_total, swap_core(gate_total), 1),
                join(core, rest_total[:, :half_channels], rest_sib[:, :half_channels], 1),
                rest_total[:, half_channels:],
            ],
            axis=1,
        ).astype(f32)

    branch_own, branch_send = call(
        branch_body,
        [whole((rows, width), f32), whole((rows, width), low)],
        (meta, out_keep, out_got, out_weight),
        4 * rows * width * half_inner,
    )
    branch_got = swap_owner(branch_send)
    block_out = (tokens.astype(f32) + branch_own + branch_got.astype(f32)).astype(low)

    dmeans_own, dmeans_send, norm_grad = call(
        input_grad_body,
        [
            whole((rows, width // 2), f32),
            whole((rows, width // 2), f32),
            whole((1, width // 2), f32),
        ],
        (meta, tokens, tokens_other, gain, in_weight, dgate, dgate_got, drest, drest_got),
        4 * rows * width * (rest_width + inner_width),
    )
    (grad_tokens,) = call(
        tokens_grad_body,
        [whole((rows, width), f32)],
        (meta, tokens, cotangent, dmeans_own, swap_owner(dmeans_send)),
        0,
    )

    total = lax.dynamic_index_in_dim(small, owner, 0, keepdims=False) + swap_owner(
        lax.dynamic_index_in_dim(small, 1 - owner, 0, keepdims=False)
    )
    total = jnp.concatenate([total[:7], row(norm_grad)], axis=0)
    bit = 1
    while bit < 2 * chips:
        total = total + swap(total, bit, 0)
        bit *= 2
    return (
        block_out,
        grad_tokens,
        total[7, : width // 2],
        in_weight_grad,
        total[0:4],
        total[4],
        total[6, 0:half_heads],
        total[6, LANES : LANES + half_heads],
        total[6, 2 * LANES : 2 * LANES + half_heads],
        total[5, :half_inner],
        out_weight_grad,
    )


def solution(mesh):
    placed = (
        P(("replica", "fsdp"), None),
        P(("replica", "fsdp"), None),
        P("fsdp"),
        P("fsdp", None),
        P(None, "fsdp"),
        P("fsdp"),
        P("fsdp"),
        P("fsdp"),
        P("fsdp"),
        P("fsdp"),
        P("fsdp", None),
        P(("replica", "fsdp"), None),
    )
    return jax.shard_map(
        per_device,
        mesh=mesh,
        in_specs=placed,
        out_specs=(
            P(("replica", "fsdp"), None),
            P(("replica", "fsdp"), None),
            P("fsdp"),
            P("fsdp", None),
            P(None, "fsdp"),
            P("fsdp"),
            P("fsdp"),
            P("fsdp"),
            P("fsdp"),
            P("fsdp"),
            P("fsdp", None),
        ),
        check_vma=False,
    )
```

time: 780 us -> 263 us (0.34)
  waiting for transfers between devices: 569 us -> 96.9 us
  blocking collectives: 96.1 us -> 0 us
  starting transfers between devices: 0.46 us -> 51.7 us
  Pallas kernels: 0 us -> 49.5 us
  matrix products: 42.7 us -> 0 us
  local copies, waits for them, and re-layouts: 31 us -> 52 us
  between operations: 18.5 us -> 1.49 us
  other arithmetic: 21.2 us -> 9.51 us
    reduce_scatter x2 -> x0, waiting for transfers between devices: 266 us -> none  [the longest x1 204 us: per_device(): lax.psum_scatter(in_weight_grad, 'fsdp', scatter_dimension=0, tiled=True)]
    psum x1 -> x0, waiting for transfers between devices: 181 us -> none  [per_device(): lax.psum((shares[0], shares[1], shares[2], shares[3], shares[4], shares[5...]
    all_gather x2 -> x0, waiting for transfers between devices: 118 us -> none  [the longest x1 87.8 us: per_device(): lax.all_gather(in_weight, 'fsdp', axis=0, tiled=True)]
    ppermute x0 -> x69, waiting for transfers between devices: none -> 96.9 us  [swap(): return lax.ppermute(value, AXES, pairs)]
    psum x1 -> x0, blocking collectives: 65 us -> none  [per_device(): lax.psum((shares[0], shares[1], shares[2], shares[3], shares[4], shares[5...]
    ppermute x0 -> x69, starting transfers between devices: none -> 51.7 us  [swap(): return lax.ppermute(value, AXES, pairs)]
    pallas_call x0 -> x23, Pallas kernels: none -> 49.5 us  [the longest x21 40.6 us: call(): pl.pallas_call(body, out_shape=out_shape, in_specs=in_specs, out_specs=[p...]
    dot_general x12 -> x0, matrix products: 42.7 us -> none  [the longest x1 8.78 us: per_device(): lax.dot_general(normed, grad_projected, (((0,), (0,)), ((), ())), preferr...]
  transfers between devices with their start and end apart: 6 -> 69, of which waited for: 6 -> 30; matrix products, arithmetic and copies ran while one was open for 10% -> 15% of each run, Pallas kernels for 0% -> 16%
where the time goes in v2:
time: 263 us; the launch traced here: 261 us
  waiting for transfers between devices  96.9 us (37%)
  local copies, waits for them, and re-layouts  52 us (20%)
  starting transfers between devices  51.7 us (20%)
  Pallas kernels  49.5 us (19%)
  other arithmetic  9.51 us (4%)
    ppermute x69, waiting for transfers between devices, swap(): return lax.ppermute(value, AXES, pairs)  96.9 us
    ppermute x69, starting transfers between devices, swap(): return lax.ppermute(value, AXES, pairs)  51.7 us
    pallas_call x21, Pallas kernels, call(): pl.pallas_call(body, out_shape=out_shape, in_specs=in_specs, out_specs=[p...  40.6 us
    unnamed x92, local copies, waits for them, and re-layouts  28.3 us
    pallas_call x2, Pallas kernels, assemble(): pl.pallas_call(body, grid=(out.shape[0] // LANES,), out_shape=out, in_spe...  8.97 us
  transfers between devices with their start and end apart: 69, of which 30 were waited for; matrix products, arithmetic and copies ran while one was open for 15% of the time, Pallas kernels for 16%

profile of v2, /device:TPU:0, one launch (start us, length us, event | category | flops | bytes accessed | tf_op | source)
XLA Modules:
  0.0 261.2 jit_solution(7930371239732901487)
XLA Ops:
  0.6 3.0 %collective-permute-start = (bf16[128,1024]{1,0:T(8,128)(2,1)}, bf16[128,1024]{1,0:T(8,128)(2,1)S(1)}, u32[]{:S(2)}, u32[]{:S(2)}) collective-permute-start(bf16[128,1024]{1,0:T(8,128)(2,1)} %tokens_ref.5), channel_id=1, source_target_pairs={{0,1},{1,0},{2,3},{3,2},{4,5},{5,4},{6,7},{7,6},{8,9},{9,8},{10,11... | collective-permute-start | bytes 786440 | tf_op jit(solution)/shard_map/ppermute | solution.py:582
  5.6 6.5 %copy.37.weight_ref = bf16[512,4384]{1,0:T(8,128)(2,1)} copy(bf16[512,4384]{0,1:T(8,128)(2,1)} %param.15) | data formatting | bytes 8978432 | tf_op args[3]
  28.0 13.5 %collective-permute-done.4.other_ref.refs_5_ = bf16[128,1024]{1,0:T(8,128)(2,1)S(1)} collective-permute-done((bf16[128,1024]{1,0:T(8,128)(2,1)S(1)}, bf16[128,1024]{1,0:T(8,128)(2,1)S(1)}, u32[]{:S(2)}, u32[]{:S(2)}) %collective-permute-start.4) | collective-permute-done | bytes 262176 | tf_op jit(solution)/shard_map/ppermute | solution.py:582
  47.9 5.8 %collective-permute-done.2.peer_ref = f32[8,1152]{1,0:T(8,128)} collective-permute-done((f32[8,1152]{1,0:T(8,128)}, f32[8,1152]{1,0:T(8,128)}, u32[]{:S(2)}, u32[]{:S(2)}) %collective-permute-start.2) | collective-permute-done | bytes 36896 | tf_op jit(solution)/shard_map/ppermute | solution.py:582
  55.0 3.0 %shard_map.205 = (f32[128,2304]{1,0:T(8,128)S(1)}, f32[128,2304]{1,0:T(8,128)S(1)}, f32[128,2048]{1,0:T(8,128)S(1)}, f32[3,128,32]{2,1,0:T(8,128)S(1)}) custom-call(s32[7]{0:T(128)S(1)} %stack.23.meta_ref.refs_0_, f32[128,2336]{1,0:T(8,128)S(1)} %copy-done.21, bf16[128,2336]{1,0:T(8,128)(2,1)S(1)} %copy.40.got_ref, f32[8,1152]{1,0:T(8,128)} %concatenate.91.mine_ref, ...), custom_call_target="tpu_custom_call" | custom-call | flops 1000000000 | bytes 5324828 | tf_op jit(solution)/shard_map/pallas_call | solution.py:319
  58.0 3.7 %shard_map.207 = (bf16[128,1024]{1,0:T(8,128)(2,1)S(1)}, bf16[128,1024]{1,0:T(8,128)(2,1)S(1)}, bf16[2,128,1024]{2,1,0:T(8,128)(2,1)}, f32[128,2048]{1,0:T(8,128)S(1)}, f32[1,2048]{1,0:T(1,128)S(1)}) custom-call(s32[7]{0:T(128)S(1)} %stack.23.meta_ref.refs_0_, f32[128,2048]{1,0:T(8,128)S(1)} %get-tuple-element.80.mixed_ref, f32[128,2048]{1,0:T(8,128)S(1)} %copy-done.23, ...), custom_call_target="tpu_custom_call" | custom-call | flops 1000000000 | bytes 5586972 | tf_op jit(solution)/shard_map/pallas_call | solution.py:319
  62.5 6.6 %shard_map.209 = (bf16[2,128,1184]{2,1,0:T(8,128)(2,1)S(1)}, f32[2,8,1152]{2,1,0:T(8,128)S(1)}) custom-call(s32[7]{0:T(128)S(1)} %stack.23.meta_ref.refs_0_, f32[128,2048]{1,0:T(8,128)S(1)} %get-tuple-element.91.dmixed_ref, f32[128,2304]{1,0:T(8,128)S(1)} %get-tuple-element.92.xbc_ref, f32[128,2304]{1,0:T(8,128)S(1)} %get-tuple-element.93.conv_ref, ...), custom_call_target="tpu_custom_call" | custom-call | flops 1000000000 | bytes 4218908 | tf_op jit(solution)/shard_map/pallas_call | solution.py:319
  99.8 4.3 %shard_map.210 = (f32[128,512]{1,0:T(8,128)S(1)}, f32[128,512]{1,0:T(8,128)S(1)}, f32[1,512]{1,0:T(1,128)S(1)}) custom-call(s32[7]{0:T(128)S(1)} %stack.23.meta_ref.refs_0_, bf16[128,1024]{1,0:T(8,128)(2,1)S(1)} %copy-done.4, bf16[128,1024]{1,0:T(8,128)(2,1)S(1)} %copy-done.14, f32[1,512]{1,0:T(1,128)S(1)} %bitcast.29, bf16[512,4384]{1,0:T(8,128)(2,1)S(1)} %copy-done.2, ...), custom_call_target="tpu_custom_call" | custom-call | flops 2298478592 | bytes 7802908 | tf_op jit(solution)/shard_map/pallas_call | solution.py:319
  109.6 5.8 %collective-permute-done.53.refs_2_ = bf16[128,1024]{1,0:T(8,128)(2,1)S(1)} collective-permute-done((bf16[128,1024]{1,0:T(8,128)(2,1)S(1)}, bf16[128,1024]{1,0:T(8,128)(2,1)S(1)}, u32[]{:S(2)}, u32[]{:S(2)}) %collective-permute-start.53) | collective-permute-done | bytes 262176 | tf_op jit(solution)/shard_map/ppermute | solution.py:582
  141.5 3.0 %collective-permute-done.18.refs_2_ = bf16[128,1024]{1,0:T(8,128)(2,1)S(1)} collective-permute-done((bf16[128,1024]{1,0:T(8,128)(2,1)S(1)}, bf16[128,1024]{1,0:T(8,128)(2,1)S(1)}, u32[]{:S(2)}, u32[]{:S(2)}) %collective-permute-start.18) | collective-permute-done | bytes 262176 | tf_op jit(solution)/shard_map/ppermute | solution.py:582
  163.3 3.6 %collective-permute-done.23.refs_4_ = bf16[32,1024]{1,0:T(8,128)(2,1)S(1)} collective-permute-done((bf16[32,1024]{1,0:T(8,128)(2,1)S(1)}, bf16[32,1024]{1,0:T(8,128)(2,1)S(1)}, u32[]{:S(2)}, u32[]{:S(2)}) %collective-permute-start.23) | collective-permute-done | bytes 65568 | tf_op jit(solution)/shard_map/ppermute | solution.py:582
  167.7 3.0 %collective-permute-start.29 = (bf16[32,1024]{1,0:T(8,128)(2,1)S(1)}, bf16[32,1024]{1,0:T(8,128)(2,1)S(1)}, u32[]{:S(2)}, u32[]{:S(2)}) collective-permute-start(bf16[32,1024]{1,0:T(8,128)(2,1)S(1)} %get-tuple-element.116), channel_id=1, source_target_pairs={{0,16},{1,17},{2,18},{3,19},{4,20},{5,21},{6,22},{7,23},{8,24},{9,... | collective-permute-start | bytes 196616 | tf_op jit(solution)/shard_map/ppermute | solution.py:582
  179.7 2.8 %collective-permute-start.39 = (bf16[32,1184]{1,0:T(8,128)(2,1)S(1)}, bf16[32,1184]{1,0:T(8,128)(2,1)S(1)}, u32[]{:S(2)}, u32[]{:S(2)}) collective-permute-start(bf16[32,1184]{1,0:T(8,128)(2,1)S(1)} %get-tuple-element.126), channel_id=1, source_target_pairs={{0,16},{1,17},{2,18},{3,19},{4,20},{5,21},{6,22},{7,23},{8,24},{9,... | collective-permute-start | bytes 227336 | tf_op jit(solution)/shard_map/ppermute | solution.py:582
  182.7 2.8 %collective-permute-done.39.refs_2_ = bf16[32,1184]{1,0:T(8,128)(2,1)S(1)} collective-permute-done((bf16[32,1184]{1,0:T(8,128)(2,1)S(1)}, bf16[32,1184]{1,0:T(8,128)(2,1)S(1)}, u32[]{:S(2)}, u32[]{:S(2)}) %collective-permute-start.39) | collective-permute-done | bytes 75808 | tf_op jit(solution)/shard_map/ppermute | solution.py:582
  190.1 6.0 %collective-permute-done.41 = bf16[32,1184]{1,0:T(8,128)(2,1)S(1)} collective-permute-done((bf16[32,1184]{1,0:T(8,128)(2,1)S(1)}, bf16[32,1184]{1,0:T(8,128)(2,1)S(1)}, u32[]{:S(2)}, u32[]{:S(2)}) %collective-permute-start.41) | collective-permute-done | bytes 75808 | tf_op jit(solution)/shard_map/ppermute | solution.py:582
  196.1 5.4 %collective-permute-done.46 = bf16[32,1184]{1,0:T(8,128)(2,1)S(1)} collective-permute-done((bf16[32,1184]{1,0:T(8,128)(2,1)S(1)}, bf16[32,1184]{1,0:T(8,128)(2,1)S(1)}, u32[]{:S(2)}, u32[]{:S(2)}) %collective-permute-start.46) | collective-permute-done | bytes 75808 | tf_op jit(solution)/shard_map/ppermute | solution.py:582
  204.0 9.9 %collective-permute-done.42 = bf16[64,1184]{1,0:T(8,128)(2,1)S(1)} collective-permute-done((bf16[64,1184]{1,0:T(8,128)(2,1)S(1)}, bf16[64,1184]{1,0:T(8,128)(2,1)S(1)}, u32[]{:S(2)}, u32[]{:S(2)}) %collective-permute-start.42) | collective-permute-done | bytes 151584 | tf_op jit(solution)/shard_map/ppermute | solution.py:582
  216.2 4.7 %collective-permute-done.47 = bf16[64,1184]{1,0:T(8,128)(2,1)S(1)} collective-permute-done((bf16[64,1184]{1,0:T(8,128)(2,1)S(1)}, bf16[64,1184]{1,0:T(8,128)(2,1)S(1)}, u32[]{:S(2)}, u32[]{:S(2)}) %collective-permute-start.47) | collective-permute-done | bytes 151584 | tf_op jit(solution)/shard_map/ppermute | solution.py:582
  221.0 2.8 %collective-permute-done.30 = bf16[64,1024]{1,0:T(8,128)(2,1)S(1)} collective-permute-done((bf16[64,1024]{1,0:T(8,128)(2,1)S(1)}, bf16[64,1024]{1,0:T(8,128)(2,1)S(1)}, u32[]{:S(2)}, u32[]{:S(2)}) %collective-permute-start.30) | collective-permute-done | bytes 131104 | tf_op jit(solution)/shard_map/ppermute | solution.py:582
  225.9 3.5 %collective-permute-done.26.refs_1_ = bf16[128,1024]{1,0:T(8,128)(2,1)S(1)} collective-permute-done((bf16[128,1024]{1,0:T(8,128)(2,1)S(1)}, bf16[128,1024]{1,0:T(8,128)(2,1)S(1)}, u32[]{:S(2)}, u32[]{:S(2)}) %collective-permute-start.26) | collective-permute-done | bytes 262176 | tf_op jit(solution)/shard_map/ppermute | solution.py:582
  231.7 5.4 %collective-permute-done.31.refs_5_ = bf16[128,1024]{1,0:T(8,128)(2,1)S(1)} collective-permute-done((bf16[128,1024]{1,0:T(8,128)(2,1)S(1)}, bf16[128,1024]{1,0:T(8,128)(2,1)S(1)}, u32[]{:S(2)}, u32[]{:S(2)}) %collective-permute-start.31) | collective-permute-done | bytes 262176 | tf_op jit(solution)/shard_map/ppermute | solution.py:582
  242.7 4.3 %shard_map.225 = f32[1024,1024]{1,0:T(8,128)} custom-call(s32[7]{0:T(128)S(1)} %stack.23.meta_ref.refs_0_, bf16[128,1024]{1,0:T(8,128)(2,1)S(1)} %constant_dynamic-update-slice_fusion.12.refs_0_, bf16[128,1024]{1,0:T(8,128)(2,1)S(1)} %collective-permute-done.61.refs_1_, bf16[128,1024]{1,0:T(8,128)(2,1)S(1)} %collective-permute-done.62.refs_2_, ...), custom_call_target="tpu_custom_call" | custom-call | flops 1048576 | bytes 6291456 | tf_op jit(solution)/shard_map/pallas_call | solution.py:561
  247.0 4.7 %shard_map.220 = f32[512,4384]{1,0:T(8,128)} custom-call(s32[7]{0:T(128)S(1)} %stack.23.meta_ref.refs_0_, bf16[128,1024]{1,0:T(8,128)(2,1)S(1)} %constant_dynamic-update-slice_fusion.refs_0_, bf16[128,1024]{1,0:T(8,128)(2,1)S(1)} %collective-permute-done.26.refs_1_, bf16[128,1024]{1,0:T(8,128)(2,1)S(1)} %collective-permute-done.27.refs_2_, ...), custom_call_target="tpu_custom_call" | custom-call | flops 2244608 | bytes 13467648 | tf_op jit(solution)/shard_map/pallas_call | solution.py:561
  251.7 9.4 %copy.47 = f32[512,4384]{0,1:T(8,128)} copy(f32[512,4384]{1,0:T(8,128)} %shard_map.220) | data formatting | bytes 17956864
  (287 shorter events, 136.1 us)
Async XLA Ops:
  19.3 26.6 %collective-permute-start.1 = (bf16[128,2336]{0,1:T(8,128)(2,1)}, bf16[128,2336]{0,1:T(8,128)(2,1)}, u32[]{:S(2)}, u32[]{:S(2)}) collective-permute-start(bf16[128,2336]{0,1:T(8,128)(2,1)} %copy.39), channel_id=1, source_target_pairs={{0,1},{1,0},{2,3},{3,2},{4,5},{5,4},{6,7},{7,6},{8,9},{9,8},{10,11... | collective-permute-start | bytes 1794056 | tf_op jit(solution)/shard_map/ppermute | solution.py:582
  19.4 22.1 %collective-permute-start.4 = (bf16[128,1024]{1,0:T(8,128)(2,1)S(1)}, bf16[128,1024]{1,0:T(8,128)(2,1)S(1)}, u32[]{:S(2)}, u32[]{:S(2)}) collective-permute-start(bf16[128,1024]{1,0:T(8,128)(2,1)S(1)} %copy-done.5), channel_id=1, source_target_pairs={{0,1},{1,0},{2,3},{3,2},{4,5},{5,4},{6,7},{7,6},{8,9},{9,8},{10,11... | collective-permute-start | bytes 786440 | tf_op jit(solution)/shard_map/ppermute | solution.py:582
  21.6 36.4 %collective-permute-start.3 = (bf16[128,2048]{1,0:T(8,128)(2,1)}, bf16[128,2048]{1,0:T(8,128)(2,1)}, u32[]{:S(2)}, u32[]{:S(2)}) collective-permute-start(bf16[128,2048]{1,0:T(8,128)(2,1)} %get-tuple-element.82), channel_id=1, source_target_pairs={{0,1},{1,0},{2,3},{3,2},{4,5},{5,4},{6,7},{7,6},{8,9},{9,8},{10,11... | collective-permute-start | bytes 1572872 | tf_op jit(solution)/shard_map/ppermute | solution.py:582
  22.3 31.4 %collective-permute-start.2 = (f32[8,1152]{1,0:T(8,128)}, f32[8,1152]{1,0:T(8,128)}, u32[]{:S(2)}, u32[]{:S(2)}) collective-permute-start(f32[8,1152]{1,0:T(8,128)} %concatenate.91.mine_ref), channel_id=1, source_target_pairs={{0,1},{1,0},{2,3},{3,2},{4,5},{5,4},{6,7},{7,6},{8,9},{9,8},{10,11... | collective-permute-start | bytes 110600 | tf_op jit(solution)/shard_map/ppermute | solution.py:582
  44.3 13.7 %collective-permute-start.5 = (bf16[128,1024]{1,0:T(8,128)(2,1)}, bf16[128,1024]{1,0:T(8,128)(2,1)}, u32[]{:S(2)}, u32[]{:S(2)}) collective-permute-start(bf16[128,1024]{1,0:T(8,128)(2,1)} %get-tuple-element.85), channel_id=1, source_target_pairs={{0,1},{1,0},{2,3},{3,2},{4,5},{5,4},{6,7},{7,6},{8,9},{9,8},{10,11... | collective-permute-start | bytes 786440 | tf_op jit(solution)/shard_map/ppermute | solution.py:582
  45.1 87.9 %collective-permute-start.16 = (bf16[256,512]{1,0:T(8,128)(2,1)}, bf16[256,512]{1,0:T(8,128)(2,1)}, u32[]{:S(2)}, u32[]{:S(2)}) collective-permute-start(bf16[256,512]{1,0:T(8,128)(2,1)} %pad_maximum_fusion.3), channel_id=1, source_target_pairs={{0,2},{1,3},{2,0},{3,1},{4,6},{5,7},{6,4},{7,5},{8,10},{9,11},{10,... | collective-permute-start | bytes 786440 | tf_op jit(solution)/shard_map/ppermute | solution.py:582
  45.9 58.3 %collective-permute-start.52 = (bf16[256,1024]{1,0:T(8,128)(2,1)}, bf16[256,1024]{1,0:T(8,128)(2,1)}, u32[]{:S(2)}, u32[]{:S(2)}) collective-permute-start(bf16[256,1024]{1,0:T(8,128)(2,1)} %pad_maximum_fusion.2), channel_id=1, source_target_pairs={{0,2},{1,3},{2,0},{3,1},{4,6},{5,7},{6,4},{7,5},{8,10},{9,11},{10,... | collective-permute-start | bytes 1572872 | tf_op jit(solution)/shard_map/ppermute | solution.py:582
  62.5 27.5 %collective-permute-start.8 = (bf16[2,128,1024]{2,1,0:T(8,128)(2,1)}, bf16[2,128,1024]{2,1,0:T(8,128)(2,1)}, u32[]{:S(2)}, u32[]{:S(2)}) collective-permute-start(bf16[2,128,1024]{2,1,0:T(8,128)(2,1)} %get-tuple-element.90.gate_own_ref.refs_4_), channel_id=1, source_target_pairs={{0,1},{1,0},{2,3},{3,2},{4,5},{5,4},{6,7},{7,6},{8,9},{9,8},{10,11... | collective-permute-start | bytes 1572872 | tf_op jit(solution)/shard_map/ppermute | solution.py:582
  81.4 13.8 %collective-permute-start.9 = (bf16[2,128,1184]{1,2,0:T(8,128)(2,1)}, bf16[2,128,1184]{1,2,0:T(8,128)(2,1)}, u32[]{:S(2)}, u32[]{:S(2)}) collective-permute-start(bf16[2,128,1184]{1,2,0:T(8,128)(2,1)} %copy.41), channel_id=1, source_target_pairs={{0,1},{1,0},{2,3},{3,2},{4,5},{5,4},{6,7},{7,6},{8,9},{9,8},{10,11... | collective-permute-start | bytes 1818632 | tf_op jit(solution)/shard_map/ppermute | solution.py:582
  86.6 17.6 %collective-permute-start.51 = (bf16[256,512]{1,0:T(8,128)(2,1)}, bf16[256,512]{1,0:T(8,128)(2,1)}, u32[]{:S(2)}, u32[]{:S(2)}) collective-permute-start(bf16[256,512]{1,0:T(8,128)(2,1)} %pad_maximum_fusion.4), channel_id=1, source_target_pairs={{0,2},{1,3},{2,0},{3,1},{4,6},{5,7},{6,4},{7,5},{8,10},{9,11},{10,... | collective-permute-start | bytes 786440 | tf_op jit(solution)/shard_map/ppermute | solution.py:582
  91.9 43.8 %collective-permute-start.17 = (bf16[256,1024]{1,0:T(8,128)(2,1)}, bf16[256,1024]{1,0:T(8,128)(2,1)S(1)}, u32[]{:S(2)}, u32[]{:S(2)}) collective-permute-start(bf16[256,1024]{1,0:T(8,128)(2,1)} %pad_maximum_fusion.1), channel_id=1, source_target_pairs={{0,2},{1,3},{2,0},{3,1},{4,6},{5,7},{6,4},{7,5},{8,10},{9,11},{10,... | collective-permute-start | bytes 1572872 | tf_op jit(solution)/shard_map/ppermute | solution.py:582
  126.8 74.8 %collective-permute-start.7 = (bf16[128,1024]{1,0:T(8,128)(2,1)}, bf16[128,1024]{1,0:T(8,128)(2,1)}, u32[]{:S(2)}, u32[]{:S(2)}) collective-permute-start(bf16[128,1024]{1,0:T(8,128)(2,1)} %get-tuple-element.89), channel_id=1, source_target_pairs={{0,1},{1,0},{2,3},{3,2},{4,5},{5,4},{6,7},{7,6},{8,9},{9,8},{10,11... | collective-permute-start | bytes 786440 | tf_op jit(solution)/shard_map/ppermute | solution.py:582
  130.2 19.7 %collective-permute-start.34 = (bf16[256,1184]{0,1:T(8,128)(2,1)S(1)}, bf16[256,1184]{0,1:T(8,128)(2,1)}, u32[]{:S(2)}, u32[]{:S(2)}) collective-permute-start(bf16[256,1184]{0,1:T(8,128)(2,1)S(1)} %pad_maximum_fusion), channel_id=1, source_target_pairs={{0,2},{1,3},{2,0},{3,1},{4,6},{5,7},{6,4},{7,5},{8,10},{9,11},{10,... | collective-permute-start | bytes 1818632 | tf_op jit(solution)/shard_map/ppermute | solution.py:582
  144.5 14.0 %collective-permute-start.65 = (bf16[64,1024]{1,0:T(8,128)(2,1)}, bf16[64,1024]{1,0:T(8,128)(2,1)}, u32[]{:S(2)}, u32[]{:S(2)}) collective-permute-start(bf16[64,1024]{1,0:T(8,128)(2,1)} %pad_maximum_fusion.10), channel_id=1, source_target_pairs={{0,4},{1,5},{2,6},{3,7},{4,0},{5,1},{6,2},{7,3},{8,12},{9,13},{10,... | collective-permute-start | bytes 393224 | tf_op jit(solution)/shard_map/ppermute | solution.py:582
  153.2 14.4 %collective-permute-start.35 = (bf16[128,1184]{1,0:T(8,128)(2,1)S(1)}, bf16[128,1184]{1,0:T(8,128)(2,1)S(1)}, u32[]{:S(2)}, u32[]{:S(2)}) collective-permute-start(bf16[128,1184]{1,0:T(8,128)(2,1)S(1)} %get-tuple-element.118), channel_id=1, source_target_pairs={{0,4},{1,5},{2,6},{3,7},{4,0},{5,1},{6,2},{7,3},{8,12},{9,13},{10,... | collective-permute-start | bytes 909320 | tf_op jit(solution)/shard_map/ppermute | solution.py:582
  154.9 15.7 %collective-permute-start.36 = (bf16[128,1184]{1,0:T(8,128)(2,1)S(1)}, bf16[128,1184]{1,0:T(8,128)(2,1)S(1)}, u32[]{:S(2)}, u32[]{:S(2)}) collective-permute-start(bf16[128,1184]{1,0:T(8,128)(2,1)S(1)} %get-tuple-element.120), channel_id=1, source_target_pairs={{0,8},{1,9},{2,10},{3,11},{4,12},{5,13},{6,14},{7,15},{8,0},{9,1},... | collective-permute-start | bytes 909320 | tf_op jit(solution)/shard_map/ppermute | solution.py:582
  162.3 39.9 %collective-permute-start.10 = (f32[128,512]{1,0:T(8,128)S(1)}, f32[128,512]{1,0:T(8,128)S(1)}, u32[]{:S(2)}, u32[]{:S(2)}) collective-permute-start(f32[128,512]{1,0:T(8,128)S(1)} %copy-done.27), channel_id=1, source_target_pairs={{0,1},{1,0},{2,3},{3,2},{4,5},{5,4},{6,7},{7,6},{8,9},{9,8},{10,11... | collective-permute-start | bytes 786440 | tf_op jit(solution)/shard_map/ppermute | solution.py:582
  178.9 22.8 %collective-permute-start.15 = (f32[8,1152]{1,0:T(8,128)S(1)}, f32[8,1152]{1,0:T(8,128)S(1)}, u32[]{:S(2)}, u32[]{:S(2)}) collective-permute-start(f32[8,1152]{1,0:T(8,128)S(1)} %copy-done.32), channel_id=1, source_target_pairs={{0,16},{1,17},{2,18},{3,19},{4,20},{5,21},{6,22},{7,23},{8,24},{9,... | collective-permute-start | bytes 110600 | tf_op jit(solution)/shard_map/ppermute | solution.py:582
  185.5 18.4 %collective-permute-start.61 = (bf16[128,1024]{1,0:T(8,128)(2,1)S(1)}, bf16[128,1024]{1,0:T(8,128)(2,1)S(1)}, u32[]{:S(2)}, u32[]{:S(2)}) collective-permute-start(bf16[128,1024]{1,0:T(8,128)(2,1)S(1)} %constant_dynamic-update-slice_fusion.12.refs_0_), channel_id=1, source_target_pairs={{0,4},{1,5},{2,6},{3,7},{4,0},{5,1},{6,2},{7,3},{8,12},{9,13},{10,... | collective-permute-start | bytes 786440 | tf_op jit(solution)/shard_map/ppermute | solution.py:582
  201.7 14.4 %collective-permute-start.67 = (bf16[128,1024]{1,0:T(8,128)(2,1)S(1)}, bf16[128,1024]{1,0:T(8,128)(2,1)S(1)}, u32[]{:S(2)}, u32[]{:S(2)}) collective-permute-start(bf16[128,1024]{1,0:T(8,128)(2,1)S(1)} %constant_dynamic-update-slice_fusion.15.refs_4_), channel_id=1, source_target_pairs={{0,2},{1,3},{2,0},{3,1},{4,6},{5,7},{6,4},{7,5},{8,10},{9,11},{10,... | collective-permute-start | bytes 786440 | tf_op jit(solution)/shard_map/ppermute | solution.py:582
  203.9 19.9 %collective-permute-start.63 = (bf16[128,1024]{1,0:T(8,128)(2,1)S(1)}, bf16[128,1024]{1,0:T(8,128)(2,1)S(1)}, u32[]{:S(2)}, u32[]{:S(2)}) collective-permute-start(bf16[128,1024]{1,0:T(8,128)(2,1)S(1)} %collective-permute-done.61.refs_1_), channel_id=1, source_target_pairs={{0,2},{1,3},{2,0},{3,1},{4,6},{5,7},{6,4},{7,5},{8,10},{9,11},{10,... | collective-permute-start | bytes 786440 | tf_op jit(solution)/shard_map/ppermute | solution.py:582
  216.1 13.3 %collective-permute-start.26 = (bf16[128,1024]{1,0:T(8,128)(2,1)S(1)}, bf16[128,1024]{1,0:T(8,128)(2,1)S(1)}, u32[]{:S(2)}, u32[]{:S(2)}) collective-permute-start(bf16[128,1024]{1,0:T(8,128)(2,1)S(1)} %constant_dynamic-update-slice_fusion.refs_0_), channel_id=1, source_target_pairs={{0,4},{1,5},{2,6},{3,7},{4,0},{5,1},{6,2},{7,3},{8,12},{9,13},{10,... | collective-permute-start | bytes 786440 | tf_op jit(solution)/shard_map/ppermute | solution.py:582
  223.8 13.9 %collective-permute-start.43 = (bf16[128,1184]{1,0:T(8,128)(2,1)S(1)}, bf16[128,1184]{1,0:T(8,128)(2,1)S(1)}, u32[]{:S(2)}, u32[]{:S(2)}) collective-permute-start(bf16[128,1184]{1,0:T(8,128)(2,1)S(1)} %constant_dynamic-update-slice_fusion.6.refs_8_), channel_id=1, source_target_pairs={{0,4},{1,5},{2,6},{3,7},{4,0},{5,1},{6,2},{7,3},{8,12},{9,13},{10,... | collective-permute-start | bytes 909320 | tf_op jit(solution)/shard_map/ppermute | solution.py:582
  223.8 14.3 %collective-permute-start.48 = (bf16[128,1184]{1,0:T(8,128)(2,1)S(1)}, bf16[128,1184]{1,0:T(8,128)(2,1)S(1)}, u32[]{:S(2)}, u32[]{:S(2)}) collective-permute-start(bf16[128,1184]{1,0:T(8,128)(2,1)S(1)} %constant_dynamic-update-slice_fusion.9.refs_12_), channel_id=1, source_target_pairs={{0,8},{1,9},{2,10},{3,11},{4,12},{5,13},{6,14},{7,15},{8,0},{9,1},... | collective-permute-start | bytes 909320 | tf_op jit(solution)/shard_map/ppermute | solution.py:582
  (84 other events, 652.5 us)

commit v3 on v2

v3 whole, which is shorter than its diff:
```python
import jax
import jax.numpy as jnp
from jax import lax
from jax.experimental import pallas as pl
from jax.experimental.pallas import tpu as pltpu
from jax.sharding import PartitionSpec as P

EPSILON = 1e-05
AXES = ("replica", "fsdp")
LANES = 128
FAR = -1e30


def owner_place():
    return lax.axis_index("fsdp")


def core_place():
    return lax.rem(lax.axis_index("replica"), 2)


def chip_bit(bit):
    return lax.rem(lax.div(lax.axis_index("replica"), 2 << bit), 2)


def full_rows(mine_ref, peer_ref):
    first = owner_place() == 0
    mine, peer = mine_ref[...], peer_ref[...]
    return (jnp.where(first, mine, peer), jnp.where(first, peer, mine), mine + peer)


def row_marks(lens_ref, rows):
    end_one, end_two = lens_ref[0, 0], lens_ref[0, 0] + lens_ref[0, 1]
    position = lax.broadcasted_iota(jnp.int32, (rows, 1), 0)
    start = jnp.where(position >= end_two, end_two, jnp.where(position >= end_one, end_one, 0))
    return (position, start)


def kept_pairs(start, rows):
    key = lax.broadcasted_iota(jnp.int32, (rows, rows), 1)
    query = lax.broadcasted_iota(jnp.int32, (rows, rows), 0)
    return (key <= query) & (key >= start)


def channel_row(low, high, row, tile):
    half = low.shape[1] // LANES
    source = low if tile < half else high
    at = (tile if tile < half else tile - half) * LANES
    return source[row : row + 1, at : at + LANES]


def exact_dot(left, right):
    return jnp.dot(
        left, right, precision=lax.Precision.HIGHEST, preferred_element_type=jnp.float32
    )


def pair_operand(values, lane):
    zero = jnp.zeros_like(values)
    return jnp.concatenate(
        [jnp.where(lane < LANES // 2, values, zero), jnp.where(lane < LANES // 2, zero, values)],
        axis=0,
    )


def forward_body(lens_ref, own_ref, got_ref, mine_ref, peer_ref, xbc_ref, conv_ref, mixed_ref, rates_ref):
    rows, channels = conv_ref.shape
    tiles = channels // LANES
    pairs = tiles - 2
    heads = 2 * pairs
    taps = 4
    low, high, both = full_rows(mine_ref, peer_ref)
    position, start = row_marks(lens_ref, rows)
    usable = [position - (taps - 1 - k) >= start for k in range(taps)]
    lane = lax.broadcasted_iota(jnp.int32, (1, LANES), 1)
    bias = both[6:7, 0:heads]
    decay = both[6:7, LANES : LANES + heads]
    skip = both[6:7, 2 * LANES : 2 * LANES + heads]
    tail = slice(channels, channels + heads)
    rate = own_ref[:, tail] + got_ref[:, tail].astype(jnp.float32) + bias
    step = jnp.maximum(rate, 0.0) + jnp.log1p(jnp.exp(-jnp.abs(rate)))
    rate_sigmoid = jax.nn.sigmoid(rate)
    lower = jnp.where(
        lax.broadcasted_iota(jnp.int32, (rows, rows), 1)
        <= lax.broadcasted_iota(jnp.int32, (rows, rows), 0),
        1.0,
        0.0,
    ).astype(jnp.float32)
    cum = exact_dot(lower, step * -jnp.exp(decay))
    rates_ref[0] = step
    rates_ref[1] = cum
    rates_ref[2] = rate_sigmoid
    step_t, cum_t = step.T, cum.T
    mask = kept_pairs(start, rows)

    def active_tile(tile):
        at = tile * LANES
        xbc = own_ref[:, at : at + LANES] + got_ref[:, at : at + LANES].astype(jnp.float32)
        xbc_ref[:, at : at + LANES] = xbc
        conv = channel_row(low, high, 4, tile) + channel_row(low, high, taps - 1, tile) * xbc
        for k in range(taps - 1):
            shifted = pltpu.roll(xbc, taps - 1 - k, 0)
            conv = conv + channel_row(low, high, k, tile) * jnp.where(usable[k], shifted, 0.0)
        conv_ref[:, at : at + LANES] = conv
        return conv * jax.nn.sigmoid(conv)

    keys = active_tile(tiles - 2).astype(jnp.bfloat16)
    queries = active_tile(tiles - 1).astype(jnp.bfloat16)
    inner = lax.dot_general(
        queries, keys, (((1,), (1,)), ((), ())), preferred_element_type=jnp.float32
    )
    for pair in range(pairs):
        act = active_tile(pair)
        mixing = []
        for h in (2 * pair, 2 * pair + 1):
            spread = jnp.where(mask, cum[:, h : h + 1] - cum_t[h : h + 1, :], FAR)
            mixing.append((inner * jnp.exp(spread) * step_t[h : h + 1, :]).astype(jnp.bfloat16))
        scan = jnp.dot(
            jnp.concatenate(mixing, axis=1),
            pair_operand(act.astype(jnp.bfloat16), lane),
            preferred_element_type=jnp.float32,
        )
        gain = jnp.where(
            lane < LANES // 2, skip[:, 2 * pair : 2 * pair + 1], skip[:, 2 * pair + 1 : 2 * pair + 2]
        )
        mixed_ref[:, pair * LANES : (pair + 1) * LANES] = scan + gain * act


def gate_body(mixed_ref, own_ref, got_ref, q_own_ref, q_got_ref, mine_ref, peer_ref, keep_ref, send_ref, dkeep_ref, dsend_ref, dmixed_ref, gain_grad_ref, out_ref, dgate_ref):
    rows, inner_width = mixed_ref.shape
    half = inner_width // 2
    owner, core = owner_place(), core_place()
    first = owner == 0
    low, high, _ = full_rows(mine_ref, peer_ref)
    width = 2 * LANES
    tiles = inner_width // width

    def cut(tile):
        return slice(tile * width, (tile + 1) * width)

    def gate_of(tile):
        gate = own_ref[:, cut(tile)] + got_ref[:, cut(tile)].astype(jnp.float32)
        return (gate, jax.nn.sigmoid(gate))

    def half_cut(tile):
        at = tile * width % half
        return slice(at, at + width)

    def gain_of(tile):
        return (low if tile * width < half else high)[5:6, half_cut(tile)]

    def q_of(tile):
        own = q_own_ref[:, half_cut(tile)]
        got = q_got_ref[:, half_cut(tile)].astype(jnp.float32)
        return jnp.where(first == (tile * width < half), own, got)

    squares = jnp.zeros((rows, 1), jnp.float32)
    cross = jnp.zeros((rows, 1), jnp.float32)
    for tile in range(tiles):
        gate, sigmoid = gate_of(tile)
        gated = mixed_ref[:, cut(tile)] * (gate * sigmoid)
        squares = squares + jnp.sum(gated * gated, axis=1, keepdims=True)
        cross = cross + jnp.sum(q_of(tile) * gain_of(tile) * gated, axis=1, keepdims=True)
    inverse = lax.rsqrt(squares / inner_width + EPSILON)
    mean_cross = cross * inverse / inner_width
    for tile in range(tiles):
        gate, sigmoid = gate_of(tile)
        silu = gate * sigmoid
        mixed = mixed_ref[:, cut(tile)]
        normed = mixed * silu * inverse
        gain = gain_of(tile)
        out = (normed * gain).astype(jnp.bfloat16)
        out_ref[tile * width // half, :, half_cut(tile)] = out
        q = q_of(tile)
        gain_grad_ref[:, cut(tile)] = jnp.sum(q * normed, axis=0, keepdims=True)
        dgated = inverse * (q * gain - normed * mean_cross)
        dmixed_ref[:, cut(tile)] = dgated * silu
        dgate_ref[tile * width // half, :, half_cut(tile)] = (
            dgated * mixed * (sigmoid * (1.0 + gate * (1.0 - sigmoid)))
        ).astype(jnp.bfloat16)
    keep_ref[...] = out_ref[owner]
    send_ref[...] = out_ref[1 - owner]
    dkeep_ref[...] = dgate_ref[core]
    dsend_ref[...] = dgate_ref[1 - core]


def backward_body(lens_ref, dmixed_ref, xbc_ref, conv_ref, rates_ref, mine_ref, peer_ref, gain_grad_ref, keep_ref, send_ref, small_keep_ref, small_send_ref, rest_ref, small_ref):
    rows, channels = conv_ref.shape
    tiles = channels // LANES
    pairs = tiles - 2
    heads = 2 * pairs
    taps = 4
    half_tiles = tiles // 2
    small_ref[...] = jnp.zeros(small_ref.shape, jnp.float32)
    low, high, both = full_rows(mine_ref, peer_ref)
    position, start = row_marks(lens_ref, rows)
    usable = [position - (taps - 1 - k) >= start for k in range(taps)]
    lane = lax.broadcasted_iota(jnp.int32, (1, LANES), 1)
    decay = both[6:7, LANES : LANES + heads]
    skip = both[6:7, 2 * LANES : 2 * LANES + heads]
    step, cum, rate_sigmoid = rates_ref[0], rates_ref[1], rates_ref[2]
    step_t, cum_t = step.T, cum.T
    mask = kept_pairs(start, rows)

    def cut(tile):
        return slice(tile * LANES, (tile + 1) * LANES)

    def act_of(tile):
        conv = conv_ref[:, cut(tile)]
        sigmoid = jax.nn.sigmoid(conv)
        return (conv * sigmoid, sigmoid * (1.0 + conv * (1.0 - sigmoid)))

    def finish_tile(tile, dconv):
        owner, at = tile // half_tiles, tile % half_tiles * LANES
        xbc = xbc_ref[:, cut(tile)]
        small_ref[owner, 4:5, at : at + LANES] = jnp.sum(dconv, axis=0, keepdims=True)
        small_ref[owner, taps - 1 : taps, at : at + LANES] = jnp.sum(
            dconv * xbc, axis=0, keepdims=True
        )
        total = channel_row(low, high, taps - 1, tile) * dconv
        for k in range(taps - 1):
            behind = taps - 1 - k
            kept = jnp.where(usable[k], dconv, 0.0)
            small_ref[owner, k : k + 1, at : at + LANES] = jnp.sum(
                kept * pltpu.roll(xbc, behind, 0), axis=0, keepdims=True
            )
            total = total + channel_row(low, high, k, tile) * pltpu.roll(kept, rows - behind, 0)
        rest_ref[owner, :, at : at + LANES] = total.astype(jnp.bfloat16)

    keys_act, keys_slope = act_of(tiles - 2)
    queries_act, queries_slope = act_of(tiles - 1)
    keys, queries = keys_act.astype(jnp.bfloat16), queries_act.astype(jnp.bfloat16)
    inner = lax.dot_general(
        queries, keys, (((1,), (1,)), ((), ())), preferred_element_type=jnp.float32
    )
    dinner = jnp.zeros((rows, rows), jnp.float32)
    dstep_rows = []
    dcum = jnp.zeros((rows, heads), jnp.float32)
    skip_grad = jnp.zeros((1, heads), jnp.float32)
    head_lane = lax.broadcasted_iota(jnp.int32, (1, heads), 1)
    for pair in range(pairs):
        act, slope = act_of(pair)
        dmixed = dmixed_ref[:, cut(pair)]
        dscan = dmixed.astype(jnp.bfloat16)
        operand = pair_operand(act.astype(jnp.bfloat16), lane)
        dmixing = lax.dot_general(
            dscan, operand, (((1,), (1,)), ((), ())), preferred_element_type=jnp.float32
        )
        direct = jnp.sum(dmixed * act, axis=0, keepdims=True)
        mixing = []
        for j in range(2):
            h = 2 * pair + j
            spread = jnp.where(mask, cum[:, h : h + 1] - cum_t[h : h + 1, :], FAR)
            decays = jnp.exp(spread)
            step_row = step_t[h : h + 1, :]
            weight = inner * decays
            mixing.append((weight * step_row).astype(jnp.bfloat16))
            grad = dmixing[:, j * rows : (j + 1) * rows]
            dinner = dinner + grad * decays * step_row
            term = grad * weight
            dstep_rows.append(jnp.sum(term, axis=0, keepdims=True))
            dcum = dcum + jnp.where(
                head_lane == h, jnp.sum(term * step_row, axis=1, keepdims=True), 0.0
            )
            in_head = (lane < LANES // 2) if j == 0 else (lane >= LANES // 2)
            skip_grad = skip_grad + jnp.where(
                head_lane == h,
                jnp.sum(jnp.where(in_head, direct, 0.0), axis=1, keepdims=True),
                0.0,
            )
        dinput = lax.dot_general(
            jnp.concatenate(mixing, axis=1),
            dscan,
            (((0,), (0,)), ((), ())),
            preferred_element_type=jnp.float32,
        )
        gain = jnp.where(
            lane < LANES // 2, skip[:, 2 * pair : 2 * pair + 1], skip[:, 2 * pair + 1 : 2 * pair + 2]
        )
        dact = jnp.where(lane < LANES // 2, dinput[:rows], dinput[rows:]) + gain * dmixed
        finish_tile(pair, dact * slope)
    dinner_low = dinner.astype(jnp.bfloat16)
    dqueries = jnp.dot(dinner_low, keys, preferred_element_type=jnp.float32)
    dkeys = lax.dot_general(
        dinner_low, queries, (((0,), (0,)), ((), ())), preferred_element_type=jnp.float32
    )
    finish_tile(tiles - 2, dkeys * keys_slope)
    finish_tile(tiles - 1, dqueries * queries_slope)
    dstep_t = jnp.concatenate(dstep_rows, axis=0)
    dstep = dstep_t.T
    dcum = dcum - step * dstep
    upper = jnp.where(
        lax.broadcasted_iota(jnp.int32, (rows, rows), 1)
        >= lax.broadcasted_iota(jnp.int32, (rows, rows), 0),
        1.0,
        0.0,
    ).astype(jnp.float32)
    drate = exact_dot(upper, dcum)
    speed = jnp.exp(decay)
    draw = (dstep - drate * speed) * rate_sigmoid
    tail = jnp.concatenate([draw, jnp.zeros((rows, LANES - heads), jnp.float32)], axis=1)
    for side in range(2):
        rest_ref[side, :, channels // 2 :] = tail.astype(jnp.bfloat16)
    bias_grad = jnp.sum(draw, axis=0, keepdims=True)
    decay_grad = jnp.sum(-drate * step * speed, axis=0, keepdims=True)
    half_inner = pairs * LANES // 2
    half_heads = heads // 2
    for owner in range(2):
        small_ref[owner, 5:6, 0:half_inner] = gain_grad_ref[
            :, owner * half_inner : (owner + 1) * half_inner
        ]
        for place, item in enumerate((bias_grad, decay_grad, skip_grad)):
            at = place * LANES
            small_ref[owner, 6:7, at : at + half_heads] = item[
                :, owner * half_heads : (owner + 1) * half_heads
            ]
    core, place = core_place(), owner_place()
    keep_ref[...] = rest_ref[core]
    send_ref[...] = rest_ref[1 - core]
    small_keep_ref[...] = small_ref[place]
    small_send_ref[...] = small_ref[1 - place]


def whole(shape, dtype):
    return jax.ShapeDtypeStruct(shape, dtype)


def call(body, out_shape, operands, work, scratch=(), lens=None):
    moved = sum(item.size * item.dtype.itemsize for item in (*operands, *out_shape))
    vmem = pl.BlockSpec(memory_space=pltpu.VMEM)
    in_specs = [vmem for _ in operands]
    if lens is not None:
        operands = (lens, *operands)
        in_specs = [pl.BlockSpec(memory_space=pltpu.SMEM), *in_specs]
    return pl.pallas_call(
        body,
        out_shape=out_shape,
        in_specs=in_specs,
        out_specs=[vmem for _ in out_shape],
        scratch_shapes=[pltpu.VMEM(item.shape, item.dtype) for item in scratch],
        compiler_params=pltpu.CompilerParams(vmem_limit_bytes=40 << 20),
        cost_estimate=pl.CostEstimate(flops=work, bytes_accessed=moved, transcendentals=0),
    )(*operands)


def unit_rows(tokens):
    values = tokens.astype(jnp.float32)
    return lax.rsqrt(jnp.mean(values * values, axis=-1, keepdims=True) + EPSILON)


def lanes_product(left, right):
    return lax.dot_general(
        left, right, (((1,), (1,)), ((), ())), preferred_element_type=jnp.float32
    )


def rows_product(left, right):
    return lax.dot_general(
        left, right, (((0,), (0,)), ((), ())), preferred_element_type=jnp.float32
    )


def lane_half(size):
    return pl.ds(pl.multiple_of(owner_place() * size, LANES), size)


def half_means(tokens_ref, size):
    return tokens_ref[:, lane_half(size)].astype(jnp.float32) * unit_rows(tokens_ref[...])


def norm_body(first_ref, second_ref, gain_ref, out_first_ref, out_second_ref):
    for tokens_ref, out_ref in ((first_ref, out_first_ref), (second_ref, out_second_ref)):
        means = half_means(tokens_ref, out_ref.shape[1])
        out_ref[...] = (means * gain_ref[...]).astype(jnp.bfloat16)


def project_body(tokens_ref, gain_ref, weight_ref, normed_ref, rest_ref, gate_ref):
    inner_width = gate_ref.shape[1]
    rest_width = weight_ref.shape[0] - inner_width
    normed = (half_means(tokens_ref, normed_ref.shape[1]) * gain_ref[...]).astype(jnp.bfloat16)
    normed_ref[...] = normed
    whole_tiles = rest_width // LANES * LANES
    rest_ref[:, :whole_tiles] = lanes_product(
        normed, weight_ref[inner_width : inner_width + whole_tiles, :]
    ).astype(rest_ref.dtype)
    tail = lanes_product(normed, weight_ref[inner_width + whole_tiles :, :])
    blank = jnp.zeros((tail.shape[0], LANES - tail.shape[1]), jnp.float32)
    rest_ref[:, whole_tiles:] = jnp.concatenate([tail, blank], axis=1).astype(rest_ref.dtype)
    gate_ref[...] = lanes_product(normed, weight_ref[:inner_width, :]).astype(gate_ref.dtype)


def cotangent_body(own_ref, other_ref, weight_ref, q_own_ref, q_send_ref):
    q_send_ref[...] = lanes_product(other_ref[...], weight_ref[...]).astype(q_send_ref.dtype)
    q_own_ref[...] = lanes_product(own_ref[...], weight_ref[...])


def branch_body(keep_ref, got_ref, weight_ref, own_ref, send_ref):
    send_ref[...] = jnp.dot(
        got_ref[...], weight_ref[...], preferred_element_type=jnp.float32
    ).astype(send_ref.dtype)
    own_ref[...] = jnp.dot(keep_ref[...], weight_ref[...], preferred_element_type=jnp.float32)


def input_grad_body(*refs):
    tokens, gates, rests = refs[0:4], refs[4:8], refs[8:12]
    gain_ref, weight_ref = refs[12:14]
    outs, gain_grad_ref = refs[14:18], refs[18]
    core = core_place()
    half_inner = gates[0].shape[1]
    half_channels = rests[0].shape[1] - LANES
    tail = weight_ref.shape[0] - 2 * (half_inner + half_channels)
    gate_rows = pl.ds(pl.multiple_of(core * half_inner, LANES), half_inner)
    rest_rows = pl.ds(
        pl.multiple_of(2 * half_inner + core * half_channels, LANES), half_channels
    )
    gate_weight = weight_ref[gate_rows, :]
    rest_weight = weight_ref[rest_rows, :]
    tail_weight = weight_ref[2 * (half_inner + half_channels) :, :]
    gain = gain_ref[...]
    gain_grad = jnp.zeros_like(gain)
    for tokens_ref, gate_ref, rest_ref, out_ref in zip(tokens, gates, rests, outs):
        dnormed = jnp.dot(gate_ref[...], gate_weight, preferred_element_type=jnp.float32)
        dnormed = dnormed + jnp.dot(
            rest_ref[:, :half_channels], rest_weight, preferred_element_type=jnp.float32
        )
        dtail = jnp.dot(
            rest_ref[:, half_channels : half_channels + tail],
            tail_weight,
            preferred_element_type=jnp.float32,
        )
        dnormed = dnormed + jnp.where(core == 0, dtail, 0.0)
        means = half_means(tokens_ref, gain.shape[1])
        gain_grad = gain_grad + jnp.sum(dnormed * means, axis=0, keepdims=True)
        out_ref[...] = (dnormed * gain).astype(out_ref.dtype)
    gain_grad_ref[...] = gain_grad


def tokens_grad_body(tokens_ref, cotangent_ref, own_ref, sib_ref, far_ref, far_sib_ref, out_ref):
    half = own_ref.shape[1]
    first = owner_place() == 0
    inverse = unit_rows(tokens_ref[...])
    own = own_ref[...] + sib_ref[...].astype(jnp.float32)
    far = far_ref[...].astype(jnp.float32) + far_sib_ref[...].astype(jnp.float32)
    parts = []
    cross = jnp.zeros_like(inverse)
    for side in range(2):
        cut = slice(side * half, (side + 1) * half)
        dmeans = jnp.where(first == (side == 0), own, far)
        means = tokens_ref[:, cut].astype(jnp.float32) * inverse
        cross = cross + jnp.sum(dmeans * means, axis=1, keepdims=True)
        parts.append((cut, dmeans, means))
    for cut, dmeans, means in parts:
        out_ref[:, cut] = cotangent_ref[:, cut].astype(jnp.float32) + inverse * (
            dmeans - means * (cross / (2 * half))
        )


def block_grad_body(parts, right_half, *refs):
    lefts, rights, outs = refs[0:4], refs[4:8], refs[8:]
    width = outs[0].shape[1]
    lanes = slice(None)
    if right_half:
        lanes = pl.ds(pl.multiple_of(core_place() * width, LANES), width)
    right = jnp.concatenate([ref[:, lanes] for ref in rights], axis=0)
    for place, (at, size, order) in enumerate(parts):
        bit = chip_bit(order[0])
        half = size // 2
        for ref, side in ((outs[2 * place], 1 - bit), (outs[2 * place + 1], bit)):
            cut = pl.ds(pl.multiple_of(at + side * half, LANES), half)
            left = jnp.concatenate([left_ref[:, cut] for left_ref in lefts], axis=0)
            ref[...] = rows_product(left, right).astype(ref.dtype)


def sum_step_body(parts, step, *refs):
    count = len(parts)
    kept, got, outs = refs[0:count], refs[count : 2 * count], refs[2 * count :]
    for place, (_, _, order) in enumerate(parts):
        if step == len(order):
            outs[place][...] = (
                kept[place][...] + got[place][...].astype(jnp.float32)
            ).astype(outs[place].dtype)
            continue
        rows = kept[place].shape[0] // 2
        bit = chip_bit(order[step])
        for ref, side in ((outs[2 * place], 1 - bit), (outs[2 * place + 1], bit)):
            cut = pl.ds(pl.multiple_of(side * rows, 16), rows)
            ref[...] = (kept[place][cut, :] + got[place][cut, :].astype(jnp.float32)).astype(
                ref.dtype
            )


def stream_pieces(parts, lefts, rights, width, right_half):
    f32, low = jnp.float32, jnp.bfloat16

    def sizes(step):
        return [
            whole((size >> step, width), dtype) for _, size, _ in parts for dtype in (low, f32)
        ]

    def block(*refs):
        block_grad_body(parts, right_half, *refs)

    now = call(
        block, sizes(1), (*lefts, *rights), 1024 * width * sum(size for _, size, _ in parts)
    )
    depth = len(parts[0][2])
    for step in range(1, depth + 1):
        got = [swap_chip(now[2 * p], order[step - 1]) for p, (_, _, order) in enumerate(parts)]

        def add(*refs, step=step):
            sum_step_body(parts, step, *refs)

        last = [whole((size >> depth, width), low) for _, size, _ in parts]
        now = call(add, sizes(step + 1) if step < depth else last, (*now[1::2], *got), 0)
    out = []
    for chunk, (_, _, order) in zip(now, parts):
        for bit in reversed(order[1:]):
            chunk = jnp.concatenate([chunk, swap_chip(chunk, bit)], axis=0)
        got = swap_chip(chunk, order[0])
        out += [chunk, got, swap_core(chunk), swap_core(got)]
    return out


def write_part(out_ref, base, part, pieces, other, limit=None, tail_at=None):
    at, size, order = part
    half, size = size // 2, size >> 3
    first, second, third = (chip_bit(bit) for bit in order)
    for which in range(2):
        side = first if which == 0 else 1 - first
        mine, sibling = pieces[which], pieces[2 + which]
        for p in range(4):
            middle = second if p < 2 else 1 - second
            last = third if p % 2 == 0 else 1 - third
            rows = slice(p * size, (p + 1) * size)
            value = jnp.where(other, sibling[rows, :], mine[rows, :]).astype(jnp.float32)
            place = at + side * half + (2 * middle + last) * size

            def store():
                out_ref[pl.ds(pl.multiple_of(base + place, 8), size), :] = value

            def store_tail():
                out_ref[tail_at:, :] = value[: out_ref.shape[0] - tail_at]

            if limit is None or at + 2 * half <= limit:
                store()
            else:
                pl.when(place < limit)(store)
            if tail_at is not None and at <= limit < at + 2 * half:
                pl.when(place == limit)(store_tail)


def in_weight_body(gate_parts, rest_parts, *refs):
    out_ref = refs[-1]
    gates, rests = refs[: 4 * len(gate_parts)], refs[4 * len(gate_parts) : -1]
    core = core_place()
    half_inner = sum(size for _, size, _ in gate_parts)
    half_channels = sum(size for _, size, _ in rest_parts) - LANES
    for side in range(2):
        other = core != side
        for place, part in enumerate(gate_parts):
            write_part(out_ref, side * half_inner, part, gates[4 * place : 4 * place + 4], other)
        for place, part in enumerate(rest_parts):
            write_part(
                out_ref,
                2 * half_inner + side * half_channels,
                part,
                rests[4 * place : 4 * place + 4],
                other,
                half_channels,
                2 * (half_inner + half_channels) if side == 0 else None,
            )


def out_weight_body(parts, blocks, *refs):
    side = lax.div(pl.program_id(0), blocks)
    other = core_place() != side
    for place, part in enumerate(parts):
        write_part(refs[-1], 0, part, refs[4 * place : 4 * place + 4], other)


def assemble(body, out, pieces, block):
    blocks = pieces[0].shape[1] // block
    return pl.pallas_call(
        body,
        grid=(out.shape[1] // block,),
        out_shape=out,
        in_specs=[
            pl.BlockSpec((item.shape[0], block), lambda i: (0, lax.rem(i, blocks)))
            for item in pieces
        ],
        out_specs=pl.BlockSpec((out.shape[0], block), lambda i: (0, i)),
        compiler_params=pltpu.CompilerParams(vmem_limit_bytes=48 << 20),
        cost_estimate=pl.CostEstimate(
            flops=out.size, bytes_accessed=out.size * 6, transcendentals=0
        ),
    )(*pieces)


def swap(value, replica_bits, fsdp_bits):
    replicas, owners = lax.axis_size("replica"), lax.axis_size("fsdp")
    pairs = [
        (r * owners + f, (r ^ replica_bits) * owners + (f ^ fsdp_bits))
        for r in range(replicas)
        for f in range(owners)
    ]
    return lax.ppermute(value, AXES, pairs)


def swap_owner(value):
    return swap(value, 0, 1)


def swap_core(value):
    return swap(value, 1, 0)


def swap_chip(value, bit):
    return swap(value, 2 << bit, 0)


def join(place, own, other, axis):
    return jnp.where(
        place == 0,
        jnp.concatenate([own, other], axis=axis),
        jnp.concatenate([other, own], axis=axis),
    )


def part_of(value, place, parts, axis):
    size = value.shape[axis] // parts
    return lax.dynamic_slice_in_dim(value, place * size, size, axis)


def total_over_chips(block):
    chip = lax.axis_index("replica") // 2
    bits = range((lax.axis_size("replica") // 2).bit_length() - 1)
    rows, cols = block.shape
    kept = block.reshape((2,) * len(bits) + (rows >> len(bits), cols))
    for bit in bits:
        mine = (chip >> bit) & 1
        sent = lax.dynamic_index_in_dim(kept, 1 - mine, 0, keepdims=False).astype(jnp.bfloat16)
        got = swap_chip(sent, bit)
        kept = lax.dynamic_index_in_dim(kept, mine, 0, keepdims=False) + got.astype(jnp.float32)
    chunk = kept.astype(jnp.bfloat16)
    for bit in reversed(bits):
        chunk = join((chip >> bit) & 1, chunk, swap_chip(chunk, bit), 0)
    return chunk


def per_device(
    tokens,
    seq_lens,
    norm_gain,
    in_weight,
    conv_weight,
    conv_bias,
    step_bias,
    decay_log,
    skip_gain,
    out_gain,
    out_weight,
    cotangent,
):
    f32, low = jnp.float32, jnp.bfloat16
    owner = lax.axis_index("fsdp")
    core = lax.axis_index("replica") % 2
    chips = lax.axis_size("replica") // 2
    rows, width = tokens.shape
    half_width = width // 2
    half_inner = out_weight.shape[0]
    inner_width = 2 * half_inner
    half_channels = conv_bias.shape[0]
    channels = 2 * half_channels
    half_heads = skip_gain.shape[0]
    heads = 2 * half_heads
    weight = in_weight.T
    gain = norm_gain.astype(f32).reshape(1, -1)

    def row(item):
        item = item.astype(f32).reshape(-1, item.shape[-1])
        return jnp.pad(item, ((0, 0), (0, half_channels - item.shape[-1])))

    def head_row(item):
        item = item.astype(f32)
        there = jnp.zeros_like(item)
        placed = jnp.where(
            owner == 0, jnp.concatenate([item, there]), jnp.concatenate([there, item])
        )
        return jnp.pad(placed, (0, LANES - heads))

    head_rows = jnp.concatenate([head_row(step_bias), head_row(decay_log), head_row(skip_gain)])
    mine = jnp.concatenate(
        [
            row(conv_weight),
            row(conv_bias),
            row(out_gain),
            row(head_rows),
            jnp.zeros((1, half_channels), f32),
        ],
        axis=0,
    )

    def project(source, dtype):
        return call(
            project_body,
            [
                whole((rows, half_width), low),
                whole((rows, channels + LANES), dtype),
                whole((rows, inner_width), dtype),
            ],
            (source, gain, weight),
            2 * rows * half_width * weight.shape[0],
        )

    tokens_far = swap_owner(tokens)
    peer = swap_owner(mine)
    held, _ = lax.optimization_barrier((cotangent, tokens_far))
    cotangent_far = swap_owner(held)
    normed_own, rest_own, gate_own = project(tokens, f32)
    normed_far, rest_send, gate_send = project(tokens_far, low)
    rest_got = swap_owner(rest_send)
    q_own, q_send = call(
        cotangent_body,
        [whole((rows, half_inner), f32), whole((rows, half_inner), low)],
        (cotangent, cotangent_far, out_weight),
        4 * rows * width * half_inner,
    )
    q_got = swap_owner(q_send)
    held, _ = lax.optimization_barrier((gate_send, rest_got))
    gate_got = swap_owner(held)
    tokens_sib, tokens_far_sib = swap_core(tokens), swap_core(tokens_far)
    cotangent_sib, cotangent_far_sib = swap_core(cotangent), swap_core(cotangent_far)
    normed_sib, normed_far_sib = call(
        norm_body,
        [whole((rows, half_width), low)] * 2,
        (tokens_sib, tokens_far_sib, gain),
        0,
    )

    xbc, conv, mixed, rates = call(
        forward_body,
        [
            whole((rows, channels), f32),
            whole((rows, channels), f32),
            whole((rows, inner_width), f32),
            whole((3, rows, heads), f32),
        ],
        (rest_own, rest_got, mine, peer),
        10**9,
        lens=seq_lens,
    )
    out_keep, out_send, dgate, dgate_send, dmixed, gain_grad = call(
        gate_body,
        [
            *[whole((rows, half_inner), low)] * 4,
            whole((rows, inner_width), f32),
            whole((1, inner_width), f32),
        ],
        (mixed, gate_own, gate_got, q_own, q_got, mine, peer),
        10**9,
        scratch=[whole((2, rows, half_inner), low)] * 2,
    )
    out_far = swap_owner(out_send)
    dgate_far, dgate_far_sib = swap_owner(dgate), swap(dgate_send, 1, 1)
    out_sib, dgate_sib = swap_core(out_keep), swap_core(dgate_send)
    out_far_sib = swap_core(out_far)
    drest, drest_send, small_keep, small_send = call(
        backward_body,
        [
            *[whole((rows, half_channels + LANES), low)] * 2,
            *[whole((8, half_channels), f32)] * 2,
        ],
        (dmixed, xbc, conv, rates, mine, peer, gain_grad),
        10**9,
        scratch=[
            whole((2, rows, half_channels + LANES), low),
            whole((2, 8, half_channels), f32),
        ],
        lens=seq_lens,
    )
    drest_far, drest_far_sib = swap_owner(drest), swap(drest_send, 1, 1)
    drest_sib = swap_core(drest_send)

    tokens_all = (tokens, tokens_far, tokens_sib, tokens_far_sib)
    normed_all = (normed_own, normed_far, normed_sib, normed_far_sib)
    cotangent_all = (cotangent, cotangent_far, cotangent_sib, cotangent_far_sib)
    out_all = (out_keep, out_far, out_sib, out_far_sib)
    dgate_all = (dgate, dgate_far, dgate_sib, dgate_far_sib)
    drest_all = (drest, drest_far, drest_sib, drest_far_sib)
    if chips == 8:
        out_parts = ((0, half_inner, (0, 1, 2)),)
        gate_parts = ((0, half_inner, (1, 0, 2)),)
        cut = (half_channels + LANES) * 3 // 5 // LANES * LANES
        rest_parts = ((0, cut, (0, 1, 2)), (cut, half_channels + LANES - cut, (1, 0, 2)))
        out_pieces = stream_pieces(out_parts, out_all, cotangent_all, half_width, True)
        gate_pieces = stream_pieces(gate_parts, dgate_all, normed_all, half_width, False)
        rest_pieces = stream_pieces(rest_parts, drest_all, normed_all, half_width, False)

        def in_weight_rows(*refs):
            in_weight_body(gate_parts, rest_parts, *refs)

        def out_weight_lanes(*refs):
            out_weight_body(out_parts, 2, *refs)

        in_weight_grad = assemble(
            in_weight_rows, whole(weight.shape, f32), [*gate_pieces, *rest_pieces], LANES
        ).T
        out_weight_grad = assemble(
            out_weight_lanes, whole(out_weight.shape, f32), out_pieces, half_width // 2
        )
    else:

        def total_of(left, right):
            return total_over_chips(
                rows_product(jnp.concatenate(left, axis=0), jnp.concatenate(right, axis=0))
            )

        out_total = total_of(
            out_all, [part_of(item, core, 2, 1) for item in cotangent_all]
        )
        gate_total = total_of(dgate_all, normed_all)
        rest_total = total_of(drest_all, normed_all)
        rest_sib = swap_core(rest_total)
        out_weight_grad = join(core, out_total, swap_core(out_total), 1).astype(f32)
        in_weight_grad = (
            jnp.concatenate(
                [
                    join(core, gate_total, swap_core(gate_total), 0),
                    join(core, rest_total[:half_channels], rest_sib[:half_channels], 0),
                    rest_total[half_channels : half_channels + heads],
                ],
                axis=0,
            )
            .astype(f32)
            .T
        )

    branch_own, branch_send = call(
        branch_body,
        [whole((rows, width), f32), whole((rows, width), low)],
        (out_keep, out_far, out_weight),
        4 * rows * width * half_inner,
    )
    branch_far = swap_owner(branch_send)
    block_out = (tokens.astype(f32) + branch_own + branch_far.astype(f32)).astype(low)

    own, far_send, sib_send, far_sib_send, norm_grad = call(
        input_grad_body,
        [
            whole((rows, half_width), f32),
            *[whole((rows, half_width), low)] * 3,
            whole((1, half_width), f32),
        ],
        (*tokens_all, *dgate_all, *drest_all, gain, weight),
        4 * rows * width * weight.shape[0],
    )
    (grad_tokens,) = call(
        tokens_grad_body,
        [whole((rows, width), f32)],
        (
            tokens,
            cotangent,
            own,
            swap_core(sib_send),
            swap_owner(far_send),
            swap(far_sib_send, 1, 1),
        ),
        0,
    )

    total = small_keep + swap_owner(small_send)
    total = jnp.concatenate([total[:7], row(norm_grad)], axis=0)
    bit = 1
    while bit < 2 * chips:
        total = total + swap(total, bit, 0)
        bit *= 2
    return (
        block_out,
        grad_tokens,
        total[7, :half_width],
        in_weight_grad,
        total[0:4],
        total[4],
        total[6, 0:half_heads],
        total[6, LANES : LANES + half_heads],
        total[6, 2 * LANES : 2 * LANES + half_heads],
        total[5, :half_inner],
        out_weight_grad,
    )


def solution(mesh):
    placed = (
        P(("replica", "fsdp"), None),
        P(("replica", "fsdp"), None),
        P("fsdp"),
        P("fsdp", None),
        P(None, "fsdp"),
        P("fsdp"),
        P("fsdp"),
        P("fsdp"),
        P("fsdp"),
        P("fsdp"),
        P("fsdp", None),
        P(("replica", "fsdp"), None),
    )
    return jax.shard_map(
        per_device,
        mesh=mesh,
        in_specs=placed,
        out_specs=(
            P(("replica", "fsdp"), None),
            P(("replica", "fsdp"), None),
            P("fsdp"),
            P("fsdp", None),
            P(None, "fsdp"),
            P("fsdp"),
            P("fsdp"),
            P("fsdp"),
            P("fsdp"),
            P("fsdp"),
            P("fsdp", None),
        ),
        check_vma=False,
    )
```

time: 263 us -> 218 us (0.83)
  local copies, waits for them, and re-layouts: 52 us -> 9.9 us
  waiting for transfers between devices: 96.9 us -> 122 us
  Pallas kernels: 49.5 us -> 33.2 us
  other arithmetic: 9.51 us -> 1.83 us
    ppermute x69 -> x60, waiting for transfers between devices: 96.9 us -> 122 us  [swap(): return lax.ppermute(value, AXES, pairs)]
    unnamed x92 -> x42, local copies, waits for them, and re-layouts: 28.3 us -> 6.87 us
    pallas_call x23 -> x24, Pallas kernels: 49.5 us -> 33.2 us  [the longest x22 25.5 us: call(): pl.pallas_call(body, out_shape=out_shape, in_specs=in_specs, out_specs=[v...]
    squeeze x4 -> x0, local copies, waits for them, and re-layouts: 5.23 us -> none  [the longest x2 2.12 us: sibling_part(): lax.dynamic_index_in_dim(got, 1 - core, 0, keepdims=False)]
    dynamic_slice x4 -> x0, local copies, waits for them, and re-layouts: 5.08 us -> none  [the longest x2 2.61 us: sibling_part(): lax.dynamic_index_in_dim(own, 1 - core, 0, keepdims=False)]
    concatenate x11 -> x6, other arithmetic: 4.84 us -> 0.13 us  [stream_pieces(): chunk = jnp.concatenate([chunk, swap_chip(chunk, bit)], axis=0)]
    ppermute x3 -> x0, local copies, waits for them, and re-layouts: 3.98 us -> none  [swap(): return lax.ppermute(value, AXES, pairs)]
    ppermute x69 -> x60, starting transfers between devices: 51.7 us -> 50 us  [swap(): return lax.ppermute(value, AXES, pairs)]
  transfers between devices with their start and end apart: 69 -> 60, of which waited for: 30 -> 21; matrix products, arithmetic and copies ran while one was open for 15% -> 2% of each run, Pallas kernels for 16% -> 13%
where the time goes in v3:
time: 218 us
  waiting for transfers between devices  122 us (56%)
  starting transfers between devices  50 us (23%)
  Pallas kernels  33.2 us (15%)
  local copies, waits for them, and re-layouts  9.9 us (5%)
    ppermute x60, waiting for transfers between devices, swap(): return lax.ppermute(value, AXES, pairs)  122 us
    ppermute x60, starting transfers between devices, swap(): return lax.ppermute(value, AXES, pairs)  50 us
    pallas_call x22, Pallas kernels, call(): pl.pallas_call(body, out_shape=out_shape, in_specs=in_specs, out_specs=[v...  25.5 us
    pallas_call x2, Pallas kernels, assemble(): pl.pallas_call(body, grid=(out.shape[1] // block,), out_shape=out, in_spe...  7.77 us
    unnamed x42, local copies, waits for them, and re-layouts  6.87 us
  transfers between devices with their start and end apart: 60, of which 21 were waited for; matrix products, arithmetic and copies ran while one was open for 2% of the time, Pallas kernels for 13%

profile of v3, /device:TPU:0, one launch (start us, length us, event | category | flops | bytes accessed | tf_op | source)
XLA Modules:
  0.0 218.2 jit_solution(5306141732460653726)
XLA Ops:
  0.6 3.0 %collective-permute-start = (bf16[128,1024]{1,0:T(8,128)(2,1)}, bf16[128,1024]{1,0:T(8,128)(2,1)S(1)}, u32[]{:S(2)}, u32[]{:S(2)}) collective-permute-start(bf16[128,1024]{1,0:T(8,128)(2,1)} %tokens_ref.3), channel_id=1, source_target_pairs={{0,1},{1,0},{2,3},{3,2},{4,5},{5,4},{6,7},{7,6},{8,9},{9,8},{10,11... | collective-permute-start | bytes 786440 | tf_op jit(solution)/shard_map/ppermute | solution.py:606
  4.3 5.8 %collective-permute-done.tokens_ref.refs_1_ = bf16[128,1024]{1,0:T(8,128)(2,1)S(1)} collective-permute-done((bf16[128,1024]{1,0:T(8,128)(2,1)}, bf16[128,1024]{1,0:T(8,128)(2,1)S(1)}, u32[]{:S(2)}, u32[]{:S(2)}) %collective-permute-start) | collective-permute-done | bytes 262176 | tf_op jit(solution)/shard_map/ppermute | solution.py:606
  18.6 14.9 %collective-permute-done.1.got_ref = bf16[128,2432]{1,0:T(8,128)(2,1)} collective-permute-done((bf16[128,2432]{1,0:T(8,128)(2,1)}, bf16[128,2432]{1,0:T(8,128)(2,1)}, u32[]{:S(2)}, u32[]{:S(2)}) %collective-permute-start.1) | collective-permute-done | bytes 622624 | tf_op jit(solution)/shard_map/ppermute | solution.py:606
  35.3 3.7 %collective-permute-done.4.other_ref.refs_5_ = bf16[128,1024]{1,0:T(8,128)(2,1)S(1)} collective-permute-done((bf16[128,1024]{1,0:T(8,128)(2,1)S(1)}, bf16[128,1024]{1,0:T(8,128)(2,1)S(1)}, u32[]{:S(2)}, u32[]{:S(2)}) %collective-permute-start.4) | collective-permute-done | bytes 262176 | tf_op jit(solution)/shard_map/ppermute | solution.py:606
  48.0 6.9 %collective-permute-done.2.peer_ref = f32[8,1152]{1,0:T(8,128)S(1)} collective-permute-done((f32[8,1152]{1,0:T(8,128)S(1)}, f32[8,1152]{1,0:T(8,128)S(1)}, u32[]{:S(2)}, u32[]{:S(2)}) %collective-permute-start.2) | collective-permute-done | bytes 36896 | tf_op jit(solution)/shard_map/ppermute | solution.py:606
  54.9 3.2 %shard_map.205 = (f32[128,2304]{1,0:T(8,128)S(1)}, f32[128,2304]{1,0:T(8,128)S(1)}, f32[128,2048]{1,0:T(8,128)S(1)}, f32[3,128,32]{2,1,0:T(8,128)S(1)}) custom-call(s32[1,2]{1,0:T(1,128)S(1)} %copy-done.10, f32[128,2432]{1,0:T(8,128)S(1)} %get-tuple-element.70.own_ref, bf16[128,2432]{1,0:T(8,128)(2,1)} %collective-permute-done.1.got_ref, ...), custom_call_target="tpu_custom_call" | custom-call | flops 1000000000 | bytes 5398528 | tf_op jit(solution)/shard_map/pallas_call | solution.py:335
  58.2 2.8 %shard_map.207 = (bf16[128,1024]{1,0:T(8,128)(2,1)S(1)}, bf16[128,1024]{1,0:T(8,128)(2,1)S(1)}, bf16[128,1024]{1,0:T(8,128)(2,1)S(1)}, bf16[128,1024]{1,0:T(8,12...) custom-call(f32[128,2048]{1,0:T(8,128)S(1)} %get-tuple-element.72.mixed_ref, ...), custom_call_target="tpu_custom_call" | custom-call | flops 1000000000 | bytes 5586944 | tf_op jit(solution)/shard_map/pallas_call | solution.py:335
  63.1 6.8 %shard_map.209 = (bf16[128,1280]{1,0:T(8,128)(2,1)S(1)}, bf16[128,1280]{1,0:T(8,128)(2,1)S(1)}, f32[8,1152]{1,0:T(8,128)S(1)}, f32[8,1152]{1,0:T(8,128)S(1)}) custom-call(s32[1,2]{1,0:T(1,128)S(1)} %copy-done.10, f32[128,2048]{1,0:T(8,128)S(1)} %get-tuple-element.85.dmixed_ref, f32[128,2304]{1,0:T(8,128)S(1)} %get-tuple-element.86.xbc_ref, ...), custom_call_target="tpu_custom_call" | custom-call | flops 1000000000 | bytes 4268032 | tf_op jit(solution)/shard_map/pallas_call | solution.py:335
  72.1 3.8 %collective-permute-done.10.refs_5_.refs_1_ = bf16[128,1024]{1,0:T(8,128)(2,1)S(1)} collective-permute-done((bf16[128,1024]{1,0:T(8,128)(2,1)S(1)}, bf16[128,1024]{1,0:T(8,128)(2,1)S(1)}, u32[]{:S(2)}, u32[]{:S(2)}) %collective-permute-start.10) | collective-permute-done | bytes 262176 | tf_op jit(solution)/shard_map/ppermute | solution.py:606
  77.5 10.0 %collective-permute-done.12.refs_7_.refs_3_ = bf16[128,1024]{1,0:T(8,128)(2,1)S(1)} collective-permute-done((bf16[128,1024]{1,0:T(8,128)(2,1)S(1)}, bf16[128,1024]{1,0:T(8,128)(2,1)S(1)}, u32[]{:S(2)}, u32[]{:S(2)}) %collective-permute-start.12) | collective-permute-done | bytes 262176 | tf_op jit(solution)/shard_map/ppermute | solution.py:606
  100.1 13.7 %collective-permute-done.33.refs_3_ = bf16[256,512]{1,0:T(8,128)(2,1)S(1)} collective-permute-done((bf16[256,512]{1,0:T(8,128)(2,1)S(1)}, bf16[256,512]{1,0:T(8,128)(2,1)S(1)}, u32[]{:S(2)}, u32[]{:S(2)}) %collective-permute-start.33) | collective-permute-done | bytes 262176 | tf_op jit(solution)/shard_map/ppermute | solution.py:606
  117.2 4.1 %collective-permute-done.35.refs_3_ = bf16[128,512]{1,0:T(8,128)(2,1)S(1)} collective-permute-done((bf16[128,512]{1,0:T(8,128)(2,1)S(1)}, bf16[128,512]{1,0:T(8,128)(2,1)S(1)}, u32[]{:S(2)}, u32[]{:S(2)}) %collective-permute-start.35) | collective-permute-done | bytes 131104 | tf_op jit(solution)/shard_map/ppermute | solution.py:606
  121.4 2.7 %collective-permute-start.36 = (bf16[96,512]{1,0:T(8,128)(2,1)S(1)}, bf16[96,512]{1,0:T(8,128)(2,1)S(1)}, u32[]{:S(2)}, u32[]{:S(2)}) collective-permute-start(bf16[96,512]{1,0:T(8,128)(2,1)S(1)} %get-tuple-element.119), channel_id=1, source_target_pairs={{0,16},{1,17},{2,18},{3,19},{4,20},{5,21},{6,22},{7,23},{8,24},{9,... | collective-permute-start | bytes 294920 | tf_op jit(solution)/shard_map/ppermute | solution.py:606
  131.1 3.5 %collective-permute-done.22 = f32[8,1152]{1,0:T(8,128)S(1)} collective-permute-done((f32[8,1152]{1,0:T(8,128)S(1)}, f32[8,1152]{1,0:T(8,128)S(1)}, u32[]{:S(2)}, u32[]{:S(2)}) %collective-permute-start.22) | collective-permute-done | bytes 36896 | tf_op jit(solution)/shard_map/ppermute | solution.py:606
  140.0 9.8 %collective-permute-done.26.refs_1_ = bf16[128,512]{1,0:T(8,128)(2,1)S(1)} collective-permute-done((bf16[128,512]{1,0:T(8,128)(2,1)S(1)}, bf16[128,512]{1,0:T(8,128)(2,1)S(1)}, u32[]{:S(2)}, u32[]{:S(2)}) %collective-permute-start.26) | collective-permute-done | bytes 131104 | tf_op jit(solution)/shard_map/ppermute | solution.py:606
  152.8 6.1 %collective-permute-done.54.refs_1_ = bf16[128,512]{1,0:T(8,128)(2,1)S(1)} collective-permute-done((bf16[128,512]{1,0:T(8,128)(2,1)S(1)}, bf16[128,512]{1,0:T(8,128)(2,1)S(1)}, u32[]{:S(2)}, u32[]{:S(2)}) %collective-permute-start.54) | collective-permute-done | bytes 131104 | tf_op jit(solution)/shard_map/ppermute | solution.py:606
  159.0 7.6 %collective-permute-done.27 = bf16[128,512]{1,0:T(8,128)(2,1)S(1)} collective-permute-done((bf16[128,512]{1,0:T(8,128)(2,1)S(1)}, bf16[128,512]{1,0:T(8,128)(2,1)S(1)}, u32[]{:S(2)}, u32[]{:S(2)}) %collective-permute-start.27) | collective-permute-done | bytes 131104 | tf_op jit(solution)/shard_map/ppermute | solution.py:606
  172.1 5.1 %collective-permute-done.28 = bf16[256,512]{1,0:T(8,128)(2,1)S(1)} collective-permute-done((bf16[256,512]{1,0:T(8,128)(2,1)S(1)}, bf16[256,512]{1,0:T(8,128)(2,1)S(1)}, u32[]{:S(2)}, u32[]{:S(2)}) %collective-permute-start.28) | collective-permute-done | bytes 262176 | tf_op jit(solution)/shard_map/ppermute | solution.py:606
  181.1 2.6 %collective-permute-done.23 = f32[8,1152]{1,0:T(8,128)S(1)} collective-permute-done((f32[8,1152]{1,0:T(8,128)S(1)}, f32[8,1152]{1,0:T(8,128)S(1)}, u32[]{:S(2)}, u32[]{:S(2)}) %collective-permute-start.23) | collective-permute-done | bytes 36896 | tf_op jit(solution)/shard_map/ppermute | solution.py:606
  183.7 2.4 %collective-permute-start.29 = (bf16[512,512]{1,0:T(8,128)(2,1)S(1)}, bf16[512,512]{1,0:T(8,128)(2,1)S(1)}, u32[]{:S(2)}, u32[]{:S(2)}) collective-permute-start(bf16[512,512]{1,0:T(8,128)(2,1)S(1)} %pad_maximum_fusion.refs_0_), channel_id=1, source_target_pairs={{0,8},{1,9},{2,10},{3,11},{4,12},{5,13},{6,14},{7,15},{8,0},{9,1},... | collective-permute-start | bytes 1572872 | tf_op jit(solution)/shard_map/ppermute | solution.py:606
  188.2 3.1 %collective-permute-done.45.refs_9_ = bf16[256,512]{1,0:T(8,128)(2,1)S(1)} collective-permute-done((bf16[256,512]{1,0:T(8,128)(2,1)S(1)}, bf16[256,512]{1,0:T(8,128)(2,1)S(1)}, u32[]{:S(2)}, u32[]{:S(2)}) %collective-permute-start.45) | collective-permute-done | bytes 262176 | tf_op jit(solution)/shard_map/ppermute | solution.py:606
  192.9 12.7 %collective-permute-done.40.refs_5_ = bf16[384,512]{1,0:T(8,128)(2,1)S(1)} collective-permute-done((bf16[384,512]{1,0:T(8,128)(2,1)S(1)}, bf16[384,512]{1,0:T(8,128)(2,1)S(1)}, u32[]{:S(2)}, u32[]{:S(2)}) %collective-permute-start.40) | collective-permute-done | bytes 393248 | tf_op jit(solution)/shard_map/ppermute | solution.py:606
  210.4 5.0 %shard_map.221 = f32[4384,512]{1,0:T(8,128)} custom-call(bf16[512,512]{1,0:T(8,128)(2,1)S(1)} %pad_maximum_fusion.refs_0_, bf16[512,512]{1,0:T(8,128)(2,1)S(1)} %collective-permute-done.29.refs_1_, bf16[512,512]{1,0:T(8,128)(2,1)S(1)} %collective-permute-done.30.refs_2_, bf16[512,512]{1,0:T(8,128)(2,1)S(1)} %collective-permute-done.31.refs_3_, ...), custom_call_target="tpu_custom_call" | custom-call | flops 2244608 | bytes 13467648 | tf_op jit(solution)/shard_map/pallas_call | solution.py:583
  215.5 2.7 %shard_map.226 = f32[1024,1024]{1,0:T(8,128)} custom-call(bf16[512,512]{1,0:T(8,128)(2,1)S(1)} %pad_maximum_fusion.1.refs_0_, bf16[512,512]{1,0:T(8,128)(2,1)S(1)} %collective-permute-done.57.refs_1_, bf16[512,512]{1,0:T(8,128)(2,1)S(1)} %collective-permute-done.58.refs_2_, bf16[512,512]{1,0:T(8,128)(2,1)S(1)} %collective-permute-done.59.refs_3_), custom_call_target="tpu_custom_call" | custom-call | flops 1048576 | bytes 6291456 | tf_op jit(solution)/shard_map/pallas_call | solution.py:583
  (197 shorter events, 74.9 us)
Async XLA Ops:
  16.2 17.3 %collective-permute-start.1 = (bf16[128,2432]{1,0:T(8,128)(2,1)}, bf16[128,2432]{1,0:T(8,128)(2,1)}, u32[]{:S(2)}, u32[]{:S(2)}) collective-permute-start(bf16[128,2432]{1,0:T(8,128)(2,1)} %get-tuple-element.71), channel_id=1, source_target_pairs={{0,1},{1,0},{2,3},{3,2},{4,5},{5,4},{6,7},{7,6},{8,9},{9,8},{10,11... | collective-permute-start | bytes 1867784 | tf_op jit(solution)/shard_map/ppermute | solution.py:606
  18.0 53.3 %collective-permute-start.8 = (bf16[128,1024]{1,0:T(8,128)(2,1)S(1)}, bf16[128,1024]{1,0:T(8,128)(2,1)S(1)}, u32[]{:S(2)}, u32[]{:S(2)}) collective-permute-start(bf16[128,1024]{1,0:T(8,128)(2,1)S(1)} %copy-done.3), channel_id=1, source_target_pairs={{0,2},{1,3},{2,0},{3,1},{4,6},{5,7},{6,4},{7,5},{8,10},{9,11},{10,... | collective-permute-start | bytes 786440 | tf_op jit(solution)/shard_map/ppermute | solution.py:606
  18.0 21.0 %collective-permute-start.4 = (bf16[128,1024]{1,0:T(8,128)(2,1)S(1)}, bf16[128,1024]{1,0:T(8,128)(2,1)S(1)}, u32[]{:S(2)}, u32[]{:S(2)}) collective-permute-start(bf16[128,1024]{1,0:T(8,128)(2,1)S(1)} %copy-done.4), channel_id=1, source_target_pairs={{0,1},{1,0},{2,3},{3,2},{4,5},{5,4},{6,7},{7,6},{8,9},{9,8},{10,11... | collective-permute-start | bytes 786440 | tf_op jit(solution)/shard_map/ppermute | solution.py:606
  33.5 24.6 %collective-permute-start.3 = (bf16[128,2048]{1,0:T(8,128)(2,1)}, bf16[128,2048]{1,0:T(8,128)(2,1)}, u32[]{:S(2)}, u32[]{:S(2)}) collective-permute-start(bf16[128,2048]{1,0:T(8,128)(2,1)} %copy-done.5), channel_id=1, source_target_pairs={{0,1},{1,0},{2,3},{3,2},{4,5},{5,4},{6,7},{7,6},{8,9},{9,8},{10,11... | collective-permute-start | bytes 1572872 | tf_op jit(solution)/shard_map/ppermute | solution.py:606
  41.8 16.3 %collective-permute-start.5 = (bf16[128,1024]{1,0:T(8,128)(2,1)}, bf16[128,1024]{1,0:T(8,128)(2,1)}, u32[]{:S(2)}, u32[]{:S(2)}) collective-permute-start(bf16[128,1024]{1,0:T(8,128)(2,1)} %get-tuple-element.78), channel_id=1, source_target_pairs={{0,1},{1,0},{2,3},{3,2},{4,5},{5,4},{6,7},{7,6},{8,9},{9,8},{10,11... | collective-permute-start | bytes 786440 | tf_op jit(solution)/shard_map/ppermute | solution.py:606
  48.0 23.4 %collective-permute-start.9 = (bf16[128,1024]{1,0:T(8,128)(2,1)S(1)}, bf16[128,1024]{1,0:T(8,128)(2,1)S(1)}, u32[]{:S(2)}, u32[]{:S(2)}) collective-permute-start(bf16[128,1024]{1,0:T(8,128)(2,1)S(1)} %collective-permute-done.tokens_ref.refs_1_), channel_id=1, source_target_pairs={{0,2},{1,3},{2,0},{3,1},{4,6},{5,7},{6,4},{7,5},{8,10},{9,11},{10,... | collective-permute-start | bytes 786440 | tf_op jit(solution)/shard_map/ppermute | solution.py:606
  69.9 18.8 %collective-permute-start.13 = (bf16[128,1280]{1,0:T(8,128)(2,1)S(1)}, bf16[128,1280]{1,0:T(8,128)(2,1)S(1)}, u32[]{:S(2)}, u32[]{:S(2)}) collective-permute-start(bf16[128,1280]{1,0:T(8,128)(2,1)S(1)} %get-tuple-element.90.refs_8_.refs_0_), channel_id=1, source_target_pairs={{0,1},{1,0},{2,3},{3,2},{4,5},{5,4},{6,7},{7,6},{8,9},{9,8},{10,11... | collective-permute-start | bytes 983048 | tf_op jit(solution)/shard_map/ppermute | solution.py:606
  71.3 17.4 %collective-permute-start.14 = (bf16[128,1280]{1,0:T(8,128)(2,1)S(1)}, bf16[128,1280]{1,0:T(8,128)(2,1)S(1)}, u32[]{:S(2)}, u32[]{:S(2)}) collective-permute-start(bf16[128,1280]{1,0:T(8,128)(2,1)S(1)} %get-tuple-element.91), channel_id=1, source_target_pairs={{0,2},{1,3},{2,0},{3,1},{4,6},{5,7},{6,4},{7,5},{8,10},{9,11},{10,... | collective-permute-start | bytes 983048 | tf_op jit(solution)/shard_map/ppermute | solution.py:606
  71.8 15.7 %collective-permute-start.12 = (bf16[128,1024]{1,0:T(8,128)(2,1)S(1)}, bf16[128,1024]{1,0:T(8,128)(2,1)S(1)}, u32[]{:S(2)}, u32[]{:S(2)}) collective-permute-start(bf16[128,1024]{1,0:T(8,128)(2,1)S(1)} %get-tuple-element.84), channel_id=1, source_target_pairs={{0,3},{1,2},{2,1},{3,0},{4,7},{5,6},{6,5},{7,4},{8,11},{9,10},{10,... | collective-permute-start | bytes 786440 | tf_op jit(solution)/shard_map/ppermute | solution.py:606
  75.9 15.7 %collective-permute-start.15 = (bf16[128,1280]{1,0:T(8,128)(2,1)S(1)}, bf16[128,1280]{1,0:T(8,128)(2,1)S(1)}, u32[]{:S(2)}, u32[]{:S(2)}) collective-permute-start(bf16[128,1280]{1,0:T(8,128)(2,1)S(1)} %get-tuple-element.91), channel_id=1, source_target_pairs={{0,3},{1,2},{2,1},{3,0},{4,7},{5,6},{6,5},{7,4},{8,11},{9,10},{10,... | collective-permute-start | bytes 983048 | tf_op jit(solution)/shard_map/ppermute | solution.py:606
  75.9 17.5 %collective-permute-start.50 = (bf16[128,1024]{1,0:T(8,128)(2,1)S(1)}, bf16[128,1024]{1,0:T(8,128)(2,1)S(1)}, u32[]{:S(2)}, u32[]{:S(2)}) collective-permute-start(bf16[128,1024]{1,0:T(8,128)(2,1)S(1)} %copy-done.4), channel_id=1, source_target_pairs={{0,2},{1,3},{2,0},{3,1},{4,6},{5,7},{6,4},{7,5},{8,10},{9,11},{10,... | collective-permute-start | bytes 786440 | tf_op jit(solution)/shard_map/ppermute | solution.py:606
  93.5 23.0 %collective-permute-start.24 = (bf16[512,512]{1,0:T(8,128)(2,1)S(1)}, bf16[512,512]{1,0:T(8,128)(2,1)S(1)}, u32[]{:S(2)}, u32[]{:S(2)}) collective-permute-start(bf16[512,512]{1,0:T(8,128)(2,1)S(1)} %get-tuple-element.104), channel_id=1, source_target_pairs={{0,8},{1,9},{2,10},{3,11},{4,12},{5,13},{6,14},{7,15},{8,0},{9,1},... | collective-permute-start | bytes 1572872 | tf_op jit(solution)/shard_map/ppermute | solution.py:606
  94.7 19.1 %collective-permute-start.32 = (bf16[384,512]{1,0:T(8,128)(2,1)S(1)}, bf16[384,512]{1,0:T(8,128)(2,1)S(1)}, u32[]{:S(2)}, u32[]{:S(2)}) collective-permute-start(bf16[384,512]{1,0:T(8,128)(2,1)S(1)} %get-tuple-element.111), channel_id=1, source_target_pairs={{0,4},{1,5},{2,6},{3,7},{4,0},{5,1},{6,2},{7,3},{8,12},{9,13},{10,... | collective-permute-start | bytes 1179656 | tf_op jit(solution)/shard_map/ppermute | solution.py:606
  96.3 17.6 %collective-permute-start.33 = (bf16[256,512]{1,0:T(8,128)(2,1)S(1)}, bf16[256,512]{1,0:T(8,128)(2,1)S(1)}, u32[]{:S(2)}, u32[]{:S(2)}) collective-permute-start(bf16[256,512]{1,0:T(8,128)(2,1)S(1)} %get-tuple-element.112), channel_id=1, source_target_pairs={{0,8},{1,9},{2,10},{3,11},{4,12},{5,13},{6,14},{7,15},{8,0},{9,1},... | collective-permute-start | bytes 786440 | tf_op jit(solution)/shard_map/ppermute | solution.py:606
  97.5 26.6 %collective-permute-start.52 = (bf16[512,512]{1,0:T(8,128)(2,1)S(1)}, bf16[512,512]{1,0:T(8,128)(2,1)S(1)}, u32[]{:S(2)}, u32[]{:S(2)}) collective-permute-start(bf16[512,512]{1,0:T(8,128)(2,1)S(1)} %get-tuple-element.124), channel_id=1, source_target_pairs={{0,4},{1,5},{2,6},{3,7},{4,0},{5,1},{6,2},{7,3},{8,12},{9,13},{10,... | collective-permute-start | bytes 1572872 | tf_op jit(solution)/shard_map/ppermute | solution.py:606
  116.6 18.9 %collective-permute-start.25 = (bf16[256,512]{1,0:T(8,128)(2,1)S(1)}, bf16[256,512]{1,0:T(8,128)(2,1)S(1)}, u32[]{:S(2)}, u32[]{:S(2)}) collective-permute-start(bf16[256,512]{1,0:T(8,128)(2,1)S(1)} %get-tuple-element.106), channel_id=1, source_target_pairs={{0,4},{1,5},{2,6},{3,7},{4,0},{5,1},{6,2},{7,3},{8,12},{9,13},{10,... | collective-permute-start | bytes 786440 | tf_op jit(solution)/shard_map/ppermute | solution.py:606
  134.6 42.7 %collective-permute-start.16 = (bf16[128,512]{1,0:T(8,128)(2,1)S(1)}, bf16[128,512]{1,0:T(8,128)(2,1)S(1)}, u32[]{:S(2)}, u32[]{:S(2)}) collective-permute-start(bf16[128,512]{1,0:T(8,128)(2,1)S(1)} %get-tuple-element.93), channel_id=1, source_target_pairs={{0,2},{1,3},{2,0},{3,1},{4,6},{5,7},{6,4},{7,5},{8,10},{9,11},{10,... | collective-permute-start | bytes 393224 | tf_op jit(solution)/shard_map/ppermute | solution.py:606
  134.6 44.1 %collective-permute-start.17 = (bf16[128,512]{1,0:T(8,128)(2,1)S(1)}, bf16[128,512]{1,0:T(8,128)(2,1)S(1)}, u32[]{:S(2)}, u32[]{:S(2)}) collective-permute-start(bf16[128,512]{1,0:T(8,128)(2,1)S(1)} %get-tuple-element.94), channel_id=1, source_target_pairs={{0,1},{1,0},{2,3},{3,2},{4,5},{5,4},{6,7},{7,6},{8,9},{9,8},{10,11... | collective-permute-start | bytes 393224 | tf_op jit(solution)/shard_map/ppermute | solution.py:606
  138.8 20.1 %collective-permute-start.54 = (bf16[128,512]{1,0:T(8,128)(2,1)S(1)}, bf16[128,512]{1,0:T(8,128)(2,1)S(1)}, u32[]{:S(2)}, u32[]{:S(2)}) collective-permute-start(bf16[128,512]{1,0:T(8,128)(2,1)S(1)} %get-tuple-element.128), channel_id=1, source_target_pairs={{0,16},{1,17},{2,18},{3,19},{4,20},{5,21},{6,22},{7,23},{8,24},{9,... | collective-permute-start | bytes 393224 | tf_op jit(solution)/shard_map/ppermute | solution.py:606
  149.8 20.1 %collective-permute-start.38 = (bf16[96,512]{1,0:T(8,128)(2,1)S(1)}, bf16[96,512]{1,0:T(8,128)(2,1)S(1)}, u32[]{:S(2)}, u32[]{:S(2)}) collective-permute-start(bf16[96,512]{1,0:T(8,128)(2,1)S(1)} %get-tuple-element.121), channel_id=1, source_target_pairs={{0,16},{1,17},{2,18},{3,19},{4,20},{5,21},{6,22},{7,23},{8,24},{9,... | collective-permute-start | bytes 294920 | tf_op jit(solution)/shard_map/ppermute | solution.py:606
  151.2 15.4 %collective-permute-start.27 = (bf16[128,512]{1,0:T(8,128)(2,1)S(1)}, bf16[128,512]{1,0:T(8,128)(2,1)S(1)}, u32[]{:S(2)}, u32[]{:S(2)}) collective-permute-start(bf16[128,512]{1,0:T(8,128)(2,1)S(1)} %shard_map.216), channel_id=1, source_target_pairs={{0,16},{1,17},{2,18},{3,19},{4,20},{5,21},{6,22},{7,23},{8,24},{9,... | collective-permute-start | bytes 393224 | tf_op jit(solution)/shard_map/ppermute | solution.py:606
  183.7 22.5 %collective-permute-start.29 = (bf16[512,512]{1,0:T(8,128)(2,1)S(1)}, bf16[512,512]{1,0:T(8,128)(2,1)S(1)}, u32[]{:S(2)}, u32[]{:S(2)}) collective-permute-start(bf16[512,512]{1,0:T(8,128)(2,1)S(1)} %pad_maximum_fusion.refs_0_), channel_id=1, source_target_pairs={{0,8},{1,9},{2,10},{3,11},{4,12},{5,13},{6,14},{7,15},{8,0},{9,1},... | collective-permute-start | bytes 1572872 | tf_op jit(solution)/shard_map/ppermute | solution.py:606
  186.0 20.6 %collective-permute-start.57 = (bf16[512,512]{1,0:T(8,128)(2,1)S(1)}, bf16[512,512]{1,0:T(8,128)(2,1)S(1)}, u32[]{:S(2)}, u32[]{:S(2)}) collective-permute-start(bf16[512,512]{1,0:T(8,128)(2,1)S(1)} %pad_maximum_fusion.1.refs_0_), channel_id=1, source_target_pairs={{0,4},{1,5},{2,6},{3,7},{4,0},{5,1},{6,2},{7,3},{8,12},{9,13},{10,... | collective-permute-start | bytes 1572872 | tf_op jit(solution)/shard_map/ppermute | solution.py:606
  187.6 18.0 %collective-permute-start.40 = (bf16[384,512]{1,0:T(8,128)(2,1)S(1)}, bf16[384,512]{1,0:T(8,128)(2,1)S(1)}, u32[]{:S(2)}, u32[]{:S(2)}) collective-permute-start(bf16[384,512]{1,0:T(8,128)(2,1)S(1)} %constant_dynamic-update-slice_fusion.refs_4_), channel_id=1, source_target_pairs={{0,4},{1,5},{2,6},{3,7},{4,0},{5,1},{6,2},{7,3},{8,12},{9,13},{10,... | collective-permute-start | bytes 1179656 | tf_op jit(solution)/shard_map/ppermute | solution.py:606
  (55 other events, 548.8 us)

commit v4 on v3

--- a/solution.py
+++ b/solution.py
@@ -9,6 +9,7 @@
 AXES = ("replica", "fsdp")
 LANES = 128
 FAR = -1e30
+ORDER = "012n3x0123k0123tb0123p012301os23"
 
 
 def owner_place():
@@ -126,62 +127,81 @@
         mixed_ref[:, pair * LANES : (pair + 1) * LANES] = scan + gain * act
 
 
-def gate_body(mixed_ref, own_ref, got_ref, q_own_ref, q_got_ref, mine_ref, peer_ref, keep_ref, send_ref, dkeep_ref, dsend_ref, dmixed_ref, gain_grad_ref, out_ref, dgate_ref):
+def half_cut(tile, width, half):
+    at = tile * width % half
+    return slice(at, at + width)
+
+
+def gate_tile(own_ref, got_ref, cut):
+    gate = own_ref[:, cut] + got_ref[:, cut].astype(jnp.float32)
+    return (gate, jax.nn.sigmoid(gate))
+
+
+def gate_out_body(mixed_ref, own_ref, got_ref, mine_ref, peer_ref, keep_ref, send_ref, inverse_ref, out_ref):
+    rows, inner_width = mixed_ref.shape
+    half = inner_width // 2
+    owner = owner_place()
+    low, high, _ = full_rows(mine_ref, peer_ref)
+    width = 2 * LANES
+    cuts = [slice(at, at + width) for at in range(0, inner_width, width)]
+    squares = jnp.zeros((rows, 1), jnp.float32)
+    for cut in cuts:
+        gate, sigmoid = gate_tile(own_ref, got_ref, cut)
+        gated = mixed_ref[:, cut] * (gate * sigmoid)
+        squares = squares + jnp.sum(gated * gated, axis=1, keepdims=True)
+    inverse = lax.rsqrt(squares / inner_width + EPSILON)
+    inverse_ref[...] = inverse
+    for tile, cut in enumerate(cuts):
+        gate, sigmoid = gate_tile(own_ref, got_ref, cut)
+        near = half_cut(tile, width, half)
+        gain = (low if cut.start < half else high)[5:6, near]
+        normed = mixed_ref[:, cut] * (gate * sigmoid) * inverse
+        out_ref[cut.start // half, :, near] = (normed * gain).astype(jnp.bfloat16)
+    keep_ref[...] = out_ref[owner]
+    send_ref[...] = out_ref[1 - owner]
+
+
+def gate_grad_body(mixed_ref, own_ref, q_own_ref, got_ref, mine_ref, peer_ref, inverse_ref, keep_ref, send_ref, far_send_ref, dmixed_ref, gain_grad_ref, dgate_ref):
     rows, inner_width = mixed_ref.shape
     half = inner_width // 2
     owner, core = owner_place(), core_place()
-    first = owner == 0
     low, high, _ = full_rows(mine_ref, peer_ref)
     width = 2 * LANES
-    tiles = inner_width // width
-
-    def cut(tile):
-        return slice(tile * width, (tile + 1) * width)
-
-    def gate_of(tile):
-        gate = own_ref[:, cut(tile)] + got_ref[:, cut(tile)].astype(jnp.float32)
-        return (gate, jax.nn.sigmoid(gate))
-
-    def half_cut(tile):
-        at = tile * width % half
-        return slice(at, at + width)
-
-    def gain_of(tile):
-        return (low if tile * width < half else high)[5:6, half_cut(tile)]
-
-    def q_of(tile):
-        own = q_own_ref[:, half_cut(tile)]
-        got = q_got_ref[:, half_cut(tile)].astype(jnp.float32)
-        return jnp.where(first == (tile * width < half), own, got)
-
-    squares = jnp.zeros((rows, 1), jnp.float32)
+    cuts = [slice(at, at + width) for at in range(0, inner_width, width)]
+    inverse = inverse_ref[...]
+
+    def operands(tile, cut):
+        near = half_cut(tile, width, half)
+        in_low = cut.start < half
+        gain = (low if in_low else high)[5:6, near]
+        far = got_ref[:, inner_width + near.start : inner_width + near.stop]
+        q = jnp.where((owner == 0) == in_low, q_own_ref[:, near], far.astype(jnp.float32))
+        return (near, gain, q)
+
     cross = jnp.zeros((rows, 1), jnp.float32)
-    for tile in range(tiles):
-        gate, sigmoid = gate_of(tile)
-        gated = mixed_ref[:, cut(tile)] * (gate * sigmoid)
-        squares = squares + jnp.sum(gated * gated, axis=1, keepdims=True)
-        cross = cross + jnp.sum(q_of(tile) * gain_of(tile) * gated, axis=1, keepdims=True)
-    inverse = lax.rsqrt(squares / inner_width + EPSILON)
+    for tile, cut in enumerate(cuts):
+        _, gain, q = operands(tile, cut)
+        gate, sigmoid = gate_tile(own_ref, got_ref, cut)
+        cross = cross + jnp.sum(
+            q * gain * (mixed_ref[:, cut] * (gate * sigmoid)), axis=1, keepdims=True
+        )
     mean_cross = cross * inverse / inner_width
-    for tile in range(tiles):
-        gate, sigmoid = gate_of(tile)
+    for tile, cut in enumerate(cuts):
+        near, gain, q = operands(tile, cut)
+        gate, sigmoid = gate_tile(own_ref, got_ref, cut)
         silu = gate * sigmoid
-        mixed = mixed_ref[:, cut(tile)]
+        mixed = mixed_ref[:, cut]
         normed = mixed * silu * inverse
-        gain = gain_of(tile)
-        out = (normed * gain).astype(jnp.bfloat16)
-        out_ref[tile * width // half, :, half_cut(tile)] = out
-        q = q_of(tile)
-        gain_grad_ref[:, cut(tile)] = jnp.sum(q * normed, axis=0, keepdims=True)
+        gain_grad_ref[:, cut] = jnp.sum(q * normed, axis=0, keepdims=True)
         dgated = inverse * (q * gain - normed * mean_cross)
-        dmixed_ref[:, cut(tile)] = dgated * silu
-        dgate_ref[tile * width // half, :, half_cut(tile)] = (
+        dmixed_ref[:, cut] = dgated * silu
+        dgate_ref[cut.start // half, :, near] = (
             dgated * mixed * (sigmoid * (1.0 + gate * (1.0 - sigmoid)))
         ).astype(jnp.bfloat16)
-    keep_ref[...] = out_ref[owner]
-    send_ref[...] = out_ref[1 - owner]
-    dkeep_ref[...] = dgate_ref[core]
-    dsend_ref[...] = dgate_ref[1 - core]
+    keep_ref[...] = dgate_ref[core]
+    send_ref[...] = dgate_ref[1 - core]
+    far_send_ref[:rows] = dgate_ref[1 - core]
+    far_send_ref[rows:] = dgate_ref[core]
 
 
 def backward_body(lens_ref, dmixed_ref, xbc_ref, conv_ref, rates_ref, mine_ref, peer_ref, gain_grad_ref, keep_ref, send_ref, small_keep_ref, small_send_ref, rest_ref, small_ref):
@@ -325,8 +345,7 @@
     return jax.ShapeDtypeStruct(shape, dtype)
 
 
-def call(body, out_shape, operands, work, scratch=(), lens=None):
-    moved = sum(item.size * item.dtype.itemsize for item in (*operands, *out_shape))
+def call(body, out_shape, operands, scratch=(), lens=None):
     vmem = pl.BlockSpec(memory_space=pltpu.VMEM)
     in_specs = [vmem for _ in operands]
     if lens is not None:
@@ -339,7 +358,8 @@
         out_specs=[vmem for _ in out_shape],
         scratch_shapes=[pltpu.VMEM(item.shape, item.dtype) for item in scratch],
         compiler_params=pltpu.CompilerParams(vmem_limit_bytes=40 << 20),
-        cost_estimate=pl.CostEstimate(flops=work, bytes_accessed=moved, transcendentals=0),
+        name=body.__name__,
+        cost_estimate=pl.CostEstimate(flops=1, bytes_accessed=1, transcendentals=0),
     )(*operands)
 
 
@@ -374,11 +394,8 @@
         out_ref[...] = (means * gain_ref[...]).astype(jnp.bfloat16)
 
 
-def project_body(tokens_ref, gain_ref, weight_ref, normed_ref, rest_ref, gate_ref):
-    inner_width = gate_ref.shape[1]
+def project_rest(normed, weight_ref, rest_ref, inner_width):
     rest_width = weight_ref.shape[0] - inner_width
-    normed = (half_means(tokens_ref, normed_ref.shape[1]) * gain_ref[...]).astype(jnp.bfloat16)
-    normed_ref[...] = normed
     whole_tiles = rest_width // LANES * LANES
     rest_ref[:, :whole_tiles] = lanes_product(
         normed, weight_ref[inner_width : inner_width + whole_tiles, :]
@@ -386,17 +403,36 @@
     tail = lanes_product(normed, weight_ref[inner_width + whole_tiles :, :])
     blank = jnp.zeros((tail.shape[0], LANES - tail.shape[1]), jnp.float32)
     rest_ref[:, whole_tiles:] = jnp.concatenate([tail, blank], axis=1).astype(rest_ref.dtype)
-    gate_ref[...] = lanes_product(normed, weight_ref[:inner_width, :]).astype(gate_ref.dtype)
-
-
-def cotangent_body(own_ref, other_ref, weight_ref, q_own_ref, q_send_ref):
-    q_send_ref[...] = lanes_product(other_ref[...], weight_ref[...]).astype(q_send_ref.dtype)
-    q_own_ref[...] = lanes_product(own_ref[...], weight_ref[...])
+
+
+def project_own_body(tokens_ref, cotangent_ref, gain_ref, weight_ref, out_weight_ref, normed_ref, rest_ref, gate_ref, q_ref):
+    inner_width = gate_ref.shape[1]
+    normed = (half_means(tokens_ref, normed_ref.shape[1]) * gain_ref[...]).astype(jnp.bfloat16)
+    normed_ref[...] = normed
+    project_rest(normed, weight_ref, rest_ref, inner_width)
+    gate_ref[...] = lanes_product(normed, weight_ref[:inner_width, :])
+    q_ref[...] = lanes_product(cotangent_ref[...], out_weight_ref[...])
+
+
+def project_far_body(inner_width, tokens_ref, gain_ref, weight_ref, normed_ref, rest_ref):
+    normed = (half_means(tokens_ref, normed_ref.shape[1]) * gain_ref[...]).astype(jnp.bfloat16)
+    normed_ref[...] = normed
+    project_rest(normed, weight_ref, rest_ref, inner_width)
+
+
+def gate_far_body(normed_ref, cotangent_ref, weight_ref, out_weight_ref, send_ref):
+    inner_width = send_ref.shape[1] - out_weight_ref.shape[0]
+    send_ref[:, :inner_width] = lanes_product(
+        normed_ref[...], weight_ref[:inner_width, :]
+    ).astype(send_ref.dtype)
+    send_ref[:, inner_width:] = lanes_product(
+        cotangent_ref[...], out_weight_ref[...]
+    ).astype(send_ref.dtype)
 
 
 def branch_body(keep_ref, got_ref, weight_ref, own_ref, send_ref):
     send_ref[...] = jnp.dot(
-        got_ref[...], weight_ref[...], preferred_element_type=jnp.float32
+        got_ref[: send_ref.shape[0], :], weight_ref[...], preferred_element_type=jnp.float32
     ).astype(send_ref.dtype)
     own_ref[...] = jnp.dot(keep_ref[...], weight_ref[...], preferred_element_type=jnp.float32)
 
@@ -404,7 +440,15 @@
 def input_grad_body(*refs):
     tokens, gates, rests = refs[0:4], refs[4:8], refs[8:12]
     gain_ref, weight_ref = refs[12:14]
-    outs, gain_grad_ref = refs[14:18], refs[18]
+    rows = tokens[0].shape[0]
+    gate_starts = (0, rows, 0, 0)
+    own_ref, far_ref, sib_ref, gain_grad_ref = refs[14:18]
+    outs = (
+        own_ref,
+        far_ref.at[0:rows],
+        sib_ref,
+        far_ref.at[rows:],
+    )
     core = core_place()
     half_inner = gates[0].shape[1]
     half_channels = rests[0].shape[1] - LANES
@@ -418,8 +462,12 @@
     tail_weight = weight_ref[2 * (half_inner + half_channels) :, :]
     gain = gain_ref[...]
     gain_grad = jnp.zeros_like(gain)
-    for tokens_ref, gate_ref, rest_ref, out_ref in zip(tokens, gates, rests, outs):
-        dnormed = jnp.dot(gate_ref[...], gate_weight, preferred_element_type=jnp.float32)
+    for tokens_ref, gate_ref, at, rest_ref, out_ref in zip(
+        tokens, gates, gate_starts, rests, outs
+    ):
+        dnormed = jnp.dot(
+            gate_ref[at : at + rows, :], gate_weight, preferred_element_type=jnp.float32
+        )
         dnormed = dnormed + jnp.dot(
             rest_ref[:, :half_channels], rest_weight, preferred_element_type=jnp.float32
         )
@@ -435,12 +483,12 @@
     gain_grad_ref[...] = gain_grad
 
 
-def tokens_grad_body(tokens_ref, cotangent_ref, own_ref, sib_ref, far_ref, far_sib_ref, out_ref):
-    half = own_ref.shape[1]
+def tokens_grad_body(tokens_ref, cotangent_ref, own_ref, far_ref, sib_ref, out_ref):
+    rows, half = own_ref.shape
     first = owner_place() == 0
     inverse = unit_rows(tokens_ref[...])
-    own = own_ref[...] + sib_ref[...].astype(jnp.float32)
-    far = far_ref[...].astype(jnp.float32) + far_sib_ref[...].astype(jnp.float32)
+    own = own_ref[...] + sib_ref[:rows].astype(jnp.float32)
+    far = far_ref[:rows].astype(jnp.float32) + sib_ref[rows:].astype(jnp.float32)
     parts = []
     cross = jnp.zeros_like(inverse)
     for side in range(2):
@@ -455,144 +503,241 @@
         )
 
 
-def block_grad_body(parts, right_half, *refs):
-    lefts, rights, outs = refs[0:4], refs[4:8], refs[8:]
-    width = outs[0].shape[1]
+def left_lanes(lefts, starts, rows, at, size):
+    cut = pl.ds(pl.multiple_of(at, LANES), size)
+    return jnp.concatenate(
+        [ref[first : first + rows, cut] for ref, first in zip(lefts, starts)], axis=0
+    )
+
+
+def block_grad_body(part, starts, right_half, *refs):
+    lefts, rights, (send_ref, keep_ref) = refs[0:4], refs[4:8], refs[8:]
+    rows = rights[0].shape[0]
+    width = send_ref.shape[1]
     lanes = slice(None)
     if right_half:
         lanes = pl.ds(pl.multiple_of(core_place() * width, LANES), width)
     right = jnp.concatenate([ref[:, lanes] for ref in rights], axis=0)
-    for place, (at, size, order) in enumerate(parts):
-        bit = chip_bit(order[0])
-        half = size // 2
-        for ref, side in ((outs[2 * place], 1 - bit), (outs[2 * place + 1], bit)):
-            cut = pl.ds(pl.multiple_of(at + side * half, LANES), half)
-            left = jnp.concatenate([left_ref[:, cut] for left_ref in lefts], axis=0)
-            ref[...] = rows_product(left, right).astype(ref.dtype)
-
-
-def sum_step_body(parts, step, *refs):
-    count = len(parts)
-    kept, got, outs = refs[0:count], refs[count : 2 * count], refs[2 * count :]
-    for place, (_, _, order) in enumerate(parts):
-        if step == len(order):
-            outs[place][...] = (
-                kept[place][...] + got[place][...].astype(jnp.float32)
-            ).astype(outs[place].dtype)
-            continue
-        rows = kept[place].shape[0] // 2
-        bit = chip_bit(order[step])
-        for ref, side in ((outs[2 * place], 1 - bit), (outs[2 * place + 1], bit)):
-            cut = pl.ds(pl.multiple_of(side * rows, 16), rows)
-            ref[...] = (kept[place][cut, :] + got[place][cut, :].astype(jnp.float32)).astype(
+    at, size, order = part
+    bit = chip_bit(order[0])
+    half = size // 2
+    for ref, side in ((send_ref, 1 - bit), (keep_ref, bit)):
+        left = left_lanes(lefts, starts, rows, at + side * half, half)
+        ref[...] = rows_product(left, right).astype(ref.dtype)
+
+
+SMALL_ROWS = 16
+
+
+def block_small_body(part, starts, *refs):
+    lefts, rights, (mine_ref, far_ref, send_ref, keep_ref) = refs[0:4], refs[4:8], refs[8:]
+    rows = rights[0].shape[0]
+    width = send_ref.shape[1]
+    right = jnp.concatenate([ref[...] for ref in rights], axis=0)
+    total = mine_ref[...] + far_ref[...]
+    count, wide = total.shape
+    blank = jnp.zeros((SMALL_ROWS - count, width), jnp.float32)
+    smalls = []
+    for quarter in range(4):
+        piece = total[:, quarter * width : min(wide, (quarter + 1) * width)]
+        if piece.shape[1] < width:
+            rest = jnp.zeros((count, width - piece.shape[1]), jnp.float32)
+            piece = jnp.concatenate([piece, rest], axis=1) if piece.shape[1] else rest
+        smalls.append(jnp.concatenate([piece, blank], axis=0))
+    heads = total[6:7, :width]
+    high = heads.astype(jnp.bfloat16).astype(jnp.float32)
+    row = lax.broadcasted_iota(jnp.int32, (SMALL_ROWS, 1), 0)
+    chip = lax.div(lax.axis_index("replica"), 2)
+    smalls[3] = jnp.where(row == chip, high, 0.0) + jnp.where(
+        row == chip + SMALL_ROWS // 2, heads - high, 0.0
+    )
+    at, size, order = part
+    bit = chip_bit(order[0])
+    quarter = size // 4
+    for ref, side in ((send_ref, 1 - bit), (keep_ref, bit)):
+        left = left_lanes(lefts, starts, rows, at + side * 2 * quarter, 2 * quarter)
+        block = rows_product(left, right)
+        for q in range(2):
+            base = q * (quarter + SMALL_ROWS)
+            ref[base : base + quarter, :] = block[q * quarter : (q + 1) * quarter].astype(
                 ref.dtype
             )
-
-
-def stream_pieces(parts, lefts, rights, width, right_half):
-    f32, low = jnp.float32, jnp.bfloat16
-
-    def sizes(step):
-        return [
-            whole((size >> step, width), dtype) for _, size, _ in parts for dtype in (low, f32)
-        ]
-
-    def block(*refs):
-        block_grad_body(parts, right_half, *refs)
-
-    now = call(
-        block, sizes(1), (*lefts, *rights), 1024 * width * sum(size for _, size, _ in parts)
-    )
-    depth = len(parts[0][2])
-    for step in range(1, depth + 1):
-        got = [swap_chip(now[2 * p], order[step - 1]) for p, (_, _, order) in enumerate(parts)]
-
-        def add(*refs, step=step):
-            sum_step_body(parts, step, *refs)
-
-        last = [whole((size >> depth, width), low) for _, size, _ in parts]
-        now = call(add, sizes(step + 1) if step < depth else last, (*now[1::2], *got), 0)
-    out = []
-    for chunk, (_, _, order) in zip(now, parts):
-        for bit in reversed(order[1:]):
-            chunk = jnp.concatenate([chunk, swap_chip(chunk, bit)], axis=0)
-        got = swap_chip(chunk, order[0])
-        out += [chunk, got, swap_core(chunk), swap_core(got)]
-    return out
-
-
-def write_part(out_ref, base, part, pieces, other, limit=None, tail_at=None):
+            ref[base + quarter : base + quarter + SMALL_ROWS, :] = jnp.where(
+                side == 0, smalls[q], smalls[2 + q]
+            ).astype(ref.dtype)
+
+
+def block_norm_body(part, starts, norm_row, *refs):
+    lefts, rights, (norm_ref, send_ref, keep_ref) = refs[0:4], refs[4:8], refs[8:]
+    rows = rights[0].shape[0]
+    right = jnp.concatenate([ref[...] for ref in rights], axis=0)
     at, size, order = part
-    half, size = size // 2, size >> 3
-    first, second, third = (chip_bit(bit) for bit in order)
+    bit = chip_bit(order[0])
+    half = size // 2
+    row = lax.broadcasted_iota(jnp.int32, (half, 1), 0)
+    for ref, side in ((send_ref, 1 - bit), (keep_ref, bit)):
+        left = left_lanes(lefts, starts, rows, at + side * half, half)
+        block = rows_product(left, right)
+        here = (row + (at + side * half)) == norm_row
+        ref[...] = jnp.where(here, norm_ref[...], block).astype(ref.dtype)
+
+
+def halve_body(bit, keep_ref, got_ref, send_ref, out_ref):
+    rows = send_ref.shape[0]
+    bit = chip_bit(bit)
+    for ref, side in ((send_ref, 1 - bit), (out_ref, bit)):
+        cut = pl.ds(pl.multiple_of(side * rows, 16), rows)
+        ref[...] = (keep_ref[cut, :] + got_ref[cut, :].astype(jnp.float32)).astype(ref.dtype)
+
+
+def add_body(keep_ref, got_ref, out_ref):
+    out_ref[...] = (
+        keep_ref[...].astype(jnp.float32) + got_ref[...].astype(jnp.float32)
+    ).astype(out_ref.dtype)
+
+
+def after(value, *earlier):
+    return lax.optimization_barrier((value, *earlier))[0]
+
+
+class PartSum:
+    def __init__(self, order, make_block, early=False):
+        self.order, self.make_block, self.early = order, make_block, early
+        self.steps = 0
+        self.pieces = None
+
+    def advance(self, token):
+        f32, low = jnp.float32, jnp.bfloat16
+        step = self.steps
+        self.steps += 1
+        if step == 0:
+            send, self.keep = self.make_block(token)
+            bit = self.order[0]
+        elif step == 1:
+            keep = after(self.keep, token)
+            shape = (keep.shape[0] // 2, keep.shape[1])
+
+            def halve(*refs):
+                halve_body(self.order[1], *refs)
+
+            send, self.keep = call(
+                halve, [whole(shape, low), whole(shape, f32)], (keep, self.got)
+            )
+            bit = self.order[1]
+        elif step < 4:
+            keep = after(self.keep, token)
+            (send,) = call(add_body, [whole(keep.shape, low)], (keep, self.got))
+            self.keep = send
+            bit = self.order[2] if step == 2 else self.order[1]
+        elif step == 4:
+            send = jnp.concatenate([after(self.keep, token), self.got], axis=0)
+            self.keep = send
+            if self.early:
+                self.sibling = swap_core(send)
+            bit = self.order[0]
+        else:
+            got = after(self.got, token)
+            sibling = after(self.sibling, got) if self.early else swap_core(self.keep)
+            self.pieces = [self.keep, got, sibling, swap_core(got)]
+            return got
+        self.got = swap_chip(send, bit)
+        return send
+
+
+def part_quarters(order, pieces):
+    first, second = chip_bit(order[0]), chip_bit(order[1])
     for which in range(2):
         side = first if which == 0 else 1 - first
         mine, sibling = pieces[which], pieces[2 + which]
-        for p in range(4):
-            middle = second if p < 2 else 1 - second
-            last = third if p % 2 == 0 else 1 - third
-            rows = slice(p * size, (p + 1) * size)
-            value = jnp.where(other, sibling[rows, :], mine[rows, :]).astype(jnp.float32)
-            place = at + side * half + (2 * middle + last) * size
-
-            def store():
-                out_ref[pl.ds(pl.multiple_of(base + place, 8), size), :] = value
-
-            def store_tail():
-                out_ref[tail_at:, :] = value[: out_ref.shape[0] - tail_at]
-
-            if limit is None or at + 2 * half <= limit:
-                store()
-            else:
-                pl.when(place < limit)(store)
-            if tail_at is not None and at <= limit < at + 2 * half:
-                pl.when(place == limit)(store_tail)
-
-
-def in_weight_body(gate_parts, rest_parts, *refs):
-    out_ref = refs[-1]
-    gates, rests = refs[: 4 * len(gate_parts)], refs[4 * len(gate_parts) : -1]
+        size = mine.shape[0] // 2
+        for p in range(2):
+            quarter = 2 * side + (second if p == 0 else 1 - second)
+            yield quarter, mine, sibling, p * size
+
+
+def write_part(out_ref, base, part, pieces, other):
+    at, size, order = part
+    size = size // 4
+    for quarter, mine, sibling, row in part_quarters(order, pieces):
+        rows = slice(row, row + size)
+        value = jnp.where(other, sibling[rows, :], mine[rows, :]).astype(jnp.float32)
+        out_ref[pl.ds(pl.multiple_of(base + at + quarter * size, 8), size), :] = value
+
+
+def in_weight_body(gate_part, rest_parts, *refs):
+    (out_ref, norm_ref), refs = refs[-2:], refs[:-2]
+    gates, rests = refs[0:4], refs[4:]
     core = core_place()
-    half_inner = sum(size for _, size, _ in gate_parts)
-    half_channels = sum(size for _, size, _ in rest_parts) - LANES
+    half_inner = gate_part[1]
+    last_at, last_size, last_order = rest_parts[1]
+    half_channels = last_at + last_size - LANES
+    tail_at = 2 * (half_inner + half_channels)
+    tail = out_ref.shape[0] - tail_at
     for side in range(2):
         other = core != side
-        for place, part in enumerate(gate_parts):
-            write_part(out_ref, side * half_inner, part, gates[4 * place : 4 * place + 4], other)
-        for place, part in enumerate(rest_parts):
-            write_part(
-                out_ref,
-                2 * half_inner + side * half_channels,
-                part,
-                rests[4 * place : 4 * place + 4],
-                other,
-                half_channels,
-                2 * (half_inner + half_channels) if side == 0 else None,
-            )
-
-
-def out_weight_body(parts, blocks, *refs):
+        base = 2 * half_inner + side * half_channels
+        write_part(out_ref, side * half_inner, gate_part, gates, other)
+        write_part(out_ref, base, rest_parts[0], rests[0:4], other)
+        size = last_size // 4
+        for quarter, mine, sibling, row in part_quarters(last_order, rests[4:8]):
+            rows = slice(row, row + size)
+            value = jnp.where(other, sibling[rows, :], mine[rows, :]).astype(jnp.float32)
+
+            @pl.when(quarter < 3)
+            def _():
+                place = base + last_at + quarter * size
+                out_ref[pl.ds(pl.multiple_of(place, 8), size), :] = value
+
+            if side == 0:
+
+                @pl.when(quarter == 3)
+                def _():
+                    out_ref[tail_at:, :] = value[:tail]
+                    both = mine[rows, :].astype(jnp.float32) + sibling[rows, :].astype(
+                        jnp.float32
+                    )
+                    norm_ref[...] = both[tail : tail + norm_ref.shape[0]]
+
+
+def small_body(order, *refs):
+    pieces, out_ref = refs[:-1], refs[-1]
+    count, wide = out_ref.shape[0] // 2, out_ref.shape[1]
+    width = pieces[0].shape[1]
+    for quarter, mine, sibling, row in part_quarters(order, pieces):
+        size = mine.shape[0] // 2
+        rows = slice(row + size - SMALL_ROWS, row + size)
+        both = mine[rows, :].astype(jnp.float32) + sibling[rows, :].astype(jnp.float32)
+        for place in range((wide + width - 1) // width):
+            lanes = slice(place * width, min(wide, (place + 1) * width))
+
+            @pl.when(quarter == place)
+            def _():
+                out_ref[:count, lanes] = both[:count, : lanes.stop - lanes.start]
+
+        @pl.when(quarter == 3)
+        def _():
+            out_ref[count : count + 1, :width] = jnp.sum(both, axis=0, keepdims=True)
+
+
+def out_weight_body(part, blocks, *refs):
     side = lax.div(pl.program_id(0), blocks)
-    other = core_place() != side
-    for place, part in enumerate(parts):
-        write_part(refs[-1], 0, part, refs[4 * place : 4 * place + 4], other)
-
-
-def assemble(body, out, pieces, block):
+    write_part(refs[-1], 0, part, refs[:-1], core_place() != side)
+
+
+def assemble(body, outs, pieces, block):
     blocks = pieces[0].shape[1] // block
     return pl.pallas_call(
         body,
-        grid=(out.shape[1] // block,),
-        out_shape=out,
+        grid=(outs[0].shape[1] // block,),
+        out_shape=outs,
         in_specs=[
             pl.BlockSpec((item.shape[0], block), lambda i: (0, lax.rem(i, blocks)))
             for item in pieces
         ],
-        out_specs=pl.BlockSpec((out.shape[0], block), lambda i: (0, i)),
+        out_specs=[pl.BlockSpec((out.shape[0], block), lambda i: (0, i)) for out in outs],
         compiler_params=pltpu.CompilerParams(vmem_limit_bytes=48 << 20),
-        cost_estimate=pl.CostEstimate(
-            flops=out.size, bytes_accessed=out.size * 6, transcendentals=0
-        ),
+        name=body.__name__,
+        cost_estimate=pl.CostEstimate(flops=1, bytes_accessed=1, transcendentals=0),
     )(*pieces)
 
 
@@ -676,6 +821,36 @@
     weight = in_weight.T
     gain = norm_gain.astype(f32).reshape(1, -1)
 
+    tokens_far = swap_owner(tokens)
+    cotangent_far = swap_owner(cotangent)
+    def project_far(*refs):
+        project_far_body(inner_width, *refs)
+
+    normed_far, rest_send = call(
+        project_far,
+        [whole((rows, half_width), low), whole((rows, channels + LANES), f32)],
+        (after(tokens_far, cotangent_far), gain, weight),
+    )
+    rest_got = swap_owner(rest_send)
+    normed_own, rest_own, gate_own, q_own = call(
+        project_own_body,
+        [
+            whole((rows, half_width), low),
+            whole((rows, channels + LANES), f32),
+            whole((rows, inner_width), f32),
+            whole((rows, half_inner), f32),
+        ],
+        (after(tokens, rest_send), cotangent, gain, weight, out_weight),
+    )
+    (gate_send,) = call(
+        gate_far_body,
+        [whole((rows, inner_width + half_inner), low)],
+        (normed_far, cotangent_far, weight, out_weight),
+    )
+    conv_weight, conv_bias, step_bias, decay_log, skip_gain, out_gain = after(
+        (conv_weight, conv_bias, step_bias, decay_log, skip_gain, out_gain), gate_send
+    )
+
     def row(item):
         item = item.astype(f32).reshape(-1, item.shape[-1])
         return jnp.pad(item, ((0, 0), (0, half_channels - item.shape[-1])))
@@ -699,42 +874,14 @@
         ],
         axis=0,
     )
-
-    def project(source, dtype):
-        return call(
-            project_body,
-            [
-                whole((rows, half_width), low),
-                whole((rows, channels + LANES), dtype),
-                whole((rows, inner_width), dtype),
-            ],
-            (source, gain, weight),
-            2 * rows * half_width * weight.shape[0],
-        )
-
-    tokens_far = swap_owner(tokens)
     peer = swap_owner(mine)
-    held, _ = lax.optimization_barrier((cotangent, tokens_far))
-    cotangent_far = swap_owner(held)
-    normed_own, rest_own, gate_own = project(tokens, f32)
-    normed_far, rest_send, gate_send = project(tokens_far, low)
-    rest_got = swap_owner(rest_send)
-    q_own, q_send = call(
-        cotangent_body,
-        [whole((rows, half_inner), f32), whole((rows, half_inner), low)],
-        (cotangent, cotangent_far, out_weight),
-        4 * rows * width * half_inner,
-    )
-    q_got = swap_owner(q_send)
-    held, _ = lax.optimization_barrier((gate_send, rest_got))
-    gate_got = swap_owner(held)
+    gate_got = swap_owner(after(gate_send, rest_got, peer))
     tokens_sib, tokens_far_sib = swap_core(tokens), swap_core(tokens_far)
     cotangent_sib, cotangent_far_sib = swap_core(cotangent), swap_core(cotangent_far)
     normed_sib, normed_far_sib = call(
         norm_body,
         [whole((rows, half_width), low)] * 2,
         (tokens_sib, tokens_far_sib, gain),
-        0,
     )
 
     xbc, conv, mixed, rates = call(
@@ -746,24 +893,35 @@
             whole((3, rows, heads), f32),
         ],
         (rest_own, rest_got, mine, peer),
-        10**9,
         lens=seq_lens,
     )
-    out_keep, out_send, dgate, dgate_send, dmixed, gain_grad = call(
-        gate_body,
+    out_keep, out_send, inverse = call(
+        gate_out_body,
+        [*[whole((rows, half_inner), low)] * 2, whole((rows, 1), f32)],
+        (mixed, gate_own, gate_got, mine, peer),
+        scratch=[whole((2, rows, half_inner), low)],
+    )
+    out_far, out_sib = swap_owner(out_send), swap_core(out_keep)
+    dgate, dgate_send, far_send, dmixed, gain_grad = call(
+        gate_grad_body,
         [
-            *[whole((rows, half_inner), low)] * 4,
+            *[whole((rows, half_inner), low)] * 2,
+            whole((2 * rows, half_inner), low),
             whole((rows, inner_width), f32),
             whole((1, inner_width), f32),
         ],
-        (mixed, gate_own, gate_got, q_own, q_got, mine, peer),
-        10**9,
-        scratch=[whole((2, rows, half_inner), low)] * 2,
-    )
-    out_far = swap_owner(out_send)
-    dgate_far, dgate_far_sib = swap_owner(dgate), swap(dgate_send, 1, 1)
-    out_sib, dgate_sib = swap_core(out_keep), swap_core(dgate_send)
-    out_far_sib = swap_core(out_far)
+        (
+            after(mixed, normed_sib, normed_far_sib, cotangent_sib, cotangent_far_sib),
+            gate_own,
+            q_own,
+            gate_got,
+            mine,
+            peer,
+            inverse,
+        ),
+        scratch=[whole((2, rows, half_inner), low)],
+    )
+    far, dgate_sib = swap_owner(far_send), swap_core(dgate_send)
     drest, drest_send, small_keep, small_send = call(
         backward_body,
         [
@@ -771,55 +929,99 @@
             *[whole((8, half_channels), f32)] * 2,
         ],
         (dmixed, xbc, conv, rates, mine, peer, gain_grad),
-        10**9,
         scratch=[
             whole((2, rows, half_channels + LANES), low),
             whole((2, 8, half_channels), f32),
         ],
         lens=seq_lens,
     )
+    small_far = swap_owner(small_send)
+    out_far_sib = swap_core(after(out_far, drest))
     drest_far, drest_far_sib = swap_owner(drest), swap(drest_send, 1, 1)
     drest_sib = swap_core(drest_send)
 
     tokens_all = (tokens, tokens_far, tokens_sib, tokens_far_sib)
     normed_all = (normed_own, normed_far, normed_sib, normed_far_sib)
     cotangent_all = (cotangent, cotangent_far, cotangent_sib, cotangent_far_sib)
+    drest_all = (drest, drest_far, drest_sib, drest_far_sib)
     out_all = (out_keep, out_far, out_sib, out_far_sib)
-    dgate_all = (dgate, dgate_far, dgate_sib, dgate_far_sib)
-    drest_all = (drest, drest_far, drest_sib, drest_far_sib)
+    out_starts, gate_starts, rest_starts = (0,) * 4, (0, rows, 0, 0), (0,) * 4
+    state = {}
     if chips == 8:
-        out_parts = ((0, half_inner, (0, 1, 2)),)
-        gate_parts = ((0, half_inner, (1, 0, 2)),)
         cut = (half_channels + LANES) * 3 // 5 // LANES * LANES
+        out_part = (0, half_inner, (0, 1, 2))
+        gate_part = (0, half_inner, (1, 0, 2))
         rest_parts = ((0, cut, (0, 1, 2)), (cut, half_channels + LANES - cut, (1, 0, 2)))
-        out_pieces = stream_pieces(out_parts, out_all, cotangent_all, half_width, True)
-        gate_pieces = stream_pieces(gate_parts, dgate_all, normed_all, half_width, False)
-        rest_pieces = stream_pieces(rest_parts, drest_all, normed_all, half_width, False)
-
-        def in_weight_rows(*refs):
-            in_weight_body(gate_parts, rest_parts, *refs)
-
-        def out_weight_lanes(*refs):
-            out_weight_body(out_parts, 2, *refs)
-
-        in_weight_grad = assemble(
-            in_weight_rows, whole(weight.shape, f32), [*gate_pieces, *rest_pieces], LANES
-        ).T
-        out_weight_grad = assemble(
-            out_weight_lanes, whole(out_weight.shape, f32), out_pieces, half_width // 2
-        )
+        norm_row = half_channels + heads
+
+        def maker(body, part, given, size, extra=(), early=False):
+            lefts, starts, rights = given
+
+            def make(token):
+                def block_grad(*refs):
+                    body(part, starts, *refs)
+
+                if lefts is None:
+                    state["far_sib"] = swap_core(after(far, token))
+                    sources = (dgate, far, dgate_sib, state["far_sib"])
+                else:
+                    sources = lefts
+                tied = sources if token is None else (after(sources[0], token), *sources[1:])
+                more = [item() for item in extra]
+                sizes = [whole((size // 2, half_width), dtype) for dtype in (low, f32)]
+                return call(block_grad, sizes, (*tied, *rights, *more))
+
+            return PartSum(part[2], make, early)
+
+        def out_block(part, starts, *refs):
+            block_grad_body(part, starts, True, *refs)
+
+        def rest_block(part, starts, *refs):
+            block_grad_body(part, starts, False, *refs)
+
+        def norm_block(part, starts, *refs):
+            block_norm_body(part, starts, norm_row, *refs)
+
+        gate_sources = (None, gate_starts, normed_all)
+        rest_sources = (drest_all, rest_starts, normed_all)
+        sums = (
+            maker(out_block, out_part, (out_all, out_starts, cotangent_all), half_inner),
+            maker(
+                block_small_body,
+                gate_part,
+                gate_sources,
+                half_inner + 4 * SMALL_ROWS,
+                (lambda: small_keep, lambda: small_far),
+            ),
+            maker(rest_block, rest_parts[0], rest_sources, rest_parts[0][1], early=True),
+            maker(
+                norm_block,
+                rest_parts[1],
+                rest_sources,
+                rest_parts[1][1],
+                (lambda: state["norm_grad"],),
+                early=True,
+            ),
+        )
+        token = None
     else:
-
-        def total_of(left, right):
+        token = drest
+
+        def total_of(left, starts, right):
+            left = [item[first : first + rows] for item, first in zip(left, starts)]
             return total_over_chips(
                 rows_product(jnp.concatenate(left, axis=0), jnp.concatenate(right, axis=0))
             )
 
         out_total = total_of(
-            out_all, [part_of(item, core, 2, 1) for item in cotangent_all]
-        )
-        gate_total = total_of(dgate_all, normed_all)
-        rest_total = total_of(drest_all, normed_all)
+            out_all,
+            out_starts,
+            [part_of(item, core, 2, 1) for item in cotangent_all],
+        )
+        state["far_sib"] = swap_core(far)
+        dgate_all = (dgate, far, dgate_sib, state["far_sib"])
+        gate_total = total_of(dgate_all, gate_starts, normed_all)
+        rest_total = total_of(drest_all, rest_starts, normed_all)
         rest_sib = swap_core(rest_total)
         out_weight_grad = join(core, out_total, swap_core(out_total), 1).astype(f32)
         in_weight_grad = (
@@ -835,56 +1037,152 @@
             .T
         )
 
-    branch_own, branch_send = call(
-        branch_body,
-        [whole((rows, width), f32), whole((rows, width), low)],
-        (out_keep, out_far, out_weight),
-        4 * rows * width * half_inner,
-    )
-    branch_far = swap_owner(branch_send)
-    block_out = (tokens.astype(f32) + branch_own + branch_far.astype(f32)).astype(low)
-
-    own, far_send, sib_send, far_sib_send, norm_grad = call(
-        input_grad_body,
-        [
-            whole((rows, half_width), f32),
-            *[whole((rows, half_width), low)] * 3,
-            whole((1, half_width), f32),
-        ],
-        (*tokens_all, *dgate_all, *drest_all, gain, weight),
-        4 * rows * width * weight.shape[0],
-    )
-    (grad_tokens,) = call(
-        tokens_grad_body,
-        [whole((rows, width), f32)],
-        (
-            tokens,
-            cotangent,
-            own,
-            swap_core(sib_send),
-            swap_owner(far_send),
-            swap(far_sib_send, 1, 1),
-        ),
-        0,
-    )
-
-    total = small_keep + swap_owner(small_send)
-    total = jnp.concatenate([total[:7], row(norm_grad)], axis=0)
-    bit = 1
-    while bit < 2 * chips:
-        total = total + swap(total, bit, 0)
-        bit *= 2
+    def out_projection(token):
+        own, send = call(
+            branch_body,
+            [whole((rows, width), f32), whole((rows, width), low)],
+            (after(out_keep, token), out_far, out_weight),
+        )
+        state["branch"] = (own, swap_owner(send))
+        return send
+
+    def block_sum(token):
+        own, far = state["branch"]
+        state["block_out"] = (
+            tokens.astype(f32) + after(own, token) + far.astype(f32)
+        ).astype(low)
+        return state["block_out"]
+
+    def input_norm(token):
+        state["dmeans"] = call(
+            input_grad_body,
+            [
+                whole((rows, half_width), f32),
+                whole((2 * rows, half_width), low),
+                whole((rows, half_width), low),
+                whole((1, half_width), f32),
+            ],
+            (
+                *tokens_all,
+                after(dgate, token),
+                far,
+                dgate_sib,
+                state["far_sib"],
+                *drest_all,
+                gain,
+                weight,
+            ),
+        )
+        state["norm_grad"] = state["dmeans"][3]
+        return state["norm_grad"]
+
+    def means_far(token):
+        send = after(state["dmeans"][1], token)
+        state["means_far"] = swap_owner(send)
+        return send
+
+    def means_sib(token):
+        far = after(state["means_far"], token)
+        send = jnp.concatenate([state["dmeans"][2], far[rows:]], axis=0)
+        state["means_sib"] = swap_core(send)
+        return send
+
+    def tokens_grad(token):
+        (state["grad_tokens"],) = call(
+            tokens_grad_body,
+            [whole((rows, width), f32)],
+            (
+                tokens,
+                cotangent,
+                after(state["dmeans"][0], token),
+                state["means_far"],
+                state["means_sib"],
+            ),
+        )
+        return state["grad_tokens"]
+
+    def small_results(total, row):
+        return (
+            total[0:4],
+            total[4],
+            total[row, 0:half_heads],
+            total[row, LANES : LANES + half_heads],
+            total[row, 2 * LANES : 2 * LANES + half_heads],
+            total[5, :half_inner],
+        )
+
+    def small_assembly(token):
+        def small_rows(*refs):
+            small_body(gate_part[2], *refs)
+
+        pieces = sums[1].pieces
+        (total,) = call(
+            small_rows,
+            [whole((16, half_channels), f32)],
+            (after(pieces[0], token), *pieces[1:]),
+        )
+        state["smalls"] = small_results(total, 8)
+        return state["smalls"][1]
+
+    def out_assembly(token):
+        def out_weight_lanes(*refs):
+            out_weight_body(out_part, 2, *refs)
+
+        pieces = sums[0].pieces
+        (state["out_weight"],) = assemble(
+            out_weight_lanes,
+            [whole(out_weight.shape, f32)],
+            [after(pieces[0], token), *pieces[1:]],
+            half_width // 2,
+        )
+        return state["out_weight"]
+
+    if chips == 8:
+        steps = {
+            "n": input_norm,
+            "x": means_far,
+            "k": means_sib,
+            "t": tokens_grad,
+            "b": out_projection,
+            "p": block_sum,
+            "s": small_assembly,
+            "o": out_assembly,
+        }
+        for mark in ORDER:
+            step = steps[mark] if mark in steps else sums[int(mark)].advance
+            token = step(token)
+
+        def in_weight_rows(*refs):
+            in_weight_body(gate_part, rest_parts, *refs)
+
+        pieces = [piece for part in sums[1:] for piece in part.pieces]
+        in_weight_rows_grad, norm_rows = assemble(
+            in_weight_rows,
+            [whole(weight.shape, f32), whole((8, half_width), f32)],
+            [after(pieces[0], token), *pieces[1:]],
+            LANES,
+        )
+        in_weight_grad = in_weight_rows_grad.T
+        out_weight_grad = state["out_weight"]
+        norm_gain_grad = norm_rows[0]
+    else:
+        for step in (out_projection, block_sum, input_norm, means_far, means_sib, tokens_grad):
+            step(token)
+        total = jnp.concatenate(
+            [(small_keep + small_far)[:7], row(state["norm_grad"])], axis=0
+        )
+        bits = 1
+        while bits < 2 * chips:
+            total = total + swap(total, bits, 0)
+            bits *= 2
+        norm_gain_grad = total[7, :half_width]
+        state["smalls"] = small_results(total, 6)
     return (
-        block_out,
-        grad_tokens,
-        total[7, :half_width],
+        state["block_out"],
+        state["grad_tokens"],
+        norm_gain_grad,
         in_weight_grad,
-        total[0:4],
-        total[4],
-        total[6, 0:half_heads],
-        total[6, LANES : LANES + half_heads],
-        total[6, 2 * LANES : 2 * LANES + half_heads],
-        total[5, :half_inner],
+        *state["smalls"],
         out_weight_grad,
     )
 

time: 218 us -> 206 us (0.945)
  starting transfers between devices: 50 us -> 38.5 us
    ppermute x60 -> x50, starting transfers between devices: 50 us -> 38.5 us  [swap(): return lax.ppermute(value, AXES, pairs)]
    unnamed x42 -> x36, local copies, waits for them, and re-layouts: 6.87 us -> 7.81 us
    pallas_call x22 -> x28, Pallas kernels: 25.5 us -> 24.8 us  [call(): pl.pallas_call(body, out_shape=out_shape, in_specs=in_specs, out_specs=[v...]
    ppermute x60 -> x50, waiting for transfers between devices: 122 us -> 122 us  [swap(): return lax.ppermute(value, AXES, pairs)]
  transfers between devices with their start and end apart: 60 -> 50, of which waited for: 21 -> 21; matrix products, arithmetic and copies ran while one was open for 2% -> 2% of each run, Pallas kernels for 13% -> 12%
where the time goes in v4:
time: 206 us
  waiting for transfers between devices  122 us (59%)
  starting transfers between devices  38.5 us (19%)
  Pallas kernels  32.4 us (16%)
  local copies, waits for them, and re-layouts  10.9 us (5%)
    ppermute x50, waiting for transfers between devices, swap(): return lax.ppermute(value, AXES, pairs)  122 us
    ppermute x50, starting transfers between devices, swap(): return lax.ppermute(value, AXES, pairs)  38.5 us
    pallas_call x28, Pallas kernels, call(): pl.pallas_call(body, out_shape=out_shape, in_specs=in_specs, out_specs=[v...  24.8 us
    unnamed x36, local copies, waits for them, and re-layouts  7.81 us
    pallas_call x2, Pallas kernels, assemble(): pl.pallas_call(body, grid=(outs[0].shape[1] // block,), out_shape=outs, i...  7.65 us
  transfers between devices with their start and end apart: 50, of which 21 were waited for; matrix products, arithmetic and copies ran while one was open for 2% of the time, Pallas kernels for 12%

profile of v4, /device:TPU:0, one launch (start us, length us, event | category | flops | bytes accessed | tf_op | source)
XLA Modules:
  0.0 206.2 jit_solution(5678770336447600822)
XLA Ops:
  0.6 3.0 %collective-permute-start.1 = (bf16[128,1024]{1,0:T(8,128)(2,1)}, bf16[128,1024]{1,0:T(8,128)(2,1)S(1)}, u32[]{:S(2)}, u32[]{:S(2)}) collective-permute-start(bf16[128,1024]{1,0:T(8,128)(2,1)} %cotangent_ref.3), channel_id=1, source_target_pairs={{0,1},{1,0},{2,3},{3,2},{4,5},{5,4},{6,7},{7,6},{8,9},{9,8},{10,11... | collective-permute-start | bytes 786440 | tf_op jit(solution)/shard_map/ppermute | solution.py:751
  4.4 6.6 %collective-permute-done.1.cotangent_ref.refs_5_ = bf16[128,1024]{1,0:T(8,128)(2,1)S(1)} collective-permute-done((bf16[128,1024]{1,0:T(8,128)(2,1)}, bf16[128,1024]{1,0:T(8,128)(2,1)S(1)}, u32[]{:S(2)}, u32[]{:S(2)}) %collective-permute-start.1) | collective-permute-done | bytes 262176 | tf_op jit(solution)/shard_map/ppermute | solution.py:751
  11.0 4.8 %collective-permute-done.refs_0_.refs_1_ = bf16[128,1024]{1,0:T(8,128)(2,1)S(1)} collective-permute-done((bf16[128,1024]{1,0:T(8,128)(2,1)}, bf16[128,1024]{1,0:T(8,128)(2,1)S(1)}, u32[]{:S(2)}, u32[]{:S(2)}) %collective-permute-start) | collective-permute-done | bytes 262176 | tf_op jit(solution)/shard_map/ppermute | solution.py:751
  15.8 2.3 %copy-done = bf16[512,4384]{0,1:T(8,128)(2,1)S(1)} copy-done((bf16[512,4384]{0,1:T(8,128)(2,1)S(1)}, bf16[512,4384]{0,1:T(8,128)(2,1)}, u32[]{:S(2)}) %copy-start) | copy-done | bytes 4489240
  21.8 2.3 %copy-done.1 = bf16[512,4384]{0,1:T(8,128)(2,1)S(1)} copy-done((bf16[512,4384]{0,1:T(8,128)(2,1)S(1)}, bf16[512,4384]{0,1:T(8,128)(2,1)}, u32[]{:S(2)}) %copy-start.1) | copy-done | bytes 4489240
  27.2 22.4 %collective-permute-done.3.peer_ref = f32[8,1152]{1,0:T(8,128)S(1)} collective-permute-done((f32[8,1152]{1,0:T(8,128)S(1)}, f32[8,1152]{1,0:T(8,128)S(1)}, u32[]{:S(2)}, u32[]{:S(2)}) %collective-permute-start.3) | collective-permute-done | bytes 36896 | tf_op jit(solution)/shard_map/ppermute | solution.py:751
  52.1 2.3 %copy-done.2 = bf16[512,4384]{0,1:T(8,128)(2,1)S(1)} copy-done((bf16[512,4384]{0,1:T(8,128)(2,1)S(1)}, bf16[512,4384]{0,1:T(8,128)(2,1)}, u32[]{:S(2)}) %copy-start.2) | copy-done | bytes 4489240
  54.4 2.3 %project_own_body.1 = (bf16[128,512]{1,0:T(8,128)(2,1)S(1)}, f32[128,2432]{1,0:T(8,128)S(1)}, f32[128,2048]{1,0:T(8,128)S(1)}, f32[128,1024]{1,0:T(8,128)S(1)}) custom-call(bf16[128,1024]{1,0:T(8,128)(2,1)S(1)} %copy-done.4, bf16[128,1024]{1,0:T(8,128)(2,1)S(1)} %copy-done.5, f32[1,512]{1,0:T(1,128)S(1)} %bitcast.18, bf16[4384,512]{1,0:T(8,128)(2,1)S(1)} %bitcast.13, ...), custom_call_target="tpu_custom_call" | custom-call | flops 1 | bytes 1 | tf_op jit(solution)/shard_map/project_own_body/pallas_call | solution.py:354
  56.9 3.4 %forward_body.1 = (f32[128,2304]{1,0:T(8,128)S(1)}, f32[128,2304]{1,0:T(8,128)S(1)}, f32[128,2048]{1,0:T(8,128)S(1)}, f32[3,128,32]{2,1,0:T(8,128)S(1)}) custom-call(s32[1,2]{1,0:T(1,128)S(1)} %copy-done.7, f32[128,2432]{1,0:T(8,128)S(1)} %get-tuple-element.108.own_ref, f32[128,2432]{1,0:T(8,128)} %collective-permute-done.2.got_ref, ...), custom_call_target="tpu_custom_call" | custom-call | flops 1 | bytes 1 | tf_op jit(solution)/shard_map/forward_body/pallas_call | solution.py:354
  60.3 7.5 %collective-permute-done.4.got_ref = bf16[128,3072]{1,0:T(8,128)(2,1)S(1)} collective-permute-done((bf16[128,3072]{1,0:T(8,128)(2,1)}, bf16[128,3072]{1,0:T(8,128)(2,1)S(1)}, u32[]{:S(2)}, u32[]{:S(2)}) %collective-permute-start.4) | collective-permute-done | bytes 786464 | tf_op jit(solution)/shard_map/ppermute | solution.py:751
  71.8 6.7 %backward_body.1 = (bf16[128,1280]{1,0:T(8,128)(2,1)S(1)}, bf16[128,1280]{1,0:T(8,128)(2,1)S(1)}, f32[8,1152]{1,0:T(8,128)S(1)}, f32[8,1152]{1,0:T(8,128)S(1)}) custom-call(s32[1,2]{1,0:T(1,128)S(1)} %copy-done.7, f32[128,2048]{1,0:T(8,128)S(1)} %get-tuple-element.126.dmixed_ref, f32[128,2304]{1,0:T(8,128)S(1)} %get-tuple-element.127.xbc_ref, ...), custom_call_target="tpu_custom_call" | custom-call | flops 1 | bytes 1 | tf_op jit(solution)/shard_map/backward_body/pallas_call | solution.py:354
  81.0 4.4 %collective-permute-done.12.refs_1_.refs_5_ = bf16[256,1024]{1,0:T(8,128)(2,1)S(1)} collective-permute-done((bf16[256,1024]{1,0:T(8,128)(2,1)S(1)}, bf16[256,1024]{1,0:T(8,128)(2,1)S(1)}, u32[]{:S(2)}, u32[]{:S(2)}) %collective-permute-start.12) | collective-permute-done | bytes 524320 | tf_op jit(solution)/shard_map/ppermute | solution.py:751
  96.7 7.2 %collective-permute-done.16.refs_1_.refs_9_ = bf16[128,1280]{1,0:T(8,128)(2,1)S(1)} collective-permute-done((bf16[128,1280]{1,0:T(8,128)(2,1)S(1)}, bf16[128,1280]{1,0:T(8,128)(2,1)S(1)}, u32[]{:S(2)}, u32[]{:S(2)}) %collective-permute-start.16) | collective-permute-done | bytes 327712 | tf_op jit(solution)/shard_map/ppermute | solution.py:751
  112.0 4.6 %collective-permute-done.21.refs_1_ = bf16[384,512]{1,0:T(8,128)(2,1)S(1)} collective-permute-done((bf16[384,512]{1,0:T(8,128)(2,1)S(1)}, bf16[384,512]{1,0:T(8,128)(2,1)S(1)}, u32[]{:S(2)}, u32[]{:S(2)}) %collective-permute-start.21) | collective-permute-done | bytes 393248 | tf_op jit(solution)/shard_map/ppermute | solution.py:751
  119.7 3.1 %collective-permute-done.24.got_ref = bf16[256,512]{1,0:T(8,128)(2,1)S(1)} collective-permute-done((bf16[256,512]{1,0:T(8,128)(2,1)S(1)}, bf16[256,512]{1,0:T(8,128)(2,1)S(1)}, u32[]{:S(2)}, u32[]{:S(2)}) %collective-permute-start.24) | collective-permute-done | bytes 262176 | tf_op jit(solution)/shard_map/ppermute | solution.py:751
  122.8 2.7 %collective-permute-start.30 = (bf16[272,512]{1,0:T(8,128)(2,1)S(1)}, bf16[272,512]{1,0:T(8,128)(2,1)S(1)}, u32[]{:S(2)}, u32[]{:S(2)}) collective-permute-start(bf16[272,512]{1,0:T(8,128)(2,1)S(1)} %add_body.9.keep_ref), channel_id=1, source_target_pairs={{0,16},{1,17},{2,18},{3,19},{4,20},{5,21},{6,22},{7,23},{8,24},{9,... | collective-permute-start | bytes 835592 | tf_op jit(solution)/shard_map/ppermute | solution.py:751
  125.8 3.6 %collective-permute-done.26.got_ref = bf16[192,512]{1,0:T(8,128)(2,1)S(1)} collective-permute-done((bf16[192,512]{1,0:T(8,128)(2,1)S(1)}, bf16[192,512]{1,0:T(8,128)(2,1)S(1)}, u32[]{:S(2)}, u32[]{:S(2)}) %collective-permute-start.26) | collective-permute-done | bytes 196640 | tf_op jit(solution)/shard_map/ppermute | solution.py:751
  132.0 2.5 %collective-permute-start.32 = (bf16[128,512]{1,0:T(8,128)(2,1)S(1)}, bf16[128,512]{1,0:T(8,128)(2,1)S(1)}, u32[]{:S(2)}, u32[]{:S(2)}) collective-permute-start(bf16[128,512]{1,0:T(8,128)(2,1)S(1)} %add_body.11.keep_ref), channel_id=1, source_target_pairs={{0,16},{1,17},{2,18},{3,19},{4,20},{5,21},{6,22},{7,23},{8,24},{9,... | collective-permute-start | bytes 393224 | tf_op jit(solution)/shard_map/ppermute | solution.py:751
  134.5 23.0 %collective-permute-done.29.got_ref = bf16[256,512]{1,0:T(8,128)(2,1)S(1)} collective-permute-done((bf16[256,512]{1,0:T(8,128)(2,1)S(1)}, bf16[256,512]{1,0:T(8,128)(2,1)S(1)}, u32[]{:S(2)}, u32[]{:S(2)}) %collective-permute-start.29) | collective-permute-done | bytes 262176 | tf_op jit(solution)/shard_map/ppermute | solution.py:751
  162.7 4.6 %collective-permute-done.34 = bf16[256,512]{1,0:T(8,128)(2,1)S(1)} collective-permute-done((bf16[256,512]{1,0:T(8,128)(2,1)S(1)}, bf16[256,512]{1,0:T(8,128)(2,1)S(1)}, u32[]{:S(2)}, u32[]{:S(2)}) %collective-permute-start.34) | collective-permute-done | bytes 262176 | tf_op jit(solution)/shard_map/ppermute | solution.py:751
  171.5 14.7 %collective-permute-done.36 = bf16[192,512]{1,0:T(8,128)(2,1)S(1)} collective-permute-done((bf16[192,512]{1,0:T(8,128)(2,1)S(1)}, bf16[192,512]{1,0:T(8,128)(2,1)S(1)}, u32[]{:S(2)}, u32[]{:S(2)}) %collective-permute-start.36) | collective-permute-done | bytes 196640 | tf_op jit(solution)/shard_map/ppermute | solution.py:751
  190.0 2.7 %out_weight_lanes.1 = f32[1024,1024]{1,0:T(8,128)} custom-call(bf16[512,512]{1,0:T(8,128)(2,1)S(1)} %constant_dynamic-update-slice_fusion.refs_0_, bf16[512,512]{1,0:T(8,128)(2,1)S(1)} %collective-permute-done.41.refs_1_, bf16[512,512]{1,0:T(8,128)(2,1)S(1)} %collective-permute-done.42.refs_2_, bf16[512,512]{1,0:T(8,128)(2,1)S(1)} %collective-permute-done.43.refs_3_), custom_call_target="tpu_custom_call" | custom-call | flops 1 | bytes 1 | tf_op jit(solution)/shard_map/out_weight_lanes/pallas_call | solution.py:729
  193.5 5.0 %collective-permute-done.39.refs_5_ = bf16[384,512]{1,0:T(8,128)(2,1)S(1)} collective-permute-done((bf16[384,512]{1,0:T(8,128)(2,1)S(1)}, bf16[384,512]{1,0:T(8,128)(2,1)S(1)}, u32[]{:S(2)}, u32[]{:S(2)}) %collective-permute-start.39) | collective-permute-done | bytes 393248 | tf_op jit(solution)/shard_map/ppermute | solution.py:751
  200.7 4.9 %in_weight_rows.1 = (f32[4384,512]{1,0:T(8,128)}, f32[8,512]{1,0:T(8,128)S(1)}) custom-call(bf16[544,512]{1,0:T(8,128)(2,1)S(1)} %constant_dynamic-update-slice_fusion.2.refs_0_, bf16[544,512]{1,0:T(8,128)(2,1)S(1)} %collective-permute-done.40.refs_1_, bf16[544,512]{1,0:T(8,128)(2,1)S(1)} %collective-permute-done.44.refs_2_, ...), custom_call_target="tpu_custom_call" | custom-call | flops 1 | bytes 1 | tf_op jit(solution)/shard_map/in_weight_rows/pallas_call | solution.py:729
  (169 shorter events, 58.6 us)
Async XLA Ops:
  3.6 12.1 %collective-permute-start = (bf16[128,1024]{1,0:T(8,128)(2,1)}, bf16[128,1024]{1,0:T(8,128)(2,1)S(1)}, u32[]{:S(2)}, u32[]{:S(2)}) collective-permute-start(bf16[128,1024]{1,0:T(8,128)(2,1)} %tokens_ref.2), channel_id=1, source_target_pairs={{0,1},{1,0},{2,3},{3,2},{4,5},{5,4},{6,7},{7,6},{8,9},{9,8},{10,11... | collective-permute-start | bytes 786440 | tf_op jit(solution)/shard_map/ppermute | solution.py:751
  20.1 29.6 %collective-permute-start.2 = (f32[128,2432]{1,0:T(8,128)}, f32[128,2432]{1,0:T(8,128)}, u32[]{:S(2)}, u32[]{:S(2)}) collective-permute-start(f32[128,2432]{1,0:T(8,128)} %get-tuple-element.106), channel_id=1, source_target_pairs={{0,1},{1,0},{2,3},{3,2},{4,5},{5,4},{6,7},{7,6},{8,9},{9,8},{10,11... | collective-permute-start | bytes 3735560 | tf_op jit(solution)/shard_map/ppermute | solution.py:751
  26.9 22.7 %collective-permute-start.3 = (f32[8,1152]{1,0:T(8,128)S(1)}, f32[8,1152]{1,0:T(8,128)S(1)}, u32[]{:S(2)}, u32[]{:S(2)}) collective-permute-start(f32[8,1152]{1,0:T(8,128)S(1)} %concatenate.46.mine_ref), channel_id=1, source_target_pairs={{0,1},{1,0},{2,3},{3,2},{4,5},{5,4},{6,7},{7,6},{8,9},{9,8},{10,11... | collective-permute-start | bytes 110600 | tf_op jit(solution)/shard_map/ppermute | solution.py:751
  49.6 18.1 %collective-permute-start.4 = (bf16[128,3072]{1,0:T(8,128)(2,1)}, bf16[128,3072]{1,0:T(8,128)(2,1)S(1)}, u32[]{:S(2)}, u32[]{:S(2)}) collective-permute-start(bf16[128,3072]{1,0:T(8,128)(2,1)} %copy-done.6), channel_id=1, source_target_pairs={{0,1},{1,0},{2,3},{3,2},{4,5},{5,4},{6,7},{7,6},{8,9},{9,8},{10,11... | collective-permute-start | bytes 2359304 | tf_op jit(solution)/shard_map/ppermute | solution.py:751
  51.6 18.0 %collective-permute-start.7 = (bf16[128,1024]{1,0:T(8,128)(2,1)S(1)}, bf16[128,1024]{1,0:T(8,128)(2,1)S(1)}, u32[]{:S(2)}, u32[]{:S(2)}) collective-permute-start(bf16[128,1024]{1,0:T(8,128)(2,1)S(1)} %copy-done.5), channel_id=1, source_target_pairs={{0,2},{1,3},{2,0},{3,1},{4,6},{5,7},{6,4},{7,5},{8,10},{9,11},{10,... | collective-permute-start | bytes 786440 | tf_op jit(solution)/shard_map/ppermute | solution.py:751
  51.6 18.0 %collective-permute-start.8 = (bf16[128,1024]{1,0:T(8,128)(2,1)S(1)}, bf16[128,1024]{1,0:T(8,128)(2,1)S(1)}, u32[]{:S(2)}, u32[]{:S(2)}) collective-permute-start(bf16[128,1024]{1,0:T(8,128)(2,1)S(1)} %collective-permute-done.1.cotangent_ref.refs_5_), channel_id=1, source_target_pairs={{0,2},{1,3},{2,0},{3,1},{4,6},{5,7},{6,4},{7,5},{8,10},{9,11},{10,... | collective-permute-start | bytes 786440 | tf_op jit(solution)/shard_map/ppermute | solution.py:751
  70.8 14.6 %collective-permute-start.12 = (bf16[256,1024]{1,0:T(8,128)(2,1)S(1)}, bf16[256,1024]{1,0:T(8,128)(2,1)S(1)}, u32[]{:S(2)}, u32[]{:S(2)}) collective-permute-start(bf16[256,1024]{1,0:T(8,128)(2,1)S(1)} %get-tuple-element.136), channel_id=1, source_target_pairs={{0,1},{1,0},{2,3},{3,2},{4,5},{5,4},{6,7},{7,6},{8,9},{9,8},{10,11... | collective-permute-start | bytes 1572872 | tf_op jit(solution)/shard_map/ppermute | solution.py:751
  90.1 13.8 %collective-permute-start.16 = (bf16[128,1280]{1,0:T(8,128)(2,1)S(1)}, bf16[128,1280]{1,0:T(8,128)(2,1)S(1)}, u32[]{:S(2)}, u32[]{:S(2)}) collective-permute-start(bf16[128,1280]{1,0:T(8,128)(2,1)S(1)} %get-tuple-element.149.refs_0_.refs_8_), channel_id=1, source_target_pairs={{0,1},{1,0},{2,3},{3,2},{4,5},{5,4},{6,7},{7,6},{8,9},{9,8},{10,11... | collective-permute-start | bytes 983048 | tf_op jit(solution)/shard_map/ppermute | solution.py:751
  91.4 19.8 %collective-permute-start.20 = (bf16[544,512]{1,0:T(8,128)(2,1)S(1)}, bf16[544,512]{1,0:T(8,128)(2,1)S(1)}, u32[]{:S(2)}, u32[]{:S(2)}) collective-permute-start(bf16[544,512]{1,0:T(8,128)(2,1)S(1)} %get-tuple-element.142), channel_id=1, source_target_pairs={{0,8},{1,9},{2,10},{3,11},{4,12},{5,13},{6,14},{7,15},{8,0},{9,1},... | collective-permute-start | bytes 1671176 | tf_op jit(solution)/shard_map/ppermute | solution.py:751
  93.5 17.1 %collective-permute-start.19 = (bf16[512,512]{1,0:T(8,128)(2,1)S(1)}, bf16[512,512]{1,0:T(8,128)(2,1)S(1)}, u32[]{:S(2)}, u32[]{:S(2)}) collective-permute-start(bf16[512,512]{1,0:T(8,128)(2,1)S(1)} %get-tuple-element.134), channel_id=1, source_target_pairs={{0,4},{1,5},{2,6},{3,7},{4,0},{5,1},{6,2},{7,3},{8,12},{9,13},{10,... | collective-permute-start | bytes 1572872 | tf_op jit(solution)/shard_map/ppermute | solution.py:751
  104.6 12.1 %collective-permute-start.21 = (bf16[384,512]{1,0:T(8,128)(2,1)S(1)}, bf16[384,512]{1,0:T(8,128)(2,1)S(1)}, u32[]{:S(2)}, u32[]{:S(2)}) collective-permute-start(bf16[384,512]{1,0:T(8,128)(2,1)S(1)} %get-tuple-element.145), channel_id=1, source_target_pairs={{0,4},{1,5},{2,6},{3,7},{4,0},{5,1},{6,2},{7,3},{8,12},{9,13},{10,... | collective-permute-start | bytes 1179656 | tf_op jit(solution)/shard_map/ppermute | solution.py:751
  110.7 12.0 %collective-permute-start.24 = (bf16[256,512]{1,0:T(8,128)(2,1)S(1)}, bf16[256,512]{1,0:T(8,128)(2,1)S(1)}, u32[]{:S(2)}, u32[]{:S(2)}) collective-permute-start(bf16[256,512]{1,0:T(8,128)(2,1)S(1)} %get-tuple-element.158), channel_id=1, source_target_pairs={{0,8},{1,9},{2,10},{3,11},{4,12},{5,13},{6,14},{7,15},{8,0},{9,1},... | collective-permute-start | bytes 786440 | tf_op jit(solution)/shard_map/ppermute | solution.py:751
  117.4 12.1 %collective-permute-start.28 = (bf16[256,512]{1,0:T(8,128)(2,1)S(1)}, bf16[256,512]{1,0:T(8,128)(2,1)S(1)}, u32[]{:S(2)}, u32[]{:S(2)}) collective-permute-start(bf16[256,512]{1,0:T(8,128)(2,1)S(1)} %pad_maximum_fusion), channel_id=1, source_target_pairs={{0,2},{1,3},{2,0},{3,1},{4,6},{5,7},{6,4},{7,5},{8,10},{9,11},{10,... | collective-permute-start | bytes 786440 | tf_op jit(solution)/shard_map/ppermute | solution.py:751
  117.5 12.0 %collective-permute-start.26 = (bf16[192,512]{1,0:T(8,128)(2,1)S(1)}, bf16[192,512]{1,0:T(8,128)(2,1)S(1)}, u32[]{:S(2)}, u32[]{:S(2)}) collective-permute-start(bf16[192,512]{1,0:T(8,128)(2,1)S(1)} %get-tuple-element.162), channel_id=1, source_target_pairs={{0,8},{1,9},{2,10},{3,11},{4,12},{5,13},{6,14},{7,15},{8,0},{9,1},... | collective-permute-start | bytes 589832 | tf_op jit(solution)/shard_map/ppermute | solution.py:751
  122.8 34.8 %collective-permute-start.30 = (bf16[272,512]{1,0:T(8,128)(2,1)S(1)}, bf16[272,512]{1,0:T(8,128)(2,1)S(1)}, u32[]{:S(2)}, u32[]{:S(2)}) collective-permute-start(bf16[272,512]{1,0:T(8,128)(2,1)S(1)} %add_body.9.keep_ref), channel_id=1, source_target_pairs={{0,16},{1,17},{2,18},{3,19},{4,20},{5,21},{6,22},{7,23},{8,24},{9,... | collective-permute-start | bytes 835592 | tf_op jit(solution)/shard_map/ppermute | solution.py:751
  125.5 32.0 %collective-permute-start.29 = (bf16[256,512]{1,0:T(8,128)(2,1)S(1)}, bf16[256,512]{1,0:T(8,128)(2,1)S(1)}, u32[]{:S(2)}, u32[]{:S(2)}) collective-permute-start(bf16[256,512]{1,0:T(8,128)(2,1)S(1)} %add_body.8.keep_ref), channel_id=1, source_target_pairs={{0,16},{1,17},{2,18},{3,19},{4,20},{5,21},{6,22},{7,23},{8,24},{9,... | collective-permute-start | bytes 786440 | tf_op jit(solution)/shard_map/ppermute | solution.py:751
  131.4 30.4 %collective-permute-start.33 = (bf16[128,1024]{1,0:T(8,128)(2,1)S(1)}, bf16[128,1024]{1,0:T(8,128)(2,1)S(1)}, u32[]{:S(2)}, u32[]{:S(2)}) collective-permute-start(bf16[128,1024]{1,0:T(8,128)(2,1)S(1)} %get-tuple-element.178), channel_id=1, source_target_pairs={{0,1},{1,0},{2,3},{3,2},{4,5},{5,4},{6,7},{7,6},{8,9},{9,8},{10,11... | collective-permute-start | bytes 786440 | tf_op jit(solution)/shard_map/ppermute | solution.py:751
  131.5 28.9 %collective-permute-start.31 = (bf16[192,512]{1,0:T(8,128)(2,1)S(1)}, bf16[192,512]{1,0:T(8,128)(2,1)S(1)}, u32[]{:S(2)}, u32[]{:S(2)}) collective-permute-start(bf16[192,512]{1,0:T(8,128)(2,1)S(1)} %add_body.10.keep_ref), channel_id=1, source_target_pairs={{0,16},{1,17},{2,18},{3,19},{4,20},{5,21},{6,22},{7,23},{8,24},{9,... | collective-permute-start | bytes 589832 | tf_op jit(solution)/shard_map/ppermute | solution.py:751
  132.0 29.8 %collective-permute-start.32 = (bf16[128,512]{1,0:T(8,128)(2,1)S(1)}, bf16[128,512]{1,0:T(8,128)(2,1)S(1)}, u32[]{:S(2)}, u32[]{:S(2)}) collective-permute-start(bf16[128,512]{1,0:T(8,128)(2,1)S(1)} %add_body.11.keep_ref), channel_id=1, source_target_pairs={{0,16},{1,17},{2,18},{3,19},{4,20},{5,21},{6,22},{7,23},{8,24},{9,... | collective-permute-start | bytes 393224 | tf_op jit(solution)/shard_map/ppermute | solution.py:751
  167.4 18.9 %collective-permute-start.40 = (bf16[544,512]{1,0:T(8,128)(2,1)S(1)}, bf16[544,512]{1,0:T(8,128)(2,1)S(1)}, u32[]{:S(2)}, u32[]{:S(2)}) collective-permute-start(bf16[544,512]{1,0:T(8,128)(2,1)S(1)} %constant_dynamic-update-slice_fusion.2.refs_0_), channel_id=1, source_target_pairs={{0,8},{1,9},{2,10},{3,11},{4,12},{5,13},{6,14},{7,15},{8,0},{9,1},... | collective-permute-start | bytes 1671176 | tf_op jit(solution)/shard_map/ppermute | solution.py:751
  167.5 18.7 %collective-permute-start.36 = (bf16[192,512]{1,0:T(8,128)(2,1)S(1)}, bf16[192,512]{1,0:T(8,128)(2,1)S(1)}, u32[]{:S(2)}, u32[]{:S(2)}) collective-permute-start(bf16[192,512]{1,0:T(8,128)(2,1)S(1)} %add_body.14), channel_id=1, source_target_pairs={{0,8},{1,9},{2,10},{3,11},{4,12},{5,13},{6,14},{7,15},{8,0},{9,1},... | collective-permute-start | bytes 589832 | tf_op jit(solution)/shard_map/ppermute | solution.py:751
  169.5 16.8 %collective-permute-start.41 = (bf16[512,512]{1,0:T(8,128)(2,1)S(1)}, bf16[512,512]{1,0:T(8,128)(2,1)S(1)}, u32[]{:S(2)}, u32[]{:S(2)}) collective-permute-start(bf16[512,512]{1,0:T(8,128)(2,1)S(1)} %constant_dynamic-update-slice_fusion.refs_0_), channel_id=1, source_target_pairs={{0,4},{1,5},{2,6},{3,7},{4,0},{5,1},{6,2},{7,3},{8,12},{9,13},{10,... | collective-permute-start | bytes 1572872 | tf_op jit(solution)/shard_map/ppermute | solution.py:751
  171.0 15.2 %collective-permute-start.37 = (bf16[128,512]{1,0:T(8,128)(2,1)S(1)}, bf16[128,512]{1,0:T(8,128)(2,1)S(1)}, u32[]{:S(2)}, u32[]{:S(2)}) collective-permute-start(bf16[128,512]{1,0:T(8,128)(2,1)S(1)} %add_body.15), channel_id=1, source_target_pairs={{0,4},{1,5},{2,6},{3,7},{4,0},{5,1},{6,2},{7,3},{8,12},{9,13},{10,... | collective-permute-start | bytes 393224 | tf_op jit(solution)/shard_map/ppermute | solution.py:751
  171.5 17.0 %collective-permute-start.42 = (bf16[512,512]{1,0:T(8,128)(2,1)S(1)}, bf16[512,512]{1,0:T(8,128)(2,1)S(1)}, u32[]{:S(2)}, u32[]{:S(2)}) collective-permute-start(bf16[512,512]{1,0:T(8,128)(2,1)S(1)} %constant_dynamic-update-slice_fusion.refs_0_), channel_id=1, source_target_pairs={{0,2},{1,3},{2,0},{3,1},{4,6},{5,7},{6,4},{7,5},{8,10},{9,11},{10,... | collective-permute-start | bytes 1572872 | tf_op jit(solution)/shard_map/ppermute | solution.py:751
  (42 other events, 374.2 us)

commit v5 on v4

--- a/solution.py
+++ b/solution.py
@@ -64,7 +64,7 @@
     )
 
 
-def forward_body(lens_ref, own_ref, got_ref, mine_ref, peer_ref, xbc_ref, conv_ref, mixed_ref, rates_ref):
+def forward_body(lens_ref, own_ref, wide_ref, got_ref, mine_ref, peer_ref, xbc_ref, conv_ref, mixed_ref, rates_ref):
     rows, channels = conv_ref.shape
     tiles = channels // LANES
     pairs = tiles - 2
@@ -78,7 +78,8 @@
     decay = both[6:7, LANES : LANES + heads]
     skip = both[6:7, 2 * LANES : 2 * LANES + heads]
     tail = slice(channels, channels + heads)
-    rate = own_ref[:, tail] + got_ref[:, tail].astype(jnp.float32) + bias
+    wide = wide_ref.shape[1]
+    rate = own_ref[:, tail] + got_ref[:, channels - wide : channels - wide + heads] + bias
     step = jnp.maximum(rate, 0.0) + jnp.log1p(jnp.exp(-jnp.abs(rate)))
     rate_sigmoid = jax.nn.sigmoid(rate)
     lower = jnp.where(
@@ -96,7 +97,11 @@
 
     def active_tile(tile):
         at = tile * LANES
-        xbc = own_ref[:, at : at + LANES] + got_ref[:, at : at + LANES].astype(jnp.float32)
+        if at < wide:
+            far = wide_ref[:, at : at + LANES].astype(jnp.float32)
+        else:
+            far = got_ref[:, at - wide : at - wide + LANES]
+        xbc = own_ref[:, at : at + LANES] + far
         xbc_ref[:, at : at + LANES] = xbc
         conv = channel_row(low, high, 4, tile) + channel_row(low, high, taps - 1, tile) * xbc
         for k in range(taps - 1):
@@ -414,10 +419,14 @@
     q_ref[...] = lanes_product(cotangent_ref[...], out_weight_ref[...])
 
 
-def project_far_body(inner_width, tokens_ref, gain_ref, weight_ref, normed_ref, rest_ref):
+def project_far_body(inner_width, tokens_ref, gain_ref, weight_ref, normed_ref, wide_ref, rest_ref):
     normed = (half_means(tokens_ref, normed_ref.shape[1]) * gain_ref[...]).astype(jnp.bfloat16)
     normed_ref[...] = normed
-    project_rest(normed, weight_ref, rest_ref, inner_width)
+    wide = wide_ref.shape[1]
+    wide_ref[...] = lanes_product(
+        normed, weight_ref[inner_width : inner_width + wide, :]
+    ).astype(wide_ref.dtype)
+    project_rest(normed, weight_ref, rest_ref, inner_width + wide)
 
 
 def gate_far_body(normed_ref, cotangent_ref, weight_ref, out_weight_ref, send_ref):
@@ -826,12 +835,16 @@
     def project_far(*refs):
         project_far_body(inner_width, *refs)
 
-    normed_far, rest_send = call(
+    normed_far, wide_send, rest_send = call(
         project_far,
-        [whole((rows, half_width), low), whole((rows, channels + LANES), f32)],
+        [
+            whole((rows, half_width), low),
+            whole((rows, inner_width), low),
+            whole((rows, channels + LANES - inner_width), f32),
+        ],
         (after(tokens_far, cotangent_far), gain, weight),
     )
-    rest_got = swap_owner(rest_send)
+    rest_got, wide_got = swap_owner(rest_send), swap_owner(wide_send)
     normed_own, rest_own, gate_own, q_own = call(
         project_own_body,
         [
@@ -875,7 +888,7 @@
         axis=0,
     )
     peer = swap_owner(mine)
-    gate_got = swap_owner(after(gate_send, rest_got, peer))
+    gate_got = swap_owner(after(gate_send, rest_got, wide_got, peer))
     tokens_sib, tokens_far_sib = swap_core(tokens), swap_core(tokens_far)
     cotangent_sib, cotangent_far_sib = swap_core(cotangent), swap_core(cotangent_far)
     normed_sib, normed_far_sib = call(
@@ -892,7 +905,7 @@
             whole((rows, inner_width), f32),
             whole((3, rows, heads), f32),
         ],
-        (rest_own, rest_got, mine, peer),
+        (rest_own, wide_got, rest_got, mine, peer),
         lens=seq_lens,
     )
     out_keep, out_send, inverse = call(

time: 206 us -> 195 us (0.947)
  waiting for transfers between devices: 122 us -> 109 us
    ppermute x50 -> x51, waiting for transfers between devices: 122 us -> 109 us  [swap(): return lax.ppermute(value, AXES, pairs)]
    ppermute x50 -> x51, starting transfers between devices: 38.5 us -> 40.3 us  [swap(): return lax.ppermute(value, AXES, pairs)]
  transfers between devices with their start and end apart: 50 -> 51, of which waited for: 21 -> 21; matrix products, arithmetic and copies ran while one was open for 2% -> 3% of each run, Pallas kernels for 12% -> 13%
where the time goes in v5:
time: 195 us
  waiting for transfers between devices  109 us (56%)
  starting transfers between devices  40.3 us (21%)
  Pallas kernels  31.9 us (16%)
  local copies, waits for them, and re-layouts  10.9 us (6%)
    ppermute x51, waiting for transfers between devices, swap(): return lax.ppermute(value, AXES, pairs)  109 us
    ppermute x51, starting transfers between devices, swap(): return lax.ppermute(value, AXES, pairs)  40.3 us
    pallas_call x28, Pallas kernels, call(): pl.pallas_call(body, out_shape=out_shape, in_specs=in_specs, out_specs=[v...  24.3 us
    pallas_call x2, Pallas kernels, assemble(): pl.pallas_call(body, grid=(outs[0].shape[1] // block,), out_shape=outs, i...  7.65 us
    unnamed x36, local copies, waits for them, and re-layouts  7.13 us
  transfers between devices with their start and end apart: 51, of which 21 were waited for; matrix products, arithmetic and copies ran while one was open for 3% of the time, Pallas kernels for 13%

profile of v5, /device:TPU:0, one launch (start us, length us, event | category | flops | bytes accessed | tf_op | source)
XLA Modules:
  0.0 194.7 jit_solution(824591858136919579)
XLA Ops:
  0.6 3.0 %collective-permute-start.1 = (bf16[128,1024]{1,0:T(8,128)(2,1)}, bf16[128,1024]{1,0:T(8,128)(2,1)S(1)}, u32[]{:S(2)}, u32[]{:S(2)}) collective-permute-start(bf16[128,1024]{1,0:T(8,128)(2,1)} %cotangent_ref.3), channel_id=1, source_target_pairs={{0,1},{1,0},{2,3},{3,2},{4,5},{5,4},{6,7},{7,6},{8,9},{9,8},{10,11... | collective-permute-start | bytes 786440 | tf_op jit(solution)/shard_map/ppermute | solution.py:760
  4.4 6.6 %collective-permute-done.1.cotangent_ref.refs_5_ = bf16[128,1024]{1,0:T(8,128)(2,1)S(1)} collective-permute-done((bf16[128,1024]{1,0:T(8,128)(2,1)}, bf16[128,1024]{1,0:T(8,128)(2,1)S(1)}, u32[]{:S(2)}, u32[]{:S(2)}) %collective-permute-start.1) | collective-permute-done | bytes 262176 | tf_op jit(solution)/shard_map/ppermute | solution.py:760
  11.0 4.8 %collective-permute-done.refs_0_.refs_1_ = bf16[128,1024]{1,0:T(8,128)(2,1)S(1)} collective-permute-done((bf16[128,1024]{1,0:T(8,128)(2,1)}, bf16[128,1024]{1,0:T(8,128)(2,1)S(1)}, u32[]{:S(2)}, u32[]{:S(2)}) %collective-permute-start) | collective-permute-done | bytes 262176 | tf_op jit(solution)/shard_map/ppermute | solution.py:760
  15.8 2.3 %copy-done = bf16[512,4384]{0,1:T(8,128)(2,1)S(1)} copy-done((bf16[512,4384]{0,1:T(8,128)(2,1)S(1)}, bf16[512,4384]{0,1:T(8,128)(2,1)}, u32[]{:S(2)}) %copy-start) | copy-done | bytes 4489240
  28.7 9.4 %collective-permute-done.4.peer_ref = f32[8,1152]{1,0:T(8,128)S(1)} collective-permute-done((f32[8,1152]{1,0:T(8,128)S(1)}, f32[8,1152]{1,0:T(8,128)S(1)}, u32[]{:S(2)}, u32[]{:S(2)}) %collective-permute-start.4) | collective-permute-done | bytes 36896 | tf_op jit(solution)/shard_map/ppermute | solution.py:760
  40.6 2.3 %copy-done.2 = bf16[512,4384]{0,1:T(8,128)(2,1)S(1)} copy-done((bf16[512,4384]{0,1:T(8,128)(2,1)S(1)}, bf16[512,4384]{0,1:T(8,128)(2,1)}, u32[]{:S(2)}) %copy-start.2) | copy-done | bytes 4489240
  42.8 2.3 %project_own_body.1 = (bf16[128,512]{1,0:T(8,128)(2,1)S(1)}, f32[128,2432]{1,0:T(8,128)S(1)}, f32[128,2048]{1,0:T(8,128)S(1)}, f32[128,1024]{1,0:T(8,128)S(1)}) custom-call(bf16[128,1024]{1,0:T(8,128)(2,1)S(1)} %copy-done.5, bf16[128,1024]{1,0:T(8,128)(2,1)S(1)} %copy-done.6, f32[1,512]{1,0:T(1,128)S(1)} %bitcast.18, bf16[4384,512]{1,0:T(8,128)(2,1)S(1)} %bitcast.13, ...), custom_call_target="tpu_custom_call" | custom-call | flops 1 | bytes 1 | tf_op jit(solution)/shard_map/project_own_body/pallas_call | solution.py:359
  45.4 3.2 %forward_body.1 = (f32[128,2304]{1,0:T(8,128)S(1)}, f32[128,2304]{1,0:T(8,128)S(1)}, f32[128,2048]{1,0:T(8,128)S(1)}, f32[3,128,32]{2,1,0:T(8,128)S(1)}) custom-call(s32[1,2]{1,0:T(1,128)S(1)} %copy-done.8, f32[128,2432]{1,0:T(8,128)S(1)} %get-tuple-element.109.own_ref, bf16[128,2048]{1,0:T(8,128)(2,1)} %collective-permute-done.2.wide_ref, ...), custom_call_target="tpu_custom_call" | custom-call | flops 1 | bytes 1 | tf_op jit(solution)/shard_map/forward_body/pallas_call | solution.py:359
  48.6 7.7 %collective-permute-done.5.got_ref = bf16[128,3072]{1,0:T(8,128)(2,1)S(1)} collective-permute-done((bf16[128,3072]{1,0:T(8,128)(2,1)}, bf16[128,3072]{1,0:T(8,128)(2,1)S(1)}, u32[]{:S(2)}, u32[]{:S(2)}) %collective-permute-start.5) | collective-permute-done | bytes 786464 | tf_op jit(solution)/shard_map/ppermute | solution.py:760
  60.3 6.7 %backward_body.1 = (bf16[128,1280]{1,0:T(8,128)(2,1)S(1)}, bf16[128,1280]{1,0:T(8,128)(2,1)S(1)}, f32[8,1152]{1,0:T(8,128)S(1)}, f32[8,1152]{1,0:T(8,128)S(1)}) custom-call(s32[1,2]{1,0:T(1,128)S(1)} %copy-done.8, f32[128,2048]{1,0:T(8,128)S(1)} %get-tuple-element.128.dmixed_ref, f32[128,2304]{1,0:T(8,128)S(1)} %get-tuple-element.129.xbc_ref, ...), custom_call_target="tpu_custom_call" | custom-call | flops 1 | bytes 1 | tf_op jit(solution)/shard_map/backward_body/pallas_call | solution.py:359
  69.5 4.4 %collective-permute-done.13.refs_1_.refs_5_ = bf16[256,1024]{1,0:T(8,128)(2,1)S(1)} collective-permute-done((bf16[256,1024]{1,0:T(8,128)(2,1)S(1)}, bf16[256,1024]{1,0:T(8,128)(2,1)S(1)}, u32[]{:S(2)}, u32[]{:S(2)}) %collective-permute-start.13) | collective-permute-done | bytes 524320 | tf_op jit(solution)/shard_map/ppermute | solution.py:760
  85.2 7.2 %collective-permute-done.17.refs_1_.refs_9_ = bf16[128,1280]{1,0:T(8,128)(2,1)S(1)} collective-permute-done((bf16[128,1280]{1,0:T(8,128)(2,1)S(1)}, bf16[128,1280]{1,0:T(8,128)(2,1)S(1)}, u32[]{:S(2)}, u32[]{:S(2)}) %collective-permute-start.17) | collective-permute-done | bytes 327712 | tf_op jit(solution)/shard_map/ppermute | solution.py:760
  100.5 4.6 %collective-permute-done.22.refs_1_ = bf16[384,512]{1,0:T(8,128)(2,1)S(1)} collective-permute-done((bf16[384,512]{1,0:T(8,128)(2,1)S(1)}, bf16[384,512]{1,0:T(8,128)(2,1)S(1)}, u32[]{:S(2)}, u32[]{:S(2)}) %collective-permute-start.22) | collective-permute-done | bytes 393248 | tf_op jit(solution)/shard_map/ppermute | solution.py:760
  108.1 3.1 %collective-permute-done.25.got_ref = bf16[256,512]{1,0:T(8,128)(2,1)S(1)} collective-permute-done((bf16[256,512]{1,0:T(8,128)(2,1)S(1)}, bf16[256,512]{1,0:T(8,128)(2,1)S(1)}, u32[]{:S(2)}, u32[]{:S(2)}) %collective-permute-start.25) | collective-permute-done | bytes 262176 | tf_op jit(solution)/shard_map/ppermute | solution.py:760
  111.3 2.7 %collective-permute-start.31 = (bf16[272,512]{1,0:T(8,128)(2,1)S(1)}, bf16[272,512]{1,0:T(8,128)(2,1)S(1)}, u32[]{:S(2)}, u32[]{:S(2)}) collective-permute-start(bf16[272,512]{1,0:T(8,128)(2,1)S(1)} %add_body.9.keep_ref), channel_id=1, source_target_pairs={{0,16},{1,17},{2,18},{3,19},{4,20},{5,21},{6,22},{7,23},{8,24},{9,... | collective-permute-start | bytes 835592 | tf_op jit(solution)/shard_map/ppermute | solution.py:760
  114.3 3.6 %collective-permute-done.27.got_ref = bf16[192,512]{1,0:T(8,128)(2,1)S(1)} collective-permute-done((bf16[192,512]{1,0:T(8,128)(2,1)S(1)}, bf16[192,512]{1,0:T(8,128)(2,1)S(1)}, u32[]{:S(2)}, u32[]{:S(2)}) %collective-permute-start.27) | collective-permute-done | bytes 196640 | tf_op jit(solution)/shard_map/ppermute | solution.py:760
  120.6 2.4 %collective-permute-start.33 = (bf16[128,512]{1,0:T(8,128)(2,1)S(1)}, bf16[128,512]{1,0:T(8,128)(2,1)S(1)}, u32[]{:S(2)}, u32[]{:S(2)}) collective-permute-start(bf16[128,512]{1,0:T(8,128)(2,1)S(1)} %add_body.11.keep_ref), channel_id=1, source_target_pairs={{0,16},{1,17},{2,18},{3,19},{4,20},{5,21},{6,22},{7,23},{8,24},{9,... | collective-permute-start | bytes 393224 | tf_op jit(solution)/shard_map/ppermute | solution.py:760
  122.9 23.0 %collective-permute-done.30.got_ref = bf16[256,512]{1,0:T(8,128)(2,1)S(1)} collective-permute-done((bf16[256,512]{1,0:T(8,128)(2,1)S(1)}, bf16[256,512]{1,0:T(8,128)(2,1)S(1)}, u32[]{:S(2)}, u32[]{:S(2)}) %collective-permute-start.30) | collective-permute-done | bytes 262176 | tf_op jit(solution)/shard_map/ppermute | solution.py:760
  146.8 2.1 %collective-permute-done.32.got_ref = bf16[192,512]{1,0:T(8,128)(2,1)S(1)} collective-permute-done((bf16[192,512]{1,0:T(8,128)(2,1)S(1)}, bf16[192,512]{1,0:T(8,128)(2,1)S(1)}, u32[]{:S(2)}, u32[]{:S(2)}) %collective-permute-start.32) | collective-permute-done | bytes 196640 | tf_op jit(solution)/shard_map/ppermute | solution.py:760
  151.1 4.6 %collective-permute-done.35 = bf16[256,512]{1,0:T(8,128)(2,1)S(1)} collective-permute-done((bf16[256,512]{1,0:T(8,128)(2,1)S(1)}, bf16[256,512]{1,0:T(8,128)(2,1)S(1)}, u32[]{:S(2)}, u32[]{:S(2)}) %collective-permute-start.35) | collective-permute-done | bytes 262176 | tf_op jit(solution)/shard_map/ppermute | solution.py:760
  160.0 14.7 %collective-permute-done.37 = bf16[192,512]{1,0:T(8,128)(2,1)S(1)} collective-permute-done((bf16[192,512]{1,0:T(8,128)(2,1)S(1)}, bf16[192,512]{1,0:T(8,128)(2,1)S(1)}, u32[]{:S(2)}, u32[]{:S(2)}) %collective-permute-start.37) | collective-permute-done | bytes 196640 | tf_op jit(solution)/shard_map/ppermute | solution.py:760
  178.5 2.7 %out_weight_lanes.1 = f32[1024,1024]{1,0:T(8,128)} custom-call(bf16[512,512]{1,0:T(8,128)(2,1)S(1)} %constant_dynamic-update-slice_fusion.refs_0_, bf16[512,512]{1,0:T(8,128)(2,1)S(1)} %collective-permute-done.42.refs_1_, bf16[512,512]{1,0:T(8,128)(2,1)S(1)} %collective-permute-done.43.refs_2_, bf16[512,512]{1,0:T(8,128)(2,1)S(1)} %collective-permute-done.44.refs_3_), custom_call_target="tpu_custom_call" | custom-call | flops 1 | bytes 1 | tf_op jit(solution)/shard_map/out_weight_lanes/pallas_call | solution.py:738
  181.9 5.0 %collective-permute-done.40.refs_5_ = bf16[384,512]{1,0:T(8,128)(2,1)S(1)} collective-permute-done((bf16[384,512]{1,0:T(8,128)(2,1)S(1)}, bf16[384,512]{1,0:T(8,128)(2,1)S(1)}, u32[]{:S(2)}, u32[]{:S(2)}) %collective-permute-start.40) | collective-permute-done | bytes 393248 | tf_op jit(solution)/shard_map/ppermute | solution.py:760
  189.1 4.9 %in_weight_rows.1 = (f32[4384,512]{1,0:T(8,128)}, f32[8,512]{1,0:T(8,128)S(1)}) custom-call(bf16[544,512]{1,0:T(8,128)(2,1)S(1)} %constant_dynamic-update-slice_fusion.2.refs_0_, bf16[544,512]{1,0:T(8,128)(2,1)S(1)} %collective-permute-done.41.refs_1_, bf16[544,512]{1,0:T(8,128)(2,1)S(1)} %collective-permute-done.45.refs_2_, ...), custom_call_target="tpu_custom_call" | custom-call | flops 1 | bytes 1 | tf_op jit(solution)/shard_map/in_weight_rows/pallas_call | solution.py:738
  (171 shorter events, 60.3 us)
Async XLA Ops:
  3.6 12.1 %collective-permute-start = (bf16[128,1024]{1,0:T(8,128)(2,1)}, bf16[128,1024]{1,0:T(8,128)(2,1)S(1)}, u32[]{:S(2)}, u32[]{:S(2)}) collective-permute-start(bf16[128,1024]{1,0:T(8,128)(2,1)} %tokens_ref.2), channel_id=1, source_target_pairs={{0,1},{1,0},{2,3},{3,2},{4,5},{5,4},{6,7},{7,6},{8,9},{9,8},{10,11... | collective-permute-start | bytes 786440 | tf_op jit(solution)/shard_map/ppermute | solution.py:760
  19.8 18.3 %collective-permute-start.3 = (f32[128,384]{1,0:T(8,128)}, f32[128,384]{1,0:T(8,128)S(1)}, u32[]{:S(2)}, u32[]{:S(2)}) collective-permute-start(f32[128,384]{1,0:T(8,128)} %get-tuple-element.107), channel_id=1, source_target_pairs={{0,1},{1,0},{2,3},{3,2},{4,5},{5,4},{6,7},{7,6},{8,9},{9,8},{10,11... | collective-permute-start | bytes 589832 | tf_op jit(solution)/shard_map/ppermute | solution.py:760
  21.5 16.6 %collective-permute-start.2 = (bf16[128,2048]{1,0:T(8,128)(2,1)}, bf16[128,2048]{1,0:T(8,128)(2,1)}, u32[]{:S(2)}, u32[]{:S(2)}) collective-permute-start(bf16[128,2048]{1,0:T(8,128)(2,1)} %get-tuple-element.110), channel_id=1, source_target_pairs={{0,1},{1,0},{2,3},{3,2},{4,5},{5,4},{6,7},{7,6},{8,9},{9,8},{10,11... | collective-permute-start | bytes 1572872 | tf_op jit(solution)/shard_map/ppermute | solution.py:760
  38.1 18.1 %collective-permute-start.5 = (bf16[128,3072]{1,0:T(8,128)(2,1)}, bf16[128,3072]{1,0:T(8,128)(2,1)S(1)}, u32[]{:S(2)}, u32[]{:S(2)}) collective-permute-start(bf16[128,3072]{1,0:T(8,128)(2,1)} %copy-done.7), channel_id=1, source_target_pairs={{0,1},{1,0},{2,3},{3,2},{4,5},{5,4},{6,7},{7,6},{8,9},{9,8},{10,11... | collective-permute-start | bytes 2359304 | tf_op jit(solution)/shard_map/ppermute | solution.py:760
  40.0 18.0 %collective-permute-start.8 = (bf16[128,1024]{1,0:T(8,128)(2,1)S(1)}, bf16[128,1024]{1,0:T(8,128)(2,1)S(1)}, u32[]{:S(2)}, u32[]{:S(2)}) collective-permute-start(bf16[128,1024]{1,0:T(8,128)(2,1)S(1)} %copy-done.6), channel_id=1, source_target_pairs={{0,2},{1,3},{2,0},{3,1},{4,6},{5,7},{6,4},{7,5},{8,10},{9,11},{10,... | collective-permute-start | bytes 786440 | tf_op jit(solution)/shard_map/ppermute | solution.py:760
  40.0 18.0 %collective-permute-start.9 = (bf16[128,1024]{1,0:T(8,128)(2,1)S(1)}, bf16[128,1024]{1,0:T(8,128)(2,1)S(1)}, u32[]{:S(2)}, u32[]{:S(2)}) collective-permute-start(bf16[128,1024]{1,0:T(8,128)(2,1)S(1)} %collective-permute-done.1.cotangent_ref.refs_5_), channel_id=1, source_target_pairs={{0,2},{1,3},{2,0},{3,1},{4,6},{5,7},{6,4},{7,5},{8,10},{9,11},{10,... | collective-permute-start | bytes 786440 | tf_op jit(solution)/shard_map/ppermute | solution.py:760
  59.3 14.6 %collective-permute-start.13 = (bf16[256,1024]{1,0:T(8,128)(2,1)S(1)}, bf16[256,1024]{1,0:T(8,128)(2,1)S(1)}, u32[]{:S(2)}, u32[]{:S(2)}) collective-permute-start(bf16[256,1024]{1,0:T(8,128)(2,1)S(1)} %get-tuple-element.138), channel_id=1, source_target_pairs={{0,1},{1,0},{2,3},{3,2},{4,5},{5,4},{6,7},{7,6},{8,9},{9,8},{10,11... | collective-permute-start | bytes 1572872 | tf_op jit(solution)/shard_map/ppermute | solution.py:760
  78.5 13.9 %collective-permute-start.17 = (bf16[128,1280]{1,0:T(8,128)(2,1)S(1)}, bf16[128,1280]{1,0:T(8,128)(2,1)S(1)}, u32[]{:S(2)}, u32[]{:S(2)}) collective-permute-start(bf16[128,1280]{1,0:T(8,128)(2,1)S(1)} %get-tuple-element.151.refs_0_.refs_8_), channel_id=1, source_target_pairs={{0,1},{1,0},{2,3},{3,2},{4,5},{5,4},{6,7},{7,6},{8,9},{9,8},{10,11... | collective-permute-start | bytes 983048 | tf_op jit(solution)/shard_map/ppermute | solution.py:760
  79.9 19.8 %collective-permute-start.21 = (bf16[544,512]{1,0:T(8,128)(2,1)S(1)}, bf16[544,512]{1,0:T(8,128)(2,1)S(1)}, u32[]{:S(2)}, u32[]{:S(2)}) collective-permute-start(bf16[544,512]{1,0:T(8,128)(2,1)S(1)} %get-tuple-element.144), channel_id=1, source_target_pairs={{0,8},{1,9},{2,10},{3,11},{4,12},{5,13},{6,14},{7,15},{8,0},{9,1},... | collective-permute-start | bytes 1671176 | tf_op jit(solution)/shard_map/ppermute | solution.py:760
  82.0 17.1 %collective-permute-start.20 = (bf16[512,512]{1,0:T(8,128)(2,1)S(1)}, bf16[512,512]{1,0:T(8,128)(2,1)S(1)}, u32[]{:S(2)}, u32[]{:S(2)}) collective-permute-start(bf16[512,512]{1,0:T(8,128)(2,1)S(1)} %get-tuple-element.136), channel_id=1, source_target_pairs={{0,4},{1,5},{2,6},{3,7},{4,0},{5,1},{6,2},{7,3},{8,12},{9,13},{10,... | collective-permute-start | bytes 1572872 | tf_op jit(solution)/shard_map/ppermute | solution.py:760
  93.0 12.1 %collective-permute-start.22 = (bf16[384,512]{1,0:T(8,128)(2,1)S(1)}, bf16[384,512]{1,0:T(8,128)(2,1)S(1)}, u32[]{:S(2)}, u32[]{:S(2)}) collective-permute-start(bf16[384,512]{1,0:T(8,128)(2,1)S(1)} %get-tuple-element.147), channel_id=1, source_target_pairs={{0,4},{1,5},{2,6},{3,7},{4,0},{5,1},{6,2},{7,3},{8,12},{9,13},{10,... | collective-permute-start | bytes 1179656 | tf_op jit(solution)/shard_map/ppermute | solution.py:760
  99.2 12.0 %collective-permute-start.25 = (bf16[256,512]{1,0:T(8,128)(2,1)S(1)}, bf16[256,512]{1,0:T(8,128)(2,1)S(1)}, u32[]{:S(2)}, u32[]{:S(2)}) collective-permute-start(bf16[256,512]{1,0:T(8,128)(2,1)S(1)} %get-tuple-element.160), channel_id=1, source_target_pairs={{0,8},{1,9},{2,10},{3,11},{4,12},{5,13},{6,14},{7,15},{8,0},{9,1},... | collective-permute-start | bytes 786440 | tf_op jit(solution)/shard_map/ppermute | solution.py:760
  105.9 12.1 %collective-permute-start.29 = (bf16[256,512]{1,0:T(8,128)(2,1)S(1)}, bf16[256,512]{1,0:T(8,128)(2,1)S(1)}, u32[]{:S(2)}, u32[]{:S(2)}) collective-permute-start(bf16[256,512]{1,0:T(8,128)(2,1)S(1)} %pad_maximum_fusion), channel_id=1, source_target_pairs={{0,2},{1,3},{2,0},{3,1},{4,6},{5,7},{6,4},{7,5},{8,10},{9,11},{10,... | collective-permute-start | bytes 786440 | tf_op jit(solution)/shard_map/ppermute | solution.py:760
  105.9 12.0 %collective-permute-start.27 = (bf16[192,512]{1,0:T(8,128)(2,1)S(1)}, bf16[192,512]{1,0:T(8,128)(2,1)S(1)}, u32[]{:S(2)}, u32[]{:S(2)}) collective-permute-start(bf16[192,512]{1,0:T(8,128)(2,1)S(1)} %get-tuple-element.164), channel_id=1, source_target_pairs={{0,8},{1,9},{2,10},{3,11},{4,12},{5,13},{6,14},{7,15},{8,0},{9,1},... | collective-permute-start | bytes 589832 | tf_op jit(solution)/shard_map/ppermute | solution.py:760
  111.3 34.8 %collective-permute-start.31 = (bf16[272,512]{1,0:T(8,128)(2,1)S(1)}, bf16[272,512]{1,0:T(8,128)(2,1)S(1)}, u32[]{:S(2)}, u32[]{:S(2)}) collective-permute-start(bf16[272,512]{1,0:T(8,128)(2,1)S(1)} %add_body.9.keep_ref), channel_id=1, source_target_pairs={{0,16},{1,17},{2,18},{3,19},{4,20},{5,21},{6,22},{7,23},{8,24},{9,... | collective-permute-start | bytes 835592 | tf_op jit(solution)/shard_map/ppermute | solution.py:760
  114.0 32.0 %collective-permute-start.30 = (bf16[256,512]{1,0:T(8,128)(2,1)S(1)}, bf16[256,512]{1,0:T(8,128)(2,1)S(1)}, u32[]{:S(2)}, u32[]{:S(2)}) collective-permute-start(bf16[256,512]{1,0:T(8,128)(2,1)S(1)} %add_body.8.keep_ref), channel_id=1, source_target_pairs={{0,16},{1,17},{2,18},{3,19},{4,20},{5,21},{6,22},{7,23},{8,24},{9,... | collective-permute-start | bytes 786440 | tf_op jit(solution)/shard_map/ppermute | solution.py:760
  119.8 30.4 %collective-permute-start.34 = (bf16[128,1024]{1,0:T(8,128)(2,1)S(1)}, bf16[128,1024]{1,0:T(8,128)(2,1)S(1)}, u32[]{:S(2)}, u32[]{:S(2)}) collective-permute-start(bf16[128,1024]{1,0:T(8,128)(2,1)S(1)} %get-tuple-element.180), channel_id=1, source_target_pairs={{0,1},{1,0},{2,3},{3,2},{4,5},{5,4},{6,7},{7,6},{8,9},{9,8},{10,11... | collective-permute-start | bytes 786440 | tf_op jit(solution)/shard_map/ppermute | solution.py:760
  119.9 28.9 %collective-permute-start.32 = (bf16[192,512]{1,0:T(8,128)(2,1)S(1)}, bf16[192,512]{1,0:T(8,128)(2,1)S(1)}, u32[]{:S(2)}, u32[]{:S(2)}) collective-permute-start(bf16[192,512]{1,0:T(8,128)(2,1)S(1)} %add_body.10.keep_ref), channel_id=1, source_target_pairs={{0,16},{1,17},{2,18},{3,19},{4,20},{5,21},{6,22},{7,23},{8,24},{9,... | collective-permute-start | bytes 589832 | tf_op jit(solution)/shard_map/ppermute | solution.py:760
  120.6 29.7 %collective-permute-start.33 = (bf16[128,512]{1,0:T(8,128)(2,1)S(1)}, bf16[128,512]{1,0:T(8,128)(2,1)S(1)}, u32[]{:S(2)}, u32[]{:S(2)}) collective-permute-start(bf16[128,512]{1,0:T(8,128)(2,1)S(1)} %add_body.11.keep_ref), channel_id=1, source_target_pairs={{0,16},{1,17},{2,18},{3,19},{4,20},{5,21},{6,22},{7,23},{8,24},{9,... | collective-permute-start | bytes 393224 | tf_op jit(solution)/shard_map/ppermute | solution.py:760
  155.9 18.9 %collective-permute-start.41 = (bf16[544,512]{1,0:T(8,128)(2,1)S(1)}, bf16[544,512]{1,0:T(8,128)(2,1)S(1)}, u32[]{:S(2)}, u32[]{:S(2)}) collective-permute-start(bf16[544,512]{1,0:T(8,128)(2,1)S(1)} %constant_dynamic-update-slice_fusion.2.refs_0_), channel_id=1, source_target_pairs={{0,8},{1,9},{2,10},{3,11},{4,12},{5,13},{6,14},{7,15},{8,0},{9,1},... | collective-permute-start | bytes 1671176 | tf_op jit(solution)/shard_map/ppermute | solution.py:760
  155.9 18.7 %collective-permute-start.37 = (bf16[192,512]{1,0:T(8,128)(2,1)S(1)}, bf16[192,512]{1,0:T(8,128)(2,1)S(1)}, u32[]{:S(2)}, u32[]{:S(2)}) collective-permute-start(bf16[192,512]{1,0:T(8,128)(2,1)S(1)} %add_body.14), channel_id=1, source_target_pairs={{0,8},{1,9},{2,10},{3,11},{4,12},{5,13},{6,14},{7,15},{8,0},{9,1},... | collective-permute-start | bytes 589832 | tf_op jit(solution)/shard_map/ppermute | solution.py:760
  158.0 16.8 %collective-permute-start.42 = (bf16[512,512]{1,0:T(8,128)(2,1)S(1)}, bf16[512,512]{1,0:T(8,128)(2,1)S(1)}, u32[]{:S(2)}, u32[]{:S(2)}) collective-permute-start(bf16[512,512]{1,0:T(8,128)(2,1)S(1)} %constant_dynamic-update-slice_fusion.refs_0_), channel_id=1, source_target_pairs={{0,4},{1,5},{2,6},{3,7},{4,0},{5,1},{6,2},{7,3},{8,12},{9,13},{10,... | collective-permute-start | bytes 1572872 | tf_op jit(solution)/shard_map/ppermute | solution.py:760
  159.5 15.2 %collective-permute-start.38 = (bf16[128,512]{1,0:T(8,128)(2,1)S(1)}, bf16[128,512]{1,0:T(8,128)(2,1)S(1)}, u32[]{:S(2)}, u32[]{:S(2)}) collective-permute-start(bf16[128,512]{1,0:T(8,128)(2,1)S(1)} %add_body.15), channel_id=1, source_target_pairs={{0,4},{1,5},{2,6},{3,7},{4,0},{5,1},{6,2},{7,3},{8,12},{9,13},{10,... | collective-permute-start | bytes 393224 | tf_op jit(solution)/shard_map/ppermute | solution.py:760
  160.0 17.0 %collective-permute-start.43 = (bf16[512,512]{1,0:T(8,128)(2,1)S(1)}, bf16[512,512]{1,0:T(8,128)(2,1)S(1)}, u32[]{:S(2)}, u32[]{:S(2)}) collective-permute-start(bf16[512,512]{1,0:T(8,128)(2,1)S(1)} %constant_dynamic-update-slice_fusion.refs_0_), channel_id=1, source_target_pairs={{0,2},{1,3},{2,0},{3,1},{4,6},{5,7},{6,4},{7,5},{8,10},{9,11},{10,... | collective-permute-start | bytes 1572872 | tf_op jit(solution)/shard_map/ppermute | solution.py:760
  (43 other events, 366.8 us)

commit v6 on v5

--- a/solution.py
+++ b/solution.py
@@ -9,7 +9,7 @@
 AXES = ("replica", "fsdp")
 LANES = 128
 FAR = -1e30
-ORDER = "012n3x0123k0123tb0123p012301os23"
+ORDER = "01012n3x01k2301t2301b2301p23os23"
 
 
 def owner_place():

time: 195 us -> 186 us (0.954)
  waiting for transfers between devices: 109 us -> 98 us
  starting transfers between devices: 40.3 us -> 42.4 us
    ppermute x51, waiting for transfers between devices: 109 us -> 98 us  [swap(): return lax.ppermute(value, AXES, pairs)]
    ppermute x51, starting transfers between devices: 40.3 us -> 42.4 us  [swap(): return lax.ppermute(value, AXES, pairs)]
  transfers between devices with their start and end apart: 51 -> 51, of which waited for: 21 -> 22; matrix products, arithmetic and copies ran while one was open for 3% -> 3% of each run, Pallas kernels for 13% -> 13%
where the time goes in v6:
time: 186 us
  waiting for transfers between devices  98 us (53%)
  starting transfers between devices  42.4 us (23%)
  Pallas kernels  32.3 us (17%)
  local copies, waits for them, and re-layouts  10.6 us (6%)
    ppermute x51, waiting for transfers between devices, swap(): return lax.ppermute(value, AXES, pairs)  98 us
    ppermute x51, starting transfers between devices, swap(): return lax.ppermute(value, AXES, pairs)  42.4 us
    pallas_call x28, Pallas kernels, call(): pl.pallas_call(body, out_shape=out_shape, in_specs=in_specs, out_specs=[v...  24.6 us
    pallas_call x2, Pallas kernels, assemble(): pl.pallas_call(body, grid=(outs[0].shape[1] // block,), out_shape=outs, i...  7.65 us
    unnamed x36, local copies, waits for them, and re-layouts  6.85 us
  transfers between devices with their start and end apart: 51, of which 22 were waited for; matrix products, arithmetic and copies ran while one was open for 3% of the time, Pallas kernels for 13%

profile of v6, /device:TPU:0, one launch (start us, length us, event | category | flops | bytes accessed | tf_op | source)
XLA Modules:
  0.0 186.1 jit_solution(8483578677139255093)
XLA Ops:
  0.6 3.0 %collective-permute-start.1 = (bf16[128,1024]{1,0:T(8,128)(2,1)}, bf16[128,1024]{1,0:T(8,128)(2,1)S(1)}, u32[]{:S(2)}, u32[]{:S(2)}) collective-permute-start(bf16[128,1024]{1,0:T(8,128)(2,1)} %cotangent_ref.3), channel_id=1, source_target_pairs={{0,1},{1,0},{2,3},{3,2},{4,5},{5,4},{6,7},{7,6},{8,9},{9,8},{10,11... | collective-permute-start | bytes 786440 | tf_op jit(solution)/shard_map/ppermute | solution.py:760
  4.4 6.6 %collective-permute-done.1.cotangent_ref.refs_5_ = bf16[128,1024]{1,0:T(8,128)(2,1)S(1)} collective-permute-done((bf16[128,1024]{1,0:T(8,128)(2,1)}, bf16[128,1024]{1,0:T(8,128)(2,1)S(1)}, u32[]{:S(2)}, u32[]{:S(2)}) %collective-permute-start.1) | collective-permute-done | bytes 262176 | tf_op jit(solution)/shard_map/ppermute | solution.py:760
  11.0 4.8 %collective-permute-done.refs_0_.refs_1_ = bf16[128,1024]{1,0:T(8,128)(2,1)S(1)} collective-permute-done((bf16[128,1024]{1,0:T(8,128)(2,1)}, bf16[128,1024]{1,0:T(8,128)(2,1)S(1)}, u32[]{:S(2)}, u32[]{:S(2)}) %collective-permute-start) | collective-permute-done | bytes 262176 | tf_op jit(solution)/shard_map/ppermute | solution.py:760
  28.4 9.7 %collective-permute-done.4.peer_ref = f32[8,1152]{1,0:T(8,128)S(1)} collective-permute-done((f32[8,1152]{1,0:T(8,128)S(1)}, f32[8,1152]{1,0:T(8,128)S(1)}, u32[]{:S(2)}, u32[]{:S(2)}) %collective-permute-start.4) | collective-permute-done | bytes 36896 | tf_op jit(solution)/shard_map/ppermute | solution.py:760
  42.8 2.3 %project_own_body.1 = (bf16[128,512]{1,0:T(8,128)(2,1)S(1)}, f32[128,2432]{1,0:T(8,128)S(1)}, f32[128,2048]{1,0:T(8,128)S(1)}, f32[128,1024]{1,0:T(8,128)S(1)}) custom-call(bf16[128,1024]{1,0:T(8,128)(2,1)S(1)} %copy-done.5, bf16[128,1024]{1,0:T(8,128)(2,1)S(1)} %copy-done.6, f32[1,512]{1,0:T(1,128)S(1)} %bitcast.18, bf16[4384,512]{1,0:T(8,128)(2,1)S(1)} %bitcast.13, ...), custom_call_target="tpu_custom_call" | custom-call | flops 1 | bytes 1 | tf_op jit(solution)/shard_map/project_own_body/pallas_call | solution.py:359
  45.4 3.2 %forward_body.1 = (f32[128,2304]{1,0:T(8,128)S(1)}, f32[128,2304]{1,0:T(8,128)S(1)}, f32[128,2048]{1,0:T(8,128)S(1)}, f32[3,128,32]{2,1,0:T(8,128)S(1)}) custom-call(s32[1,2]{1,0:T(1,128)S(1)} %copy-done.8, f32[128,2432]{1,0:T(8,128)S(1)} %get-tuple-element.109.own_ref, bf16[128,2048]{1,0:T(8,128)(2,1)} %collective-permute-done.2.wide_ref, ...), custom_call_target="tpu_custom_call" | custom-call | flops 1 | bytes 1 | tf_op jit(solution)/shard_map/forward_body/pallas_call | solution.py:359
  48.6 7.7 %collective-permute-done.5.got_ref = bf16[128,3072]{1,0:T(8,128)(2,1)S(1)} collective-permute-done((bf16[128,3072]{1,0:T(8,128)(2,1)}, bf16[128,3072]{1,0:T(8,128)(2,1)S(1)}, u32[]{:S(2)}, u32[]{:S(2)}) %collective-permute-start.5) | collective-permute-done | bytes 786464 | tf_op jit(solution)/shard_map/ppermute | solution.py:760
  60.4 6.8 %backward_body.1 = (bf16[128,1280]{1,0:T(8,128)(2,1)S(1)}, bf16[128,1280]{1,0:T(8,128)(2,1)S(1)}, f32[8,1152]{1,0:T(8,128)S(1)}, f32[8,1152]{1,0:T(8,128)S(1)}) custom-call(s32[1,2]{1,0:T(1,128)S(1)} %copy-done.8, f32[128,2048]{1,0:T(8,128)S(1)} %get-tuple-element.129.dmixed_ref, f32[128,2304]{1,0:T(8,128)S(1)} %get-tuple-element.130.xbc_ref, ...), custom_call_target="tpu_custom_call" | custom-call | flops 1 | bytes 1 | tf_op jit(solution)/shard_map/backward_body/pallas_call | solution.py:359
  69.7 4.3 %collective-permute-done.13.refs_1_.refs_5_ = bf16[256,1024]{1,0:T(8,128)(2,1)S(1)} collective-permute-done((bf16[256,1024]{1,0:T(8,128)(2,1)S(1)}, bf16[256,1024]{1,0:T(8,128)(2,1)S(1)}, u32[]{:S(2)}, u32[]{:S(2)}) %collective-permute-start.13) | collective-permute-done | bytes 524320 | tf_op jit(solution)/shard_map/ppermute | solution.py:760
  75.2 3.2 %collective-permute-done.16.refs_9_ = f32[8,1152]{1,0:T(8,128)S(1)} collective-permute-done((f32[8,1152]{1,0:T(8,128)S(1)}, f32[8,1152]{1,0:T(8,128)S(1)}, u32[]{:S(2)}, u32[]{:S(2)}) %collective-permute-start.16) | collective-permute-done | bytes 36896 | tf_op jit(solution)/shard_map/ppermute | solution.py:760
  83.8 8.7 %collective-permute-done.17.refs_1_ = bf16[512,512]{1,0:T(8,128)(2,1)S(1)} collective-permute-done((bf16[512,512]{1,0:T(8,128)(2,1)S(1)}, bf16[512,512]{1,0:T(8,128)(2,1)S(1)}, u32[]{:S(2)}, u32[]{:S(2)}) %collective-permute-start.17) | collective-permute-done | bytes 524320 | tf_op jit(solution)/shard_map/ppermute | solution.py:760
  94.9 3.8 %collective-permute-done.19.refs_1_.refs_9_ = bf16[128,1280]{1,0:T(8,128)(2,1)S(1)} collective-permute-done((bf16[128,1280]{1,0:T(8,128)(2,1)S(1)}, bf16[128,1280]{1,0:T(8,128)(2,1)S(1)}, u32[]{:S(2)}, u32[]{:S(2)}) %collective-permute-start.19) | collective-permute-done | bytes 327712 | tf_op jit(solution)/shard_map/ppermute | solution.py:760
  106.8 3.0 %collective-permute-done.24.far_ref = bf16[256,512]{1,0:T(8,128)(2,1)S(1)} collective-permute-done((bf16[256,512]{1,0:T(8,128)(2,1)S(1)}, bf16[256,512]{1,0:T(8,128)(2,1)S(1)}, u32[]{:S(2)}, u32[]{:S(2)}) %collective-permute-start.24) | collective-permute-done | bytes 262176 | tf_op jit(solution)/shard_map/ppermute | solution.py:760
  109.9 3.0 %collective-permute-done.25.refs_1_ = bf16[384,512]{1,0:T(8,128)(2,1)S(1)} collective-permute-done((bf16[384,512]{1,0:T(8,128)(2,1)S(1)}, bf16[384,512]{1,0:T(8,128)(2,1)S(1)}, u32[]{:S(2)}, u32[]{:S(2)}) %collective-permute-start.25) | collective-permute-done | bytes 393248 | tf_op jit(solution)/shard_map/ppermute | solution.py:760
  113.6 3.5 %collective-permute-done.26.refs_1_ = bf16[256,512]{1,0:T(8,128)(2,1)S(1)} collective-permute-done((bf16[256,512]{1,0:T(8,128)(2,1)S(1)}, bf16[256,512]{1,0:T(8,128)(2,1)S(1)}, u32[]{:S(2)}, u32[]{:S(2)}) %collective-permute-start.26) | collective-permute-done | bytes 262176 | tf_op jit(solution)/shard_map/ppermute | solution.py:760
  117.1 8.5 %collective-permute-done.27.got_ref = bf16[256,512]{1,0:T(8,128)(2,1)S(1)} collective-permute-done((bf16[256,512]{1,0:T(8,128)(2,1)S(1)}, bf16[256,512]{1,0:T(8,128)(2,1)S(1)}, u32[]{:S(2)}, u32[]{:S(2)}) %collective-permute-start.27) | collective-permute-done | bytes 262176 | tf_op jit(solution)/shard_map/ppermute | solution.py:760
  126.8 3.2 %collective-permute-done.28.got_ref = bf16[272,512]{1,0:T(8,128)(2,1)S(1)} collective-permute-done((bf16[272,512]{1,0:T(8,128)(2,1)S(1)}, bf16[272,512]{1,0:T(8,128)(2,1)S(1)}, u32[]{:S(2)}, u32[]{:S(2)}) %collective-permute-start.28) | collective-permute-done | bytes 278560 | tf_op jit(solution)/shard_map/ppermute | solution.py:760
  134.3 2.9 %collective-permute-done.33 = bf16[272,512]{1,0:T(8,128)(2,1)S(1)} collective-permute-done((bf16[272,512]{1,0:T(8,128)(2,1)S(1)}, bf16[272,512]{1,0:T(8,128)(2,1)S(1)}, u32[]{:S(2)}, u32[]{:S(2)}) %collective-permute-start.33) | collective-permute-done | bytes 278560 | tf_op jit(solution)/shard_map/ppermute | solution.py:760
  141.3 3.0 %collective-permute-start.36 = (bf16[192,512]{1,0:T(8,128)(2,1)S(1)}, bf16[192,512]{1,0:T(8,128)(2,1)S(1)}, u32[]{:S(2)}, u32[]{:S(2)}) collective-permute-start(bf16[192,512]{1,0:T(8,128)(2,1)S(1)} %add_body.12.keep_ref), channel_id=1, source_target_pairs={{0,16},{1,17},{2,18},{3,19},{4,20},{5,21},{6,22},{7,23},{8,24},{9,... | collective-permute-start | bytes 589832 | tf_op jit(solution)/shard_map/ppermute | solution.py:760
  144.4 11.0 %collective-permute-done.36.got_ref = bf16[192,512]{1,0:T(8,128)(2,1)S(1)} collective-permute-done((bf16[192,512]{1,0:T(8,128)(2,1)S(1)}, bf16[192,512]{1,0:T(8,128)(2,1)S(1)}, u32[]{:S(2)}, u32[]{:S(2)}) %collective-permute-start.36) | collective-permute-done | bytes 196640 | tf_op jit(solution)/shard_map/ppermute | solution.py:760
  160.5 2.8 %collective-permute-done.39 = bf16[192,512]{1,0:T(8,128)(2,1)S(1)} collective-permute-done((bf16[192,512]{1,0:T(8,128)(2,1)S(1)}, bf16[192,512]{1,0:T(8,128)(2,1)S(1)}, u32[]{:S(2)}, u32[]{:S(2)}) %collective-permute-start.39) | collective-permute-done | bytes 196640 | tf_op jit(solution)/shard_map/ppermute | solution.py:760
  164.8 3.4 %collective-permute-done.40 = bf16[128,512]{1,0:T(8,128)(2,1)S(1)} collective-permute-done((bf16[128,512]{1,0:T(8,128)(2,1)S(1)}, bf16[128,512]{1,0:T(8,128)(2,1)S(1)}, u32[]{:S(2)}, u32[]{:S(2)}) %collective-permute-start.40) | collective-permute-done | bytes 131104 | tf_op jit(solution)/shard_map/ppermute | solution.py:760
  171.9 2.7 %out_weight_lanes.1 = f32[1024,1024]{1,0:T(8,128)} custom-call(bf16[512,512]{1,0:T(8,128)(2,1)S(1)} %constant_dynamic-update-slice_fusion.refs_0_, bf16[512,512]{1,0:T(8,128)(2,1)S(1)} %collective-permute-done.35.refs_1_, bf16[512,512]{1,0:T(8,128)(2,1)S(1)} %collective-permute-done.43.refs_2_, bf16[512,512]{1,0:T(8,128)(2,1)S(1)} %collective-permute-done.44.refs_3_), custom_call_target="tpu_custom_call" | custom-call | flops 1 | bytes 1 | tf_op jit(solution)/shard_map/out_weight_lanes/pallas_call | solution.py:738
  180.6 4.9 %in_weight_rows.1 = (f32[4384,512]{1,0:T(8,128)}, f32[8,512]{1,0:T(8,128)S(1)}) custom-call(bf16[544,512]{1,0:T(8,128)(2,1)S(1)} %constant_dynamic-update-slice_fusion.2.refs_0_, bf16[544,512]{1,0:T(8,128)(2,1)S(1)} %collective-permute-done.34.refs_1_, bf16[544,512]{1,0:T(8,128)(2,1)S(1)} %collective-permute-done.45.refs_2_, ...), custom_call_target="tpu_custom_call" | custom-call | flops 1 | bytes 1 | tf_op jit(solution)/shard_map/in_weight_rows/pallas_call | solution.py:738
  (171 shorter events, 69.0 us)
Async XLA Ops:
  19.8 18.3 %collective-permute-start.3 = (f32[128,384]{1,0:T(8,128)}, f32[128,384]{1,0:T(8,128)S(1)}, u32[]{:S(2)}, u32[]{:S(2)}) collective-permute-start(f32[128,384]{1,0:T(8,128)} %get-tuple-element.107), channel_id=1, source_target_pairs={{0,1},{1,0},{2,3},{3,2},{4,5},{5,4},{6,7},{7,6},{8,9},{9,8},{10,11... | collective-permute-start | bytes 589832 | tf_op jit(solution)/shard_map/ppermute | solution.py:760
  21.5 16.6 %collective-permute-start.2 = (bf16[128,2048]{1,0:T(8,128)(2,1)}, bf16[128,2048]{1,0:T(8,128)(2,1)}, u32[]{:S(2)}, u32[]{:S(2)}) collective-permute-start(bf16[128,2048]{1,0:T(8,128)(2,1)} %get-tuple-element.110), channel_id=1, source_target_pairs={{0,1},{1,0},{2,3},{3,2},{4,5},{5,4},{6,7},{7,6},{8,9},{9,8},{10,11... | collective-permute-start | bytes 1572872 | tf_op jit(solution)/shard_map/ppermute | solution.py:760
  38.1 18.1 %collective-permute-start.5 = (bf16[128,3072]{1,0:T(8,128)(2,1)}, bf16[128,3072]{1,0:T(8,128)(2,1)S(1)}, u32[]{:S(2)}, u32[]{:S(2)}) collective-permute-start(bf16[128,3072]{1,0:T(8,128)(2,1)} %copy-done.7), channel_id=1, source_target_pairs={{0,1},{1,0},{2,3},{3,2},{4,5},{5,4},{6,7},{7,6},{8,9},{9,8},{10,11... | collective-permute-start | bytes 2359304 | tf_op jit(solution)/shard_map/ppermute | solution.py:760
  40.0 18.0 %collective-permute-start.8 = (bf16[128,1024]{1,0:T(8,128)(2,1)S(1)}, bf16[128,1024]{1,0:T(8,128)(2,1)S(1)}, u32[]{:S(2)}, u32[]{:S(2)}) collective-permute-start(bf16[128,1024]{1,0:T(8,128)(2,1)S(1)} %copy-done.6), channel_id=1, source_target_pairs={{0,2},{1,3},{2,0},{3,1},{4,6},{5,7},{6,4},{7,5},{8,10},{9,11},{10,... | collective-permute-start | bytes 786440 | tf_op jit(solution)/shard_map/ppermute | solution.py:760
  40.0 18.0 %collective-permute-start.9 = (bf16[128,1024]{1,0:T(8,128)(2,1)S(1)}, bf16[128,1024]{1,0:T(8,128)(2,1)S(1)}, u32[]{:S(2)}, u32[]{:S(2)}) collective-permute-start(bf16[128,1024]{1,0:T(8,128)(2,1)S(1)} %collective-permute-done.1.cotangent_ref.refs_5_), channel_id=1, source_target_pairs={{0,2},{1,3},{2,0},{3,1},{4,6},{5,7},{6,4},{7,5},{8,10},{9,11},{10,... | collective-permute-start | bytes 786440 | tf_op jit(solution)/shard_map/ppermute | solution.py:760
  59.4 14.5 %collective-permute-start.13 = (bf16[256,1024]{1,0:T(8,128)(2,1)S(1)}, bf16[256,1024]{1,0:T(8,128)(2,1)S(1)}, u32[]{:S(2)}, u32[]{:S(2)}) collective-permute-start(bf16[256,1024]{1,0:T(8,128)(2,1)S(1)} %get-tuple-element.138), channel_id=1, source_target_pairs={{0,1},{1,0},{2,3},{3,2},{4,5},{5,4},{6,7},{7,6},{8,9},{9,8},{10,11... | collective-permute-start | bytes 1572872 | tf_op jit(solution)/shard_map/ppermute | solution.py:760
  79.2 14.7 %collective-permute-start.18 = (bf16[544,512]{1,0:T(8,128)(2,1)S(1)}, bf16[544,512]{1,0:T(8,128)(2,1)S(1)}, u32[]{:S(2)}, u32[]{:S(2)}) collective-permute-start(bf16[544,512]{1,0:T(8,128)(2,1)S(1)} %get-tuple-element.146), channel_id=1, source_target_pairs={{0,8},{1,9},{2,10},{3,11},{4,12},{5,13},{6,14},{7,15},{8,0},{9,1},... | collective-permute-start | bytes 1671176 | tf_op jit(solution)/shard_map/ppermute | solution.py:760
  80.1 12.4 %collective-permute-start.17 = (bf16[512,512]{1,0:T(8,128)(2,1)S(1)}, bf16[512,512]{1,0:T(8,128)(2,1)S(1)}, u32[]{:S(2)}, u32[]{:S(2)}) collective-permute-start(bf16[512,512]{1,0:T(8,128)(2,1)S(1)} %get-tuple-element.136), channel_id=1, source_target_pairs={{0,4},{1,5},{2,6},{3,7},{4,0},{5,1},{6,2},{7,3},{8,12},{9,13},{10,... | collective-permute-start | bytes 1572872 | tf_op jit(solution)/shard_map/ppermute | solution.py:760
  81.6 13.3 %collective-permute-start.21 = (bf16[128,1280]{1,0:T(8,128)(2,1)S(1)}, bf16[128,1280]{1,0:T(8,128)(2,1)S(1)}, u32[]{:S(2)}, u32[]{:S(2)}) collective-permute-start(bf16[128,1280]{1,0:T(8,128)(2,1)S(1)} %get-tuple-element.154), channel_id=1, source_target_pairs={{0,3},{1,2},{2,1},{3,0},{4,7},{5,6},{6,5},{7,4},{8,11},{9,10},{10,... | collective-permute-start | bytes 983048 | tf_op jit(solution)/shard_map/ppermute | solution.py:760
  81.6 13.3 %collective-permute-start.20 = (bf16[128,1280]{1,0:T(8,128)(2,1)S(1)}, bf16[128,1280]{1,0:T(8,128)(2,1)S(1)}, u32[]{:S(2)}, u32[]{:S(2)}) collective-permute-start(bf16[128,1280]{1,0:T(8,128)(2,1)S(1)} %get-tuple-element.154), channel_id=1, source_target_pairs={{0,2},{1,3},{2,0},{3,1},{4,6},{5,7},{6,4},{7,5},{8,10},{9,11},{10,... | collective-permute-start | bytes 983048 | tf_op jit(solution)/shard_map/ppermute | solution.py:760
  83.2 15.4 %collective-permute-start.19 = (bf16[128,1280]{1,0:T(8,128)(2,1)S(1)}, bf16[128,1280]{1,0:T(8,128)(2,1)S(1)}, u32[]{:S(2)}, u32[]{:S(2)}) collective-permute-start(bf16[128,1280]{1,0:T(8,128)(2,1)S(1)} %get-tuple-element.159.refs_0_.refs_8_), channel_id=1, source_target_pairs={{0,1},{1,0},{2,3},{3,2},{4,5},{5,4},{6,7},{7,6},{8,9},{9,8},{10,11... | collective-permute-start | bytes 983048 | tf_op jit(solution)/shard_map/ppermute | solution.py:760
  102.1 14.9 %collective-permute-start.26 = (bf16[256,512]{1,0:T(8,128)(2,1)S(1)}, bf16[256,512]{1,0:T(8,128)(2,1)S(1)}, u32[]{:S(2)}, u32[]{:S(2)}) collective-permute-start(bf16[256,512]{1,0:T(8,128)(2,1)S(1)} %get-tuple-element.160), channel_id=1, source_target_pairs={{0,8},{1,9},{2,10},{3,11},{4,12},{5,13},{6,14},{7,15},{8,0},{9,1},... | collective-permute-start | bytes 786440 | tf_op jit(solution)/shard_map/ppermute | solution.py:760
  103.6 21.9 %collective-permute-start.27 = (bf16[256,512]{1,0:T(8,128)(2,1)S(1)}, bf16[256,512]{1,0:T(8,128)(2,1)S(1)}, u32[]{:S(2)}, u32[]{:S(2)}) collective-permute-start(bf16[256,512]{1,0:T(8,128)(2,1)S(1)} %add_body.8.keep_ref), channel_id=1, source_target_pairs={{0,16},{1,17},{2,18},{3,19},{4,20},{5,21},{6,22},{7,23},{8,24},{9,... | collective-permute-start | bytes 786440 | tf_op jit(solution)/shard_map/ppermute | solution.py:760
  105.3 24.7 %collective-permute-start.28 = (bf16[272,512]{1,0:T(8,128)(2,1)S(1)}, bf16[272,512]{1,0:T(8,128)(2,1)S(1)}, u32[]{:S(2)}, u32[]{:S(2)}) collective-permute-start(bf16[272,512]{1,0:T(8,128)(2,1)S(1)} %add_body.9.keep_ref), channel_id=1, source_target_pairs={{0,16},{1,17},{2,18},{3,19},{4,20},{5,21},{6,22},{7,23},{8,24},{9,... | collective-permute-start | bytes 835592 | tf_op jit(solution)/shard_map/ppermute | solution.py:760
  109.8 21.1 %collective-permute-start.29 = (bf16[256,512]{1,0:T(8,128)(2,1)S(1)}, bf16[256,512]{1,0:T(8,128)(2,1)S(1)}, u32[]{:S(2)}, u32[]{:S(2)}) collective-permute-start(bf16[256,512]{1,0:T(8,128)(2,1)S(1)} %pad_maximum_fusion), channel_id=1, source_target_pairs={{0,2},{1,3},{2,0},{3,1},{4,6},{5,7},{6,4},{7,5},{8,10},{9,11},{10,... | collective-permute-start | bytes 786440 | tf_op jit(solution)/shard_map/ppermute | solution.py:760
  113.0 19.1 %collective-permute-start.30 = (bf16[192,512]{1,0:T(8,128)(2,1)S(1)}, bf16[192,512]{1,0:T(8,128)(2,1)S(1)}, u32[]{:S(2)}, u32[]{:S(2)}) collective-permute-start(bf16[192,512]{1,0:T(8,128)(2,1)S(1)} %get-tuple-element.169), channel_id=1, source_target_pairs={{0,8},{1,9},{2,10},{3,11},{4,12},{5,13},{6,14},{7,15},{8,0},{9,1},... | collective-permute-start | bytes 589832 | tf_op jit(solution)/shard_map/ppermute | solution.py:760
  137.3 21.8 %collective-permute-start.34 = (bf16[544,512]{1,0:T(8,128)(2,1)S(1)}, bf16[544,512]{1,0:T(8,128)(2,1)S(1)}, u32[]{:S(2)}, u32[]{:S(2)}) collective-permute-start(bf16[544,512]{1,0:T(8,128)(2,1)S(1)} %constant_dynamic-update-slice_fusion.2.refs_0_), channel_id=1, source_target_pairs={{0,8},{1,9},{2,10},{3,11},{4,12},{5,13},{6,14},{7,15},{8,0},{9,1},... | collective-permute-start | bytes 1671176 | tf_op jit(solution)/shard_map/ppermute | solution.py:760
  138.7 20.3 %collective-permute-start.35 = (bf16[512,512]{1,0:T(8,128)(2,1)S(1)}, bf16[512,512]{1,0:T(8,128)(2,1)S(1)}, u32[]{:S(2)}, u32[]{:S(2)}) collective-permute-start(bf16[512,512]{1,0:T(8,128)(2,1)S(1)} %constant_dynamic-update-slice_fusion.refs_0_), channel_id=1, source_target_pairs={{0,4},{1,5},{2,6},{3,7},{4,0},{5,1},{6,2},{7,3},{8,12},{9,13},{10,... | collective-permute-start | bytes 1572872 | tf_op jit(solution)/shard_map/ppermute | solution.py:760
  140.0 19.6 %collective-permute-start.38 = (bf16[128,1024]{1,0:T(8,128)(2,1)S(1)}, bf16[128,1024]{1,0:T(8,128)(2,1)S(1)}, u32[]{:S(2)}, u32[]{:S(2)}) collective-permute-start(bf16[128,1024]{1,0:T(8,128)(2,1)S(1)} %get-tuple-element.184), channel_id=1, source_target_pairs={{0,1},{1,0},{2,3},{3,2},{4,5},{5,4},{6,7},{7,6},{8,9},{9,8},{10,11... | collective-permute-start | bytes 786440 | tf_op jit(solution)/shard_map/ppermute | solution.py:760
  141.3 14.1 %collective-permute-start.36 = (bf16[192,512]{1,0:T(8,128)(2,1)S(1)}, bf16[192,512]{1,0:T(8,128)(2,1)S(1)}, u32[]{:S(2)}, u32[]{:S(2)}) collective-permute-start(bf16[192,512]{1,0:T(8,128)(2,1)S(1)} %add_body.12.keep_ref), channel_id=1, source_target_pairs={{0,16},{1,17},{2,18},{3,19},{4,20},{5,21},{6,22},{7,23},{8,24},{9,... | collective-permute-start | bytes 589832 | tf_op jit(solution)/shard_map/ppermute | solution.py:760
  144.4 12.5 %collective-permute-start.37 = (bf16[128,512]{1,0:T(8,128)(2,1)S(1)}, bf16[128,512]{1,0:T(8,128)(2,1)S(1)}, u32[]{:S(2)}, u32[]{:S(2)}) collective-permute-start(bf16[128,512]{1,0:T(8,128)(2,1)S(1)} %add_body.13.keep_ref), channel_id=1, source_target_pairs={{0,16},{1,17},{2,18},{3,19},{4,20},{5,21},{6,22},{7,23},{8,24},{9,... | collective-permute-start | bytes 393224 | tf_op jit(solution)/shard_map/ppermute | solution.py:760
  155.4 14.3 %collective-permute-start.43 = (bf16[512,512]{1,0:T(8,128)(2,1)S(1)}, bf16[512,512]{1,0:T(8,128)(2,1)S(1)}, u32[]{:S(2)}, u32[]{:S(2)}) collective-permute-start(bf16[512,512]{1,0:T(8,128)(2,1)S(1)} %constant_dynamic-update-slice_fusion.refs_0_), channel_id=1, source_target_pairs={{0,2},{1,3},{2,0},{3,1},{4,6},{5,7},{6,4},{7,5},{8,10},{9,11},{10,... | collective-permute-start | bytes 1572872 | tf_op jit(solution)/shard_map/ppermute | solution.py:760
  159.0 15.6 %collective-permute-start.45 = (bf16[544,512]{1,0:T(8,128)(2,1)S(1)}, bf16[544,512]{1,0:T(8,128)(2,1)S(1)}, u32[]{:S(2)}, u32[]{:S(2)}) collective-permute-start(bf16[544,512]{1,0:T(8,128)(2,1)S(1)} %constant_dynamic-update-slice_fusion.2.refs_0_), channel_id=1, source_target_pairs={{0,2},{1,3},{2,0},{3,1},{4,6},{5,7},{6,4},{7,5},{8,10},{9,11},{10,... | collective-permute-start | bytes 1671176 | tf_op jit(solution)/shard_map/ppermute | solution.py:760
  159.6 15.2 %collective-permute-start.46 = (bf16[544,512]{1,0:T(8,128)(2,1)S(1)}, bf16[544,512]{1,0:T(8,128)(2,1)S(1)}, u32[]{:S(2)}, u32[]{:S(2)}) collective-permute-start(bf16[544,512]{1,0:T(8,128)(2,1)S(1)} %collective-permute-done.34.refs_1_), channel_id=1, source_target_pairs={{0,2},{1,3},{2,0},{3,1},{4,6},{5,7},{6,4},{7,5},{8,10},{9,11},{10,... | collective-permute-start | bytes 1671176 | tf_op jit(solution)/shard_map/ppermute | solution.py:760
  (43 other events, 364.7 us)

commit v7 on v6

--- a/solution.py
+++ b/solution.py
@@ -9,7 +9,7 @@
 AXES = ("replica", "fsdp")
 LANES = 128
 FAR = -1e30
-ORDER = "01012n3x01k2301t2301b2301p23os23"
+ORDER = "01012n3x01k2301t2301b2301p2os323"
 
 
 def owner_place():

time: 186 us -> 187 us (level)
  waiting for transfers between devices: 98 us -> 101 us
  starting transfers between devices: 42.4 us -> 40.5 us
    ppermute x51, waiting for transfers between devices: 98 us -> 101 us  [swap(): return lax.ppermute(value, AXES, pairs)]
    ppermute x51, starting transfers between devices: 42.4 us -> 40.5 us  [swap(): return lax.ppermute(value, AXES, pairs)]
  transfers between devices with their start and end apart: 51 -> 51, of which waited for: 22 -> 24; matrix products, arithmetic and copies ran while one was open for 3% -> 3% of each run, Pallas kernels for 13% -> 13%
where the time goes in v7:
time: 187 us
  waiting for transfers between devices  101 us (54%)
  starting transfers between devices  40.5 us (22%)
  Pallas kernels  32.3 us (17%)
  local copies, waits for them, and re-layouts  10.6 us (6%)
    ppermute x51, waiting for transfers between devices, swap(): return lax.ppermute(value, AXES, pairs)  101 us
    ppermute x51, starting transfers between devices, swap(): return lax.ppermute(value, AXES, pairs)  40.5 us
    pallas_call x28, Pallas kernels, call(): pl.pallas_call(body, out_shape=out_shape, in_specs=in_specs, out_specs=[v...  24.6 us
    pallas_call x2, Pallas kernels, assemble(): pl.pallas_call(body, grid=(outs[0].shape[1] // block,), out_shape=outs, i...  7.62 us
    unnamed x36, local copies, waits for them, and re-layouts  6.85 us
  transfers between devices with their start and end apart: 51, of which 24 were waited for; matrix products, arithmetic and copies ran while one was open for 3% of the time, Pallas kernels for 13%

profile of v7, /device:TPU:0, one launch (start us, length us, event | category | flops | bytes accessed | tf_op | source)
XLA Modules:
  0.0 186.9 jit_solution(7473219147319104192)
XLA Ops:
  0.6 3.0 %collective-permute-start.1 = (bf16[128,1024]{1,0:T(8,128)(2,1)}, bf16[128,1024]{1,0:T(8,128)(2,1)S(1)}, u32[]{:S(2)}, u32[]{:S(2)}) collective-permute-start(bf16[128,1024]{1,0:T(8,128)(2,1)} %cotangent_ref.3), channel_id=1, source_target_pairs={{0,1},{1,0},{2,3},{3,2},{4,5},{5,4},{6,7},{7,6},{8,9},{9,8},{10,11... | collective-permute-start | bytes 786440 | tf_op jit(solution)/shard_map/ppermute | solution.py:760
  4.4 6.6 %collective-permute-done.1.cotangent_ref.refs_5_ = bf16[128,1024]{1,0:T(8,128)(2,1)S(1)} collective-permute-done((bf16[128,1024]{1,0:T(8,128)(2,1)}, bf16[128,1024]{1,0:T(8,128)(2,1)S(1)}, u32[]{:S(2)}, u32[]{:S(2)}) %collective-permute-start.1) | collective-permute-done | bytes 262176 | tf_op jit(solution)/shard_map/ppermute | solution.py:760
  11.0 4.8 %collective-permute-done.refs_0_.refs_1_ = bf16[128,1024]{1,0:T(8,128)(2,1)S(1)} collective-permute-done((bf16[128,1024]{1,0:T(8,128)(2,1)}, bf16[128,1024]{1,0:T(8,128)(2,1)S(1)}, u32[]{:S(2)}, u32[]{:S(2)}) %collective-permute-start) | collective-permute-done | bytes 262176 | tf_op jit(solution)/shard_map/ppermute | solution.py:760
  28.4 9.7 %collective-permute-done.4.peer_ref = f32[8,1152]{1,0:T(8,128)S(1)} collective-permute-done((f32[8,1152]{1,0:T(8,128)S(1)}, f32[8,1152]{1,0:T(8,128)S(1)}, u32[]{:S(2)}, u32[]{:S(2)}) %collective-permute-start.4) | collective-permute-done | bytes 36896 | tf_op jit(solution)/shard_map/ppermute | solution.py:760
  42.8 2.3 %project_own_body.1 = (bf16[128,512]{1,0:T(8,128)(2,1)S(1)}, f32[128,2432]{1,0:T(8,128)S(1)}, f32[128,2048]{1,0:T(8,128)S(1)}, f32[128,1024]{1,0:T(8,128)S(1)}) custom-call(bf16[128,1024]{1,0:T(8,128)(2,1)S(1)} %copy-done.5, bf16[128,1024]{1,0:T(8,128)(2,1)S(1)} %copy-done.6, f32[1,512]{1,0:T(1,128)S(1)} %bitcast.18, bf16[4384,512]{1,0:T(8,128)(2,1)S(1)} %bitcast.13, ...), custom_call_target="tpu_custom_call" | custom-call | flops 1 | bytes 1 | tf_op jit(solution)/shard_map/project_own_body/pallas_call | solution.py:359
  45.4 3.2 %forward_body.1 = (f32[128,2304]{1,0:T(8,128)S(1)}, f32[128,2304]{1,0:T(8,128)S(1)}, f32[128,2048]{1,0:T(8,128)S(1)}, f32[3,128,32]{2,1,0:T(8,128)S(1)}) custom-call(s32[1,2]{1,0:T(1,128)S(1)} %copy-done.8, f32[128,2432]{1,0:T(8,128)S(1)} %get-tuple-element.109.own_ref, bf16[128,2048]{1,0:T(8,128)(2,1)} %collective-permute-done.2.wide_ref, ...), custom_call_target="tpu_custom_call" | custom-call | flops 1 | bytes 1 | tf_op jit(solution)/shard_map/forward_body/pallas_call | solution.py:359
  48.6 7.7 %collective-permute-done.5.got_ref = bf16[128,3072]{1,0:T(8,128)(2,1)S(1)} collective-permute-done((bf16[128,3072]{1,0:T(8,128)(2,1)}, bf16[128,3072]{1,0:T(8,128)(2,1)S(1)}, u32[]{:S(2)}, u32[]{:S(2)}) %collective-permute-start.5) | collective-permute-done | bytes 786464 | tf_op jit(solution)/shard_map/ppermute | solution.py:760
  60.4 6.8 %backward_body.1 = (bf16[128,1280]{1,0:T(8,128)(2,1)S(1)}, bf16[128,1280]{1,0:T(8,128)(2,1)S(1)}, f32[8,1152]{1,0:T(8,128)S(1)}, f32[8,1152]{1,0:T(8,128)S(1)}) custom-call(s32[1,2]{1,0:T(1,128)S(1)} %copy-done.8, f32[128,2048]{1,0:T(8,128)S(1)} %get-tuple-element.129.dmixed_ref, f32[128,2304]{1,0:T(8,128)S(1)} %get-tuple-element.130.xbc_ref, ...), custom_call_target="tpu_custom_call" | custom-call | flops 1 | bytes 1 | tf_op jit(solution)/shard_map/backward_body/pallas_call | solution.py:359
  69.7 4.3 %collective-permute-done.13.refs_1_.refs_5_ = bf16[256,1024]{1,0:T(8,128)(2,1)S(1)} collective-permute-done((bf16[256,1024]{1,0:T(8,128)(2,1)S(1)}, bf16[256,1024]{1,0:T(8,128)(2,1)S(1)}, u32[]{:S(2)}, u32[]{:S(2)}) %collective-permute-start.13) | collective-permute-done | bytes 524320 | tf_op jit(solution)/shard_map/ppermute | solution.py:760
  75.2 3.2 %collective-permute-done.16.refs_9_ = f32[8,1152]{1,0:T(8,128)S(1)} collective-permute-done((f32[8,1152]{1,0:T(8,128)S(1)}, f32[8,1152]{1,0:T(8,128)S(1)}, u32[]{:S(2)}, u32[]{:S(2)}) %collective-permute-start.16) | collective-permute-done | bytes 36896 | tf_op jit(solution)/shard_map/ppermute | solution.py:760
  83.8 8.7 %collective-permute-done.17.refs_1_ = bf16[512,512]{1,0:T(8,128)(2,1)S(1)} collective-permute-done((bf16[512,512]{1,0:T(8,128)(2,1)S(1)}, bf16[512,512]{1,0:T(8,128)(2,1)S(1)}, u32[]{:S(2)}, u32[]{:S(2)}) %collective-permute-start.17) | collective-permute-done | bytes 524320 | tf_op jit(solution)/shard_map/ppermute | solution.py:760
  94.9 3.8 %collective-permute-done.19.refs_1_.refs_9_ = bf16[128,1280]{1,0:T(8,128)(2,1)S(1)} collective-permute-done((bf16[128,1280]{1,0:T(8,128)(2,1)S(1)}, bf16[128,1280]{1,0:T(8,128)(2,1)S(1)}, u32[]{:S(2)}, u32[]{:S(2)}) %collective-permute-start.19) | collective-permute-done | bytes 327712 | tf_op jit(solution)/shard_map/ppermute | solution.py:760
  106.8 3.0 %collective-permute-done.24.far_ref = bf16[256,512]{1,0:T(8,128)(2,1)S(1)} collective-permute-done((bf16[256,512]{1,0:T(8,128)(2,1)S(1)}, bf16[256,512]{1,0:T(8,128)(2,1)S(1)}, u32[]{:S(2)}, u32[]{:S(2)}) %collective-permute-start.24) | collective-permute-done | bytes 262176 | tf_op jit(solution)/shard_map/ppermute | solution.py:760
  109.9 3.0 %collective-permute-done.25.refs_1_ = bf16[384,512]{1,0:T(8,128)(2,1)S(1)} collective-permute-done((bf16[384,512]{1,0:T(8,128)(2,1)S(1)}, bf16[384,512]{1,0:T(8,128)(2,1)S(1)}, u32[]{:S(2)}, u32[]{:S(2)}) %collective-permute-start.25) | collective-permute-done | bytes 393248 | tf_op jit(solution)/shard_map/ppermute | solution.py:760
  113.6 3.5 %collective-permute-done.26.refs_1_ = bf16[256,512]{1,0:T(8,128)(2,1)S(1)} collective-permute-done((bf16[256,512]{1,0:T(8,128)(2,1)S(1)}, bf16[256,512]{1,0:T(8,128)(2,1)S(1)}, u32[]{:S(2)}, u32[]{:S(2)}) %collective-permute-start.26) | collective-permute-done | bytes 262176 | tf_op jit(solution)/shard_map/ppermute | solution.py:760
  117.1 8.5 %collective-permute-done.27.got_ref = bf16[256,512]{1,0:T(8,128)(2,1)S(1)} collective-permute-done((bf16[256,512]{1,0:T(8,128)(2,1)S(1)}, bf16[256,512]{1,0:T(8,128)(2,1)S(1)}, u32[]{:S(2)}, u32[]{:S(2)}) %collective-permute-start.27) | collective-permute-done | bytes 262176 | tf_op jit(solution)/shard_map/ppermute | solution.py:760
  126.8 3.2 %collective-permute-done.28.got_ref = bf16[272,512]{1,0:T(8,128)(2,1)S(1)} collective-permute-done((bf16[272,512]{1,0:T(8,128)(2,1)S(1)}, bf16[272,512]{1,0:T(8,128)(2,1)S(1)}, u32[]{:S(2)}, u32[]{:S(2)}) %collective-permute-start.28) | collective-permute-done | bytes 278560 | tf_op jit(solution)/shard_map/ppermute | solution.py:760
  134.3 2.9 %collective-permute-done.33 = bf16[272,512]{1,0:T(8,128)(2,1)S(1)} collective-permute-done((bf16[272,512]{1,0:T(8,128)(2,1)S(1)}, bf16[272,512]{1,0:T(8,128)(2,1)S(1)}, u32[]{:S(2)}, u32[]{:S(2)}) %collective-permute-start.33) | collective-permute-done | bytes 278560 | tf_op jit(solution)/shard_map/ppermute | solution.py:760
  139.2 3.4 %collective-permute-start.36 = (bf16[192,512]{1,0:T(8,128)(2,1)S(1)}, bf16[192,512]{1,0:T(8,128)(2,1)S(1)}, u32[]{:S(2)}, u32[]{:S(2)}) collective-permute-start(bf16[192,512]{1,0:T(8,128)(2,1)S(1)} %add_body.12.keep_ref), channel_id=1, source_target_pairs={{0,16},{1,17},{2,18},{3,19},{4,20},{5,21},{6,22},{7,23},{8,24},{9,... | collective-permute-start | bytes 589832 | tf_op jit(solution)/shard_map/ppermute | solution.py:760
  144.4 11.1 %collective-permute-done.36.got_ref = bf16[192,512]{1,0:T(8,128)(2,1)S(1)} collective-permute-done((bf16[192,512]{1,0:T(8,128)(2,1)S(1)}, bf16[192,512]{1,0:T(8,128)(2,1)S(1)}, u32[]{:S(2)}, u32[]{:S(2)}) %collective-permute-start.36) | collective-permute-done | bytes 196640 | tf_op jit(solution)/shard_map/ppermute | solution.py:760
  160.5 4.9 %collective-permute-done.39 = bf16[192,512]{1,0:T(8,128)(2,1)S(1)} collective-permute-done((bf16[192,512]{1,0:T(8,128)(2,1)S(1)}, bf16[192,512]{1,0:T(8,128)(2,1)S(1)}, u32[]{:S(2)}, u32[]{:S(2)}) %collective-permute-start.39) | collective-permute-done | bytes 196640 | tf_op jit(solution)/shard_map/ppermute | solution.py:760
  167.6 2.7 %out_weight_lanes.1 = f32[1024,1024]{1,0:T(8,128)} custom-call(bf16[512,512]{1,0:T(8,128)(2,1)S(1)} %constant_dynamic-update-slice_fusion.refs_0_, bf16[512,512]{1,0:T(8,128)(2,1)S(1)} %collective-permute-done.35.refs_1_, bf16[512,512]{1,0:T(8,128)(2,1)S(1)} %collective-permute-done.40.refs_2_, bf16[512,512]{1,0:T(8,128)(2,1)S(1)} %collective-permute-done.41.refs_3_), custom_call_target="tpu_custom_call" | custom-call | flops 1 | bytes 1 | tf_op jit(solution)/shard_map/out_weight_lanes/pallas_call | solution.py:738
  172.7 6.3 %collective-permute-done.46.refs_5_ = bf16[384,512]{1,0:T(8,128)(2,1)S(1)} collective-permute-done((bf16[384,512]{1,0:T(8,128)(2,1)S(1)}, bf16[384,512]{1,0:T(8,128)(2,1)S(1)}, u32[]{:S(2)}, u32[]{:S(2)}) %collective-permute-start.46) | collective-permute-done | bytes 393248 | tf_op jit(solution)/shard_map/ppermute | solution.py:760
  181.4 4.9 %in_weight_rows.1 = (f32[4384,512]{1,0:T(8,128)}, f32[8,512]{1,0:T(8,128)S(1)}) custom-call(bf16[544,512]{1,0:T(8,128)(2,1)S(1)} %constant_dynamic-update-slice_fusion.2.refs_0_, bf16[544,512]{1,0:T(8,128)(2,1)S(1)} %collective-permute-done.34.refs_1_, bf16[544,512]{1,0:T(8,128)(2,1)S(1)} %collective-permute-done.42.refs_2_, ...), custom_call_target="tpu_custom_call" | custom-call | flops 1 | bytes 1 | tf_op jit(solution)/shard_map/in_weight_rows/pallas_call | solution.py:738
  (171 shorter events, 64.5 us)
Async XLA Ops:
  19.8 18.3 %collective-permute-start.3 = (f32[128,384]{1,0:T(8,128)}, f32[128,384]{1,0:T(8,128)S(1)}, u32[]{:S(2)}, u32[]{:S(2)}) collective-permute-start(f32[128,384]{1,0:T(8,128)} %get-tuple-element.107), channel_id=1, source_target_pairs={{0,1},{1,0},{2,3},{3,2},{4,5},{5,4},{6,7},{7,6},{8,9},{9,8},{10,11... | collective-permute-start | bytes 589832 | tf_op jit(solution)/shard_map/ppermute | solution.py:760
  21.5 16.6 %collective-permute-start.2 = (bf16[128,2048]{1,0:T(8,128)(2,1)}, bf16[128,2048]{1,0:T(8,128)(2,1)}, u32[]{:S(2)}, u32[]{:S(2)}) collective-permute-start(bf16[128,2048]{1,0:T(8,128)(2,1)} %get-tuple-element.110), channel_id=1, source_target_pairs={{0,1},{1,0},{2,3},{3,2},{4,5},{5,4},{6,7},{7,6},{8,9},{9,8},{10,11... | collective-permute-start | bytes 1572872 | tf_op jit(solution)/shard_map/ppermute | solution.py:760
  38.1 18.1 %collective-permute-start.5 = (bf16[128,3072]{1,0:T(8,128)(2,1)}, bf16[128,3072]{1,0:T(8,128)(2,1)S(1)}, u32[]{:S(2)}, u32[]{:S(2)}) collective-permute-start(bf16[128,3072]{1,0:T(8,128)(2,1)} %copy-done.7), channel_id=1, source_target_pairs={{0,1},{1,0},{2,3},{3,2},{4,5},{5,4},{6,7},{7,6},{8,9},{9,8},{10,11... | collective-permute-start | bytes 2359304 | tf_op jit(solution)/shard_map/ppermute | solution.py:760
  40.0 18.0 %collective-permute-start.8 = (bf16[128,1024]{1,0:T(8,128)(2,1)S(1)}, bf16[128,1024]{1,0:T(8,128)(2,1)S(1)}, u32[]{:S(2)}, u32[]{:S(2)}) collective-permute-start(bf16[128,1024]{1,0:T(8,128)(2,1)S(1)} %copy-done.6), channel_id=1, source_target_pairs={{0,2},{1,3},{2,0},{3,1},{4,6},{5,7},{6,4},{7,5},{8,10},{9,11},{10,... | collective-permute-start | bytes 786440 | tf_op jit(solution)/shard_map/ppermute | solution.py:760
  40.0 18.0 %collective-permute-start.9 = (bf16[128,1024]{1,0:T(8,128)(2,1)S(1)}, bf16[128,1024]{1,0:T(8,128)(2,1)S(1)}, u32[]{:S(2)}, u32[]{:S(2)}) collective-permute-start(bf16[128,1024]{1,0:T(8,128)(2,1)S(1)} %collective-permute-done.1.cotangent_ref.refs_5_), channel_id=1, source_target_pairs={{0,2},{1,3},{2,0},{3,1},{4,6},{5,7},{6,4},{7,5},{8,10},{9,11},{10,... | collective-permute-start | bytes 786440 | tf_op jit(solution)/shard_map/ppermute | solution.py:760
  59.4 14.5 %collective-permute-start.13 = (bf16[256,1024]{1,0:T(8,128)(2,1)S(1)}, bf16[256,1024]{1,0:T(8,128)(2,1)S(1)}, u32[]{:S(2)}, u32[]{:S(2)}) collective-permute-start(bf16[256,1024]{1,0:T(8,128)(2,1)S(1)} %get-tuple-element.138), channel_id=1, source_target_pairs={{0,1},{1,0},{2,3},{3,2},{4,5},{5,4},{6,7},{7,6},{8,9},{9,8},{10,11... | collective-permute-start | bytes 1572872 | tf_op jit(solution)/shard_map/ppermute | solution.py:760
  79.2 14.7 %collective-permute-start.18 = (bf16[544,512]{1,0:T(8,128)(2,1)S(1)}, bf16[544,512]{1,0:T(8,128)(2,1)S(1)}, u32[]{:S(2)}, u32[]{:S(2)}) collective-permute-start(bf16[544,512]{1,0:T(8,128)(2,1)S(1)} %get-tuple-element.146), channel_id=1, source_target_pairs={{0,8},{1,9},{2,10},{3,11},{4,12},{5,13},{6,14},{7,15},{8,0},{9,1},... | collective-permute-start | bytes 1671176 | tf_op jit(solution)/shard_map/ppermute | solution.py:760
  80.1 12.4 %collective-permute-start.17 = (bf16[512,512]{1,0:T(8,128)(2,1)S(1)}, bf16[512,512]{1,0:T(8,128)(2,1)S(1)}, u32[]{:S(2)}, u32[]{:S(2)}) collective-permute-start(bf16[512,512]{1,0:T(8,128)(2,1)S(1)} %get-tuple-element.136), channel_id=1, source_target_pairs={{0,4},{1,5},{2,6},{3,7},{4,0},{5,1},{6,2},{7,3},{8,12},{9,13},{10,... | collective-permute-start | bytes 1572872 | tf_op jit(solution)/shard_map/ppermute | solution.py:760
  81.6 13.3 %collective-permute-start.21 = (bf16[128,1280]{1,0:T(8,128)(2,1)S(1)}, bf16[128,1280]{1,0:T(8,128)(2,1)S(1)}, u32[]{:S(2)}, u32[]{:S(2)}) collective-permute-start(bf16[128,1280]{1,0:T(8,128)(2,1)S(1)} %get-tuple-element.154), channel_id=1, source_target_pairs={{0,3},{1,2},{2,1},{3,0},{4,7},{5,6},{6,5},{7,4},{8,11},{9,10},{10,... | collective-permute-start | bytes 983048 | tf_op jit(solution)/shard_map/ppermute | solution.py:760
  81.6 13.3 %collective-permute-start.20 = (bf16[128,1280]{1,0:T(8,128)(2,1)S(1)}, bf16[128,1280]{1,0:T(8,128)(2,1)S(1)}, u32[]{:S(2)}, u32[]{:S(2)}) collective-permute-start(bf16[128,1280]{1,0:T(8,128)(2,1)S(1)} %get-tuple-element.154), channel_id=1, source_target_pairs={{0,2},{1,3},{2,0},{3,1},{4,6},{5,7},{6,4},{7,5},{8,10},{9,11},{10,... | collective-permute-start | bytes 983048 | tf_op jit(solution)/shard_map/ppermute | solution.py:760
  83.2 15.4 %collective-permute-start.19 = (bf16[128,1280]{1,0:T(8,128)(2,1)S(1)}, bf16[128,1280]{1,0:T(8,128)(2,1)S(1)}, u32[]{:S(2)}, u32[]{:S(2)}) collective-permute-start(bf16[128,1280]{1,0:T(8,128)(2,1)S(1)} %get-tuple-element.159.refs_0_.refs_8_), channel_id=1, source_target_pairs={{0,1},{1,0},{2,3},{3,2},{4,5},{5,4},{6,7},{7,6},{8,9},{9,8},{10,11... | collective-permute-start | bytes 983048 | tf_op jit(solution)/shard_map/ppermute | solution.py:760
  102.1 14.9 %collective-permute-start.26 = (bf16[256,512]{1,0:T(8,128)(2,1)S(1)}, bf16[256,512]{1,0:T(8,128)(2,1)S(1)}, u32[]{:S(2)}, u32[]{:S(2)}) collective-permute-start(bf16[256,512]{1,0:T(8,128)(2,1)S(1)} %get-tuple-element.160), channel_id=1, source_target_pairs={{0,8},{1,9},{2,10},{3,11},{4,12},{5,13},{6,14},{7,15},{8,0},{9,1},... | collective-permute-start | bytes 786440 | tf_op jit(solution)/shard_map/ppermute | solution.py:760
  103.6 21.9 %collective-permute-start.27 = (bf16[256,512]{1,0:T(8,128)(2,1)S(1)}, bf16[256,512]{1,0:T(8,128)(2,1)S(1)}, u32[]{:S(2)}, u32[]{:S(2)}) collective-permute-start(bf16[256,512]{1,0:T(8,128)(2,1)S(1)} %add_body.8.keep_ref), channel_id=1, source_target_pairs={{0,16},{1,17},{2,18},{3,19},{4,20},{5,21},{6,22},{7,23},{8,24},{9,... | collective-permute-start | bytes 786440 | tf_op jit(solution)/shard_map/ppermute | solution.py:760
  105.3 24.7 %collective-permute-start.28 = (bf16[272,512]{1,0:T(8,128)(2,1)S(1)}, bf16[272,512]{1,0:T(8,128)(2,1)S(1)}, u32[]{:S(2)}, u32[]{:S(2)}) collective-permute-start(bf16[272,512]{1,0:T(8,128)(2,1)S(1)} %add_body.9.keep_ref), channel_id=1, source_target_pairs={{0,16},{1,17},{2,18},{3,19},{4,20},{5,21},{6,22},{7,23},{8,24},{9,... | collective-permute-start | bytes 835592 | tf_op jit(solution)/shard_map/ppermute | solution.py:760
  109.8 21.1 %collective-permute-start.29 = (bf16[256,512]{1,0:T(8,128)(2,1)S(1)}, bf16[256,512]{1,0:T(8,128)(2,1)S(1)}, u32[]{:S(2)}, u32[]{:S(2)}) collective-permute-start(bf16[256,512]{1,0:T(8,128)(2,1)S(1)} %pad_maximum_fusion), channel_id=1, source_target_pairs={{0,2},{1,3},{2,0},{3,1},{4,6},{5,7},{6,4},{7,5},{8,10},{9,11},{10,... | collective-permute-start | bytes 786440 | tf_op jit(solution)/shard_map/ppermute | solution.py:760
  113.0 19.1 %collective-permute-start.30 = (bf16[192,512]{1,0:T(8,128)(2,1)S(1)}, bf16[192,512]{1,0:T(8,128)(2,1)S(1)}, u32[]{:S(2)}, u32[]{:S(2)}) collective-permute-start(bf16[192,512]{1,0:T(8,128)(2,1)S(1)} %get-tuple-element.169), channel_id=1, source_target_pairs={{0,8},{1,9},{2,10},{3,11},{4,12},{5,13},{6,14},{7,15},{8,0},{9,1},... | collective-permute-start | bytes 589832 | tf_op jit(solution)/shard_map/ppermute | solution.py:760
  137.3 20.3 %collective-permute-start.34 = (bf16[544,512]{1,0:T(8,128)(2,1)S(1)}, bf16[544,512]{1,0:T(8,128)(2,1)S(1)}, u32[]{:S(2)}, u32[]{:S(2)}) collective-permute-start(bf16[544,512]{1,0:T(8,128)(2,1)S(1)} %constant_dynamic-update-slice_fusion.2.refs_0_), channel_id=1, source_target_pairs={{0,8},{1,9},{2,10},{3,11},{4,12},{5,13},{6,14},{7,15},{8,0},{9,1},... | collective-permute-start | bytes 1671176 | tf_op jit(solution)/shard_map/ppermute | solution.py:760
  138.7 18.1 %collective-permute-start.35 = (bf16[512,512]{1,0:T(8,128)(2,1)S(1)}, bf16[512,512]{1,0:T(8,128)(2,1)S(1)}, u32[]{:S(2)}, u32[]{:S(2)}) collective-permute-start(bf16[512,512]{1,0:T(8,128)(2,1)S(1)} %constant_dynamic-update-slice_fusion.refs_0_), channel_id=1, source_target_pairs={{0,4},{1,5},{2,6},{3,7},{4,0},{5,1},{6,2},{7,3},{8,12},{9,13},{10,... | collective-permute-start | bytes 1572872 | tf_op jit(solution)/shard_map/ppermute | solution.py:760
  139.2 16.2 %collective-permute-start.36 = (bf16[192,512]{1,0:T(8,128)(2,1)S(1)}, bf16[192,512]{1,0:T(8,128)(2,1)S(1)}, u32[]{:S(2)}, u32[]{:S(2)}) collective-permute-start(bf16[192,512]{1,0:T(8,128)(2,1)S(1)} %add_body.12.keep_ref), channel_id=1, source_target_pairs={{0,16},{1,17},{2,18},{3,19},{4,20},{5,21},{6,22},{7,23},{8,24},{9,... | collective-permute-start | bytes 589832 | tf_op jit(solution)/shard_map/ppermute | solution.py:760
  143.4 14.7 %collective-permute-start.38 = (bf16[128,1024]{1,0:T(8,128)(2,1)S(1)}, bf16[128,1024]{1,0:T(8,128)(2,1)S(1)}, u32[]{:S(2)}, u32[]{:S(2)}) collective-permute-start(bf16[128,1024]{1,0:T(8,128)(2,1)S(1)} %get-tuple-element.184), channel_id=1, source_target_pairs={{0,1},{1,0},{2,3},{3,2},{4,5},{5,4},{6,7},{7,6},{8,9},{9,8},{10,11... | collective-permute-start | bytes 786440 | tf_op jit(solution)/shard_map/ppermute | solution.py:760
  144.4 12.5 %collective-permute-start.37 = (bf16[128,512]{1,0:T(8,128)(2,1)S(1)}, bf16[128,512]{1,0:T(8,128)(2,1)S(1)}, u32[]{:S(2)}, u32[]{:S(2)}) collective-permute-start(bf16[128,512]{1,0:T(8,128)(2,1)S(1)} %add_body.13.keep_ref), channel_id=1, source_target_pairs={{0,16},{1,17},{2,18},{3,19},{4,20},{5,21},{6,22},{7,23},{8,24},{9,... | collective-permute-start | bytes 393224 | tf_op jit(solution)/shard_map/ppermute | solution.py:760
  155.4 14.9 %collective-permute-start.42 = (bf16[544,512]{1,0:T(8,128)(2,1)S(1)}, bf16[544,512]{1,0:T(8,128)(2,1)S(1)}, u32[]{:S(2)}, u32[]{:S(2)}) collective-permute-start(bf16[544,512]{1,0:T(8,128)(2,1)S(1)} %constant_dynamic-update-slice_fusion.2.refs_0_), channel_id=1, source_target_pairs={{0,2},{1,3},{2,0},{3,1},{4,6},{5,7},{6,4},{7,5},{8,10},{9,11},{10,... | collective-permute-start | bytes 1671176 | tf_op jit(solution)/shard_map/ppermute | solution.py:760
  157.6 12.8 %collective-permute-start.43 = (bf16[544,512]{1,0:T(8,128)(2,1)S(1)}, bf16[544,512]{1,0:T(8,128)(2,1)S(1)}, u32[]{:S(2)}, u32[]{:S(2)}) collective-permute-start(bf16[544,512]{1,0:T(8,128)(2,1)S(1)} %collective-permute-done.34.refs_1_), channel_id=1, source_target_pairs={{0,2},{1,3},{2,0},{3,1},{4,6},{5,7},{6,4},{7,5},{8,10},{9,11},{10,... | collective-permute-start | bytes 1671176 | tf_op jit(solution)/shard_map/ppermute | solution.py:760
  166.7 14.1 %collective-permute-start.47 = (bf16[384,512]{1,0:T(8,128)(2,1)S(1)}, bf16[384,512]{1,0:T(8,128)(2,1)S(1)}, u32[]{:S(2)}, u32[]{:S(2)}) collective-permute-start(bf16[384,512]{1,0:T(8,128)(2,1)S(1)} %constant_dynamic-update-slice_fusion.4.refs_4_), channel_id=1, source_target_pairs={{0,2},{1,3},{2,0},{3,1},{4,6},{5,7},{6,4},{7,5},{8,10},{9,11},{10,... | collective-permute-start | bytes 1179656 | tf_op jit(solution)/shard_map/ppermute | solution.py:760
  (43 other events, 361.6 us)
